TPU v7x, 32 devices: a whole 2x2x4 slice. The times are simulated.
32 devices in a mesh: rows: 4 (over y, x), tp: 8 (over z, core).
Axes of the slice: x: 2, y: 2, z: 4, core: 2. Of those that a mesh axis runs over, the one named last changes fastest.
Arguments:
- hidden_in: bfloat16 [4, 2048, 2048], P('rows', 'tp'), may hold values from -6 to 6
- segment_ids: int32 [4, 2048], P('rows', 'tp'), may hold values from 0 to 7, never falling along the last dimension, each value on 1 to 1024 neighbouring positions
- ln_gain: float32 [2048], replicated, may hold values from 0.5 to 1.5
- ln_bias: float32 [2048], replicated, may hold values from -3 to 3
- w_qkv: bfloat16 [2048, 3, 2048], P(None, None, 'tp'), may hold values from -0.125 to 0.125
- b_qkv: float32 [3, 2048], P(None, 'tp'), may hold values from -3 to 3
- w_out: bfloat16 [2048, 2048], P('tp'), may hold values from -0.5 to 0.5
- out_bias: float32 [2048], replicated, may hold values from -3 to 3
- w_up: bfloat16 [2048, 8192], P(None, 'tp'), may hold values from -0.125 to 0.125
- b_up: float32 [8192], P('tp'), may hold values from -3 to 3
- w_down: bfloat16 [8192, 2048], P('tp'), may hold values from -0.0625 to 0.0625
- cotangent: bfloat16 [4, 2048, 2048], P('rows', 'tp'), may hold values from -6 to 6
Outputs:
- hidden_out: bfloat16 [4, 2048, 2048], P('rows', 'tp')
- grad_input: bfloat16 [4, 2048, 2048], P('rows', 'tp')
- grad_ln_gain: float32 [2048], replicated
- grad_ln_bias: float32 [2048], replicated
- grad_w_qkv: float32 [2048, 3, 2048], P(None, None, 'tp')
- grad_b_qkv: float32 [3, 2048], P(None, 'tp')
- grad_w_out: float32 [2048, 2048], P('tp')
- grad_out_bias: float32 [2048], replicated
- grad_w_up: float32 [2048, 8192], P(None, 'tp')
- grad_b_up: float32 [8192], P('tp')
- grad_w_down: float32 [8192, 2048], P('tp')
Inputs may be any that keep to these rules, and one draw needn't show every extreme that they name: `segment_ids`: within a row the ids never fall; every document has 1 to 1024 tokens, and one has exactly 1024.
All inputs are finite; a program needn't handle non-finite values.
Results may differ from a plain program's by a relative error of at most 0.012.
The roundings to bfloat16 on the way count: a program that leaves them out, or rounds other values in their place, can miss the bound.
Values may be sent and summed in bfloat16 or wider, within the bound.
No kernel may reach another device: no remote copies, remote signals or barrier semaphores. Data moves between devices by JAX's collectives and lax.ppermute only.
A program may use at most 256 MiB of HBM per device.

v0:
```python
from functools import partial
import math

import jax
import jax.numpy as jnp
from jax import lax
from jax.sharding import PartitionSpec as P

HEAD_DIM = 64
ROT = 32


EPSILON = 1e-05
NEGATIVE = -1e30


def doc_positions(segments):
    length = segments.shape[-1]
    index_row = jnp.arange(length, dtype=jnp.int32)
    previous = jnp.concatenate([segments[..., :1], segments[..., :-1]], axis=-1)
    marks = jnp.where(
        (index_row == 0) | (segments != previous), index_row, jnp.zeros_like(index_row)
    )
    return index_row - lax.cummax(marks, axis=segments.ndim - 1)


def rotary_tables(positions):
    ladder = jnp.arange(ROT // 2, dtype=jnp.float32)
    inverse = jnp.exp(ladder * (-2.0 * math.log(10000.0) / ROT))
    angles = positions.astype(jnp.float32)[..., None] * inverse
    return (jnp.cos(angles)[..., None, :], jnp.sin(angles)[..., None, :])


def rotate(vectors, cosine, sine):
    quarter = ROT // 2
    first = vectors[..., :quarter]
    second = vectors[..., quarter:ROT]
    remainder = vectors[..., ROT:]
    return jnp.concatenate(
        [first * cosine - second * sine, second * cosine + first * sine, remainder], axis=-1
    )


def block_scores(query_block, key_vecs, seg_block, segments_all, start):
    block_rows = query_block.shape[1]
    length = key_vecs.shape[1]
    scores = (
        jnp.einsum("rqhe,rkhe->rhqk", query_block, key_vecs, preferred_element_type=jnp.float32)
        * 0.125
    )
    key_index = jnp.arange(length, dtype=jnp.int32)
    query_index = start + jnp.arange(block_rows, dtype=jnp.int32)
    same_doc = seg_block[:, None, :, None] == segments_all[:, None, None, :]
    causal = key_index[None, :] <= query_index[:, None]
    return jnp.where(same_doc & causal[None, None], scores, NEGATIVE)


def attend_forward(queries, key_vecs, value_vecs, segments_all):
    length = queries.shape[1]
    block_rows = min(512, length)

    def one_block(block_index):
        start = block_index * block_rows
        query_block = lax.dynamic_slice_in_dim(queries, start, block_rows, 1)
        seg_block = lax.dynamic_slice_in_dim(segments_all, start, block_rows, 1)
        scores = block_scores(query_block, key_vecs, seg_block, segments_all, start)
        top_score = jnp.max(scores, axis=-1, keepdims=True)
        weights = jnp.exp(scores - top_score)
        totals = jnp.sum(weights, axis=-1, keepdims=True)
        probs = (weights / totals).astype(jnp.bfloat16)
        context = jnp.einsum(
            "rhqk,rkhe->rqhe", probs, value_vecs, preferred_element_type=jnp.float32
        )
        return (context.astype(jnp.bfloat16), (top_score + jnp.log(totals))[..., 0])

    contexts, log_totals = lax.map(one_block, jnp.arange(length // block_rows, dtype=jnp.int32))
    batch_rows, heads_here, head_size = (queries.shape[0], queries.shape[2], queries.shape[3])
    context = jnp.transpose(contexts, (1, 0, 2, 3, 4)).reshape(
        batch_rows, length, heads_here, head_size
    )
    return (context, log_totals)


def attend_backward(queries, key_vecs, value_vecs, segments_all, log_totals, grad_context):
    batch_rows, length, heads_here, head_size = queries.shape
    block_rows = min(512, length)

    def one_block(carry, inputs_pair):
        grad_keys, grad_values = carry
        block_index, block_lse = inputs_pair
        start = block_index * block_rows
        query_block = lax.dynamic_slice_in_dim(queries, start, block_rows, 1)
        seg_block = lax.dynamic_slice_in_dim(segments_all, start, block_rows, 1)
        grad_block = lax.dynamic_slice_in_dim(grad_context, start, block_rows, 1)
        scores = block_scores(query_block, key_vecs, seg_block, segments_all, start)
        soft = jnp.exp(scores - block_lse[..., None])
        probs = soft.astype(jnp.bfloat16)
        grad_probs = jnp.einsum(
            "rqhe,rkhe->rhqk", grad_block, value_vecs, preferred_element_type=jnp.float32
        )
        inner = jnp.sum(soft * grad_probs, axis=-1, keepdims=True)
        grad_scores = (soft * (grad_probs - inner)).astype(jnp.bfloat16)
        grad_query = (
            jnp.einsum("rhqk,rkhe->rqhe", grad_scores, key_vecs, preferred_element_type=jnp.float32)
            * 0.125
        )
        grad_keys = (
            grad_keys
            + jnp.einsum(
                "rhqk,rqhe->rkhe", grad_scores, query_block, preferred_element_type=jnp.float32
            )
            * 0.125
        )
        grad_values = grad_values + jnp.einsum(
            "rhqk,rqhe->rkhe", probs, grad_block, preferred_element_type=jnp.float32
        )
        return ((grad_keys, grad_values), grad_query)

    empty = jnp.zeros((batch_rows, length, heads_here, head_size), jnp.float32)
    blocks = length // block_rows
    carried, grad_blocks = lax.scan(
        one_block, (empty, empty), (jnp.arange(blocks, dtype=jnp.int32), log_totals)
    )
    grad_queries = jnp.transpose(grad_blocks, (1, 0, 2, 3, 4)).reshape(
        batch_rows, length, heads_here, head_size
    )
    return (grad_queries, carried[0], carried[1])


def token_sum(matrix):
    ones_row = jnp.ones((1, matrix.shape[0]), matrix.dtype)
    return jnp.dot(ones_row, matrix, preferred_element_type=jnp.float32)[0]


def local(
    hidden_in,
    segment_ids,
    ln_gain,
    ln_bias,
    w_qkv,
    b_qkv,
    w_out,
    out_bias,
    w_up,
    b_up,
    w_down,
    cotangent,
):
    inputs = hidden_in.astype(jnp.float32)
    average = jnp.mean(inputs, axis=-1, keepdims=True)
    centred = inputs - average
    inverse_std = lax.rsqrt(jnp.mean(centred * centred, axis=-1, keepdims=True) + EPSILON)
    unit_rows = centred * inverse_std
    normed = (unit_rows * ln_gain + ln_bias).astype(jnp.bfloat16)
    gathered, segments_all = (
        lax.all_gather(normed, "tp", axis=1, tiled=True),
        lax.all_gather(segment_ids, "tp", axis=1, tiled=True),
    )
    batch_rows, length, width = gathered.shape
    token_count = batch_rows * length
    flat_normed = gathered.reshape(token_count, width)
    local_width = w_qkv.shape[2]
    heads_here = local_width // HEAD_DIM
    qkv_matrix = w_qkv.reshape(width, 3 * local_width)
    mixed = jnp.dot(flat_normed, qkv_matrix, preferred_element_type=jnp.float32) + b_qkv.reshape(
        3 * local_width
    )
    mixed = mixed.reshape(batch_rows, length, 3, heads_here, HEAD_DIM)
    cosine, sine = rotary_tables(doc_positions(segments_all))
    queries = rotate(mixed[:, :, 0], cosine, sine).astype(jnp.bfloat16)
    key_vecs = rotate(mixed[:, :, 1], cosine, sine).astype(jnp.bfloat16)
    value_vecs = mixed[:, :, 2].astype(jnp.bfloat16)
    context, log_totals = attend_forward(queries, key_vecs, value_vecs, segments_all)
    flat_context = context.reshape(token_count, local_width)
    attention_part = jnp.dot(flat_context, w_out, preferred_element_type=jnp.float32)
    upward = jnp.dot(flat_normed, w_up, preferred_element_type=jnp.float32) + b_up
    activated, gelu_pullback = jax.vjp(partial(jax.nn.gelu, approximate=True), upward)
    activated_low = activated.astype(jnp.bfloat16)
    mlp_part = jnp.dot(activated_low, w_down, preferred_element_type=jnp.float32)
    full_shape = (batch_rows, length, width)
    branch_total = lax.psum_scatter(
        (attention_part + mlp_part).reshape(full_shape), "tp", scatter_dimension=1, tiled=True
    )
    hidden_out = (inputs + branch_total + out_bias).astype(jnp.bfloat16)
    grad_whole = lax.all_gather(cotangent, "tp", axis=1, tiled=True)
    flat_grad = grad_whole.reshape(token_count, width)
    grad_out_bias = token_sum(flat_grad)
    grad_w_down = jnp.dot(activated_low.T, flat_grad, preferred_element_type=jnp.float32)
    grad_activated = jnp.dot(flat_grad, w_down.T, preferred_element_type=jnp.float32)
    grad_upward = gelu_pullback(grad_activated)[0].astype(jnp.bfloat16)
    grad_w_out = jnp.dot(flat_context.T, flat_grad, preferred_element_type=jnp.float32)
    grad_context = jnp.dot(flat_grad, w_out.T, preferred_element_type=jnp.float32).astype(
        jnp.bfloat16
    )
    grad_context = grad_context.reshape(batch_rows, length, heads_here, HEAD_DIM)
    grad_queries, grad_keys, grad_values = attend_backward(
        queries, key_vecs, value_vecs, segments_all, log_totals, grad_context
    )
    grad_mixed = jnp.stack(
        [rotate(grad_queries, cosine, -sine), rotate(grad_keys, cosine, -sine), grad_values], axis=2
    )
    grad_mixed = grad_mixed.astype(jnp.bfloat16).reshape(token_count, 3 * local_width)
    normed_rows = lax.all_gather(normed, "tp", axis=1, tiled=True).reshape(token_count, width)
    grad_w_up = jnp.dot(normed_rows.T, grad_upward, preferred_element_type=jnp.float32)
    grad_b_up = token_sum(grad_upward)
    grad_w_qkv = jnp.dot(normed_rows.T, grad_mixed, preferred_element_type=jnp.float32).reshape(
        width, 3, local_width
    )
    grad_b_qkv = token_sum(grad_mixed).reshape(3, local_width)
    part_qkv = jnp.dot(grad_mixed, qkv_matrix.T, preferred_element_type=jnp.float32).reshape(
        full_shape
    )
    part_up = jnp.dot(grad_upward, w_up.T, preferred_element_type=jnp.float32).reshape(full_shape)
    grad_normed = lax.psum_scatter(part_qkv + part_up, "tp", scatter_dimension=1, tiled=True)
    gain_terms = jnp.sum(grad_normed * unit_rows, axis=(0, 1))
    bias_terms = jnp.sum(grad_normed, axis=(0, 1))
    grad_unit = grad_normed * ln_gain
    grad_input = cotangent.astype(jnp.float32) + inverse_std * (
        grad_unit
        - jnp.mean(grad_unit, axis=-1, keepdims=True)
        - unit_rows * jnp.mean(grad_unit * unit_rows, axis=-1, keepdims=True)
    )
    grad_ln_gain, grad_ln_bias = lax.psum((gain_terms, bias_terms), ("rows", "tp"))
    summed = (
        lax.psum(grad_w_qkv.astype(jnp.bfloat16), "rows").astype(jnp.float32),
        lax.psum(grad_b_qkv.astype(jnp.bfloat16), "rows").astype(jnp.float32),
        lax.psum(grad_w_out.astype(jnp.bfloat16), "rows").astype(jnp.float32),
        lax.psum(grad_out_bias.astype(jnp.bfloat16), "rows").astype(jnp.float32),
        lax.psum(grad_w_up.astype(jnp.bfloat16), "rows").astype(jnp.float32),
        lax.psum(grad_b_up.astype(jnp.bfloat16), "rows").astype(jnp.float32),
        lax.psum(grad_w_down.astype(jnp.bfloat16), "rows").astype(jnp.float32),
    )
    return (
        hidden_out,
        grad_input.astype(jnp.bfloat16),
        grad_ln_gain,
        grad_ln_bias,
        summed[0],
        summed[1],
        summed[2],
        summed[3],
        summed[4],
        summed[5],
        summed[6],
    )


def solution(mesh):
    in_specs = (
        P("rows", "tp", None),
        P("rows", "tp"),
        P(),
        P(),
        P(None, None, "tp"),
        P(None, "tp"),
        P("tp", None),
        P(),
        P(None, "tp"),
        P("tp"),
        P("tp", None),
        P("rows", "tp", None),
    )
    out_specs = (
        P("rows", "tp", None),
        P("rows", "tp", None),
        P(),
        P(),
        P(None, None, "tp"),
        P(None, "tp"),
        P("tp", None),
        P(),
        P(None, "tp"),
        P("tp"),
        P("tp", None),
    )
    return jax.shard_map(local, mesh=mesh, in_specs=in_specs, out_specs=out_specs, check_vma=False)
```

profile of v0, /device:TPU:0, one launch (start us, length us, event | category | flops | bytes accessed | tf_op | source)
XLA Modules:
  0.0 1163.3 jit_solution(2704268365772314584)
XLA Ops:
  14.6 13.4 %all_gather.10 = s32[1,2048]{1,0:T(1,128)S(1)} all-gather(s32[1,256]{1,0:T(1,128)S(1)} %copy-done.29), channel_id=1, replica_groups=mesh['rows'=4,'tp'=8] {'tp'}, dimensions={1}, use_global_device_ids=true | all-gather | bytes 9216 | tf_op jit(solution)/shard_map/all_gather | solution.py:157
  35.9 62.7 %all-gather.3.cloned.1.call-done = bf16[1,2048,2048]{2,1,0:T(8,128)(2,1)} async-done(((bf16[1,256,2048]{2,1,0:T(8,128)(2,1)}), bf16[1,2048,2048]{2,1,0:T(8,128)(2,1)}) %all-gather.3.cloned.1.call-update) | async-done | bytes 8388624 | tf_op jit(solution)/shard_map/all_gather | solution.py:156
  110.7 71.1 %while.27 = (s32[]{:T(128)}, bf16[4,1,512,4,64]{2,4,3,1,0:T(8,128)(2,1)}, f32[4,1,4,512]{3,2,1,0:T(4,128)}, s32[4]{0:T(128)S(1)}, s32[1,2048]{1,0:T(1,128)S(1)},...) while((s32[]{:T(128)}, ...), condition=%wide.region_7.8_spmd, body=%wide.region_4.7_spmd.sunk | while | flops 1127348736 | bytes 57232568 | solution.py:76
  188.6 296.1 %while.28 = (s32[]{:T(128)}, f32[1,2048,4,64]{1,3,2,0:T(8,128)}, f32[1,2048,4,64]{1,3,2,0:T(8,128)}, f32[4,1,512,4,64]{2,0,4,3,1:T(4,128)}, s32[4]{0:T(128)S(1)}...) while((s32[]{:T(128)}, f32[1,2048,4,64]{1,3,2,0:T(8,128)}, ...), condition=%wide.region_11.12_spmd.clone, body=%wide.region_9.11_spmd.clone.sunk | while | flops 2753165824 | bytes 250194448 | solution.py:121
  208.7 13.1 %multiply_reduce_fusion.3 = (f32[4,512]{1,0:T(4,128)}, f32[4,512,2048]{2,1,0:T(8,128)}) fusion(f32[4,512,2048]{2,1,0:T(8,128)S(1)} %fusion.173, f32[4,512]{1,0:T(4,128)} %dynamic-slice_bitcast_fusion.2, pred[512,2048]{1,0:T(8,128)(4,1)} %fusion.174, bf16[1,2048,4,64]{1,3,2,0:T(8,128)(2,1)} %copy-done.8, ...), kind=kOutput, calls=%fused_computation.23.clone.1 | convolution fusion | flops 557840384 | bytes 35930116 | tf_op jit(solution)/shard_map/while/body/eval_jaxpr/rqhe,rkhe->rhqk/dot_general | solution.py:98
  240.5 11.1 dynamic_update_slice.20
  258.3 11.9 %fusion.176 = f32[1,2048,4,64]{1,3,2,0:T(8,128)} fusion(f32[4,512,2048]{2,1,0:T(8,128)} %copy-done.1, f32[4,512]{1,0:T(4,128)S(1)} %copy-done.17, pred[512,2048]{1,0:T(8,128)(4,1)S(1)} %copy-done.4, f32[1,2048,4,64]{1,3,2,0:T(8,128)} %get-tuple-element.407, pred[]{:T(512)S(6)} %compare.3, bf16[1,2048,4,64]{1,3,2,0:T(8,128)(2,1)} %get-tuple-element.429, ...), kind=kOutput, calls=%fused_computation.34.clone.1 | convolution fusion | flops 554696704 | bytes 22290436 | tf_op jit(solution)/shard_map/while/body/eval_jaxpr/rhqk,rqhe->rkhe/dot_general | solution.py:114
  279.4 13.1 %multiply_reduce_fusion.3 = (f32[4,512]{1,0:T(4,128)}, f32[4,512,2048]{2,1,0:T(8,128)}) fusion(f32[4,512,2048]{2,1,0:T(8,128)S(1)} %fusion.173, f32[4,512]{1,0:T(4,128)} %dynamic-slice_bitcast_fusion.2, pred[512,2048]{1,0:T(8,128)(4,1)} %fusion.174, bf16[1,2048,4,64]{1,3,2,0:T(8,128)(2,1)} %copy-done.8, ...), kind=kOutput, calls=%fused_computation.23.clone.1 | convolution fusion | flops 557840384 | bytes 35930116 | tf_op jit(solution)/shard_map/while/body/eval_jaxpr/rqhe,rkhe->rhqk/dot_general | solution.py:98
  329.1 12.5 %fusion.176 = f32[1,2048,4,64]{1,3,2,0:T(8,128)} fusion(f32[4,512,2048]{2,1,0:T(8,128)} %copy-done.1, f32[4,512]{1,0:T(4,128)S(1)} %copy-done.17, pred[512,2048]{1,0:T(8,128)(4,1)S(1)} %copy-done.4, f32[1,2048,4,64]{1,3,2,0:T(8,128)} %get-tuple-element.407, pred[]{:T(512)S(6)} %compare.3, bf16[1,2048,4,64]{1,3,2,0:T(8,128)(2,1)} %get-tuple-element.429, ...), kind=kOutput, calls=%fused_computation.34.clone.1 | convolution fusion | flops 554696704 | bytes 22290436 | tf_op jit(solution)/shard_map/while/body/eval_jaxpr/rhqk,rqhe->rkhe/dot_general | solution.py:114
  350.7 13.1 %multiply_reduce_fusion.3 = (f32[4,512]{1,0:T(4,128)}, f32[4,512,2048]{2,1,0:T(8,128)}) fusion(f32[4,512,2048]{2,1,0:T(8,128)S(1)} %fusion.173, f32[4,512]{1,0:T(4,128)} %dynamic-slice_bitcast_fusion.2, pred[512,2048]{1,0:T(8,128)(4,1)} %fusion.174, bf16[1,2048,4,64]{1,3,2,0:T(8,128)(2,1)} %copy-done.8, ...), kind=kOutput, calls=%fused_computation.23.clone.1 | convolution fusion | flops 557840384 | bytes 35930116 | tf_op jit(solution)/shard_map/while/body/eval_jaxpr/rqhe,rkhe->rhqk/dot_general | solution.py:98
  400.4 12.5 %fusion.176 = f32[1,2048,4,64]{1,3,2,0:T(8,128)} fusion(f32[4,512,2048]{2,1,0:T(8,128)} %copy-done.1, f32[4,512]{1,0:T(4,128)S(1)} %copy-done.17, pred[512,2048]{1,0:T(8,128)(4,1)S(1)} %copy-done.4, f32[1,2048,4,64]{1,3,2,0:T(8,128)} %get-tuple-element.407, pred[]{:T(512)S(6)} %compare.3, bf16[1,2048,4,64]{1,3,2,0:T(8,128)(2,1)} %get-tuple-element.429, ...), kind=kOutput, calls=%fused_computation.34.clone.1 | convolution fusion | flops 554696704 | bytes 22290436 | tf_op jit(solution)/shard_map/while/body/eval_jaxpr/rhqk,rqhe->rkhe/dot_general | solution.py:114
  422.1 13.1 %multiply_reduce_fusion.3 = (f32[4,512]{1,0:T(4,128)}, f32[4,512,2048]{2,1,0:T(8,128)}) fusion(f32[4,512,2048]{2,1,0:T(8,128)S(1)} %fusion.173, f32[4,512]{1,0:T(4,128)} %dynamic-slice_bitcast_fusion.2, pred[512,2048]{1,0:T(8,128)(4,1)} %fusion.174, bf16[1,2048,4,64]{1,3,2,0:T(8,128)(2,1)} %copy-done.8, ...), kind=kOutput, calls=%fused_computation.23.clone.1 | convolution fusion | flops 557840384 | bytes 35930116 | tf_op jit(solution)/shard_map/while/body/eval_jaxpr/rqhe,rkhe->rhqk/dot_general | solution.py:98
  471.8 12.5 %fusion.176 = f32[1,2048,4,64]{1,3,2,0:T(8,128)} fusion(f32[4,512,2048]{2,1,0:T(8,128)} %copy-done.1, f32[4,512]{1,0:T(4,128)S(1)} %copy-done.17, pred[512,2048]{1,0:T(8,128)(4,1)S(1)} %copy-done.4, f32[1,2048,4,64]{1,3,2,0:T(8,128)} %get-tuple-element.407, pred[]{:T(512)S(6)} %compare.3, bf16[1,2048,4,64]{1,3,2,0:T(8,128)(2,1)} %get-tuple-element.429, ...), kind=kOutput, calls=%fused_computation.34.clone.1 | convolution fusion | flops 554696704 | bytes 22290436 | tf_op jit(solution)/shard_map/while/body/eval_jaxpr/rhqk,rqhe->rkhe/dot_general | solution.py:114
  510.1 14.5 %fusion.73 = bf16[1024,2048]{1,0:T(8,128)(2,1)} fusion(bf16[1,2048,2048]{2,1,0:T(8,128)(2,1)S(1)} %bitcast.225, f32[2048,1024]{1,0:T(8,128)} %fusion.69, f32[1024]{0:T(1024)S(1)} %copy-done.31), kind=kOutput, calls=%fused_computation.90 | convolution fusion | flops 8613003264 | bytes 20975616 | tf_op jit(solution)/shard_map/dot_general | solution.py:188
  524.6 17.6 %fusion.54 = bf16[2048,1024]{1,0:T(8,128)(2,1)S(1)} fusion(f32[2048,1024]{1,0:T(8,128)} %fusion.69, f32[1024]{0:T(1024)S(1)} %copy-done.31, bf16[1024,2048]{1,0:T(8,128)(2,1)} %param.26, bf16[1,2048,2048]{2,1,0:T(8,128)(2,1)S(1)} %bitcast.225), kind=kOutput, calls=%fused_computation.69 | convolution fusion | flops 8633974784 | bytes 25169920 | tf_op jit(solution)/shard_map/dot_general | solution.py:189
  542.2 12.4 %fusion.79 = bf16[2048,3,256]{2,0,1:T(8,128)(2,1)} fusion(bf16[3,256,2048]{2,1,0:T(8,128)(2,1)S(1)} %bitcast.226, bf16[1,2048,2048]{2,1,0:T(8,128)(2,1)} %all-gather.3.cloned.1.call-done), kind=kOutput, calls=%fused_computation.92 | convolution fusion | flops 6444023808 | bytes 14680064 | tf_op jit(solution)/shard_map/dot_general | solution.py:206
  558.0 12.8 %fusion.76 = bf16[2048,1024]{1,0:T(8,128)(2,1)} fusion(bf16[2048,1024]{1,0:T(8,128)(2,1)S(1)} %fusion.54, bf16[1,2048,2048]{2,1,0:T(8,128)(2,1)} %all-gather.3.cloned.1.call-done), kind=kOutput, calls=%fused_computation.91 | convolution fusion | flops 8592031744 | bytes 16777216 | tf_op jit(solution)/shard_map/dot_general | solution.py:204
  570.9 12.7 %fusion.123 = f32[2048,2048]{1,0:T(8,128)} fusion(bf16[2048,768]{0,1:T(8,128)(2,1)} %bitcast.227, bf16[2048,768]{0,1:T(8,128)(2,1)} %bitcast.235), kind=kOutput, calls=%fused_computation.159 | convolution fusion | flops 6442450944 | bytes 23068672 | tf_op jit(solution)/shard_map/dot_general | solution.py:210
  583.7 18.9 %add_bitcast_fusion = f32[1,2048,2048]{2,1,0:T(8,128)} fusion(f32[2048,2048]{1,0:T(8,128)} %fusion.123, bf16[2048,1024]{1,0:T(8,128)(2,1)S(1)} %copy-done.14, bf16[2048,1024]{1,0:T(8,128)(2,1)} %param.24), kind=kOutput, calls=%fused_computation.59 | convolution fusion | flops 8594128896 | bytes 41943040 | tf_op jit(solution)/shard_map/dot_general | solution.py:213
  602.7 14.0 %fusion.122 = f32[2048,2048]{1,0:T(8,128)S(1)} fusion(bf16[1024,2048]{1,0:T(8,128)(2,1)} %param.26, f32[2048,1024]{1,0:T(8,128)} %fusion.69, f32[1024]{0:T(1024)S(1)} %copy-done.31), kind=kOutput, calls=%fused_computation.158 | convolution fusion | flops 8610906112 | bytes 29364224 | tf_op jit(solution)/shard_map/dot_general | solution.py:179
  648.5 163.0 %all-reduce.5.cloned.1.call-done = (bf16[2048,3,256]{2,0,1:T(8,128)(2,1)}, bf16[256,2048]{1,0:T(8,128)(2,1)}, bf16[2048,1024]{1,0:T(8,128)(2,1)}, bf16[1024,2048]{1,0:T(8,128)(2,1)}) async-done(((bf16[2048,3,256]{2,0,1:T(8,128)(2,1)}, bf16[256,2048]{1,0:T(8,128)(2,1)}, bf16[2048,1024]{1,0:T(8,128)(2,1)}, bf16[1024,2048]{1,0:T(8,128)(2,1)}), (bf16[2048,3,256]{2,0,1:T(8,128)(2,1)}, ...) | async-done | bytes 12582928 | tf_op jit(solution)/shard_map/psum | solution.py:225
  827.7 154.4 %reduce-scatter.5.cloned.1.call-done = f32[1,256,2048]{2,1,0:T(8,128)} async-done(((f32[1,2048,2048]{2,1,0:T(8,128)}), f32[1,256,2048]{2,1,0:T(8,128)}) %reduce-scatter.5.cloned.1.call-update) | async-done | bytes 2097168 | tf_op jit(solution)/shard_map/reduce_scatter | solution.py:214
  984.6 39.7 %all-reduce = (f32[2048]{0:T(1024)}, f32[2048]{0:T(1024)}) all-reduce(f32[2048]{0:T(1024)S(1)} %get-tuple-element.154, f32[2048]{0:T(1024)S(1)} %get-tuple-element.157), channel_id=1, replica_groups=mesh['rows'=4,'tp'=8] {'rows','tp'}, use_global_device_ids=true, to_apply=%region_16.17 | all-reduce | flops 4096 | bytes 32768 | tf_op jit(solution)/shard_map/psum | solution.py:223
  1024.3 127.6 %reduce-scatter.3.cloned.1.call-done = f32[1,256,2048]{2,1,0:T(8,128)} async-done(((f32[1,2048,2048]{2,1,0:T(8,128)}), f32[1,256,2048]{2,1,0:T(8,128)}) %reduce-scatter.3.cloned.1.call-update) | async-done | bytes 2097168 | tf_op jit(solution)/shard_map/reduce_scatter | solution.py:181
  (276 shorter events, 355.0 us)
Async XLA Ops:
  7.2 174.6 %copy-start = (bf16[256,2048]{1,0:T(8,128)(2,1)S(1)}, bf16[256,2048]{1,0:T(8,128)(2,1)}, u32[]{:S(2)}) copy-start(bf16[256,2048]{1,0:T(8,128)(2,1)} %param.22) | copy-start | bytes 3145732
  7.2 27.5 %copy-start.28 = (f32[3,256]{1,0:T(4,128)S(1)}, f32[3,256]{1,0:T(4,128)}, u32[]{:S(2)}) copy-start(f32[3,256]{1,0:T(4,128)} %param.21) | copy-start | bytes 9220
  7.2 91.4 %all-gather.3.cloned.1.call-start = ((), (), s32[]{:S(2)}) async-start(), calls=%async_computation.2 | async-start | bytes 9437184 | tf_op jit(solution)/shard_map/all_gather | solution.py:156
  13.7 168.1 %all-gather.5.cloned.1.call-start = ((), (), s32[]{:S(2)}) async-start(), calls=%async_computation.4 | async-start | bytes 9437184 | tf_op jit(solution)/shard_map/all_gather | solution.py:185
  14.5 797.1 %all-reduce.5.cloned.1.call-start = ((), (), s32[]{:S(2)}) async-start(), calls=%async_computation.6 | async-start | bytes 25165824 | tf_op jit(solution)/shard_map/psum | solution.py:225
  35.9 73.4 %copy-start.18 = (f32[2048,16]{0,1:T(8,128)}, f32[2048,16]{0,1:T(8,128)S(1)}, u32[]{:S(2)}) copy-start(f32[2048,16]{0,1:T(8,128)S(1)} %get-tuple-element.227) | copy-start | bytes 393220
  206.8 15.0 %copy-start.1 = (f32[4,512,2048]{2,1,0:T(8,128)}, f32[4,512,2048]{2,1,0:T(8,128)S(1)}, u32[]{:S(2)}) copy-start(f32[4,512,2048]{2,1,0:T(8,128)S(1)} %fusion.173) | copy-start | bytes 50331652 | tf_op jit(solution)/shard_map/while
  232.7 18.9 %copy-start.5 = (f32[1,2048,4,64]{1,3,2,0:T(8,128)S(1)}, f32[1,2048,4,64]{1,3,2,0:T(8,128)}, u32[]{:S(2)}) copy-start(f32[1,2048,4,64]{1,3,2,0:T(8,128)} %get-tuple-element.406) | copy-start | bytes 6291460 | tf_op jit(solution)/shard_map/while
  277.6 15.0 %copy-start.1 = (f32[4,512,2048]{2,1,0:T(8,128)}, f32[4,512,2048]{2,1,0:T(8,128)S(1)}, u32[]{:S(2)}) copy-start(f32[4,512,2048]{2,1,0:T(8,128)S(1)} %fusion.173) | copy-start | bytes 50331652 | tf_op jit(solution)/shard_map/while
  303.5 18.9 %copy-start.5 = (f32[1,2048,4,64]{1,3,2,0:T(8,128)S(1)}, f32[1,2048,4,64]{1,3,2,0:T(8,128)}, u32[]{:S(2)}) copy-start(f32[1,2048,4,64]{1,3,2,0:T(8,128)} %get-tuple-element.406) | copy-start | bytes 6291460 | tf_op jit(solution)/shard_map/while
  348.9 15.0 %copy-start.1 = (f32[4,512,2048]{2,1,0:T(8,128)}, f32[4,512,2048]{2,1,0:T(8,128)S(1)}, u32[]{:S(2)}) copy-start(f32[4,512,2048]{2,1,0:T(8,128)S(1)} %fusion.173) | copy-start | bytes 50331652 | tf_op jit(solution)/shard_map/while
  374.8 18.9 %copy-start.5 = (f32[1,2048,4,64]{1,3,2,0:T(8,128)S(1)}, f32[1,2048,4,64]{1,3,2,0:T(8,128)}, u32[]{:S(2)}) copy-start(f32[1,2048,4,64]{1,3,2,0:T(8,128)} %get-tuple-element.406) | copy-start | bytes 6291460 | tf_op jit(solution)/shard_map/while
  420.2 15.0 %copy-start.1 = (f32[4,512,2048]{2,1,0:T(8,128)}, f32[4,512,2048]{2,1,0:T(8,128)S(1)}, u32[]{:S(2)}) copy-start(f32[4,512,2048]{2,1,0:T(8,128)S(1)} %fusion.173) | copy-start | bytes 50331652 | tf_op jit(solution)/shard_map/while
  446.2 18.9 %copy-start.5 = (f32[1,2048,4,64]{1,3,2,0:T(8,128)S(1)}, f32[1,2048,4,64]{1,3,2,0:T(8,128)}, u32[]{:S(2)}) copy-start(f32[1,2048,4,64]{1,3,2,0:T(8,128)} %get-tuple-element.406) | copy-start | bytes 6291460 | tf_op jit(solution)/shard_map/while
  499.1 43.1 %copy-start.11 = (bf16[1,2048,3,4,64]{1,4,3,2,0:T(8,128)(2,1)}, bf16[1,2048,3,4,64]{1,4,3,2,0:T(8,128)(2,1)S(1)}, u32[]{:S(2)}) copy-start(bf16[1,2048,3,4,64]{1,4,3,2,0:T(8,128)(2,1)S(1)} %maximum_convert_fusion) | copy-start | bytes 9437188
  542.2 15.8 %copy-start.13 = (bf16[2048,1024]{1,0:T(8,128)(2,1)}, bf16[2048,1024]{1,0:T(8,128)(2,1)S(1)}, u32[]{:S(2)}) copy-start(bf16[2048,1024]{1,0:T(8,128)(2,1)S(1)} %fusion.54) | copy-start | bytes 12582916
  570.9 411.2 %reduce-scatter.5.cloned.1.call-start = ((), (), s32[]{:S(2)}) async-start(), calls=%async_computation.5 | async-start | bytes 18874368 | tf_op jit(solution)/shard_map/reduce_scatter | solution.py:214
  602.6 549.3 %reduce-scatter.3.cloned.1.call-start = ((), (), s32[]{:S(2)}) async-start(), calls=%async_computation.3 | async-start | bytes 18874368 | tf_op jit(solution)/shard_map/reduce_scatter | solution.py:181
  822.8 159.2 %copy-start.10 = (bf16[1,256,2048]{2,1,0:T(8,128)(2,1)S(1)}, bf16[1,256,2048]{2,1,0:T(8,128)(2,1)}, u32[]{:S(2)}) copy-start(bf16[1,256,2048]{2,1,0:T(8,128)(2,1)} %param.16) | copy-start | bytes 3145732
  822.8 159.2 %copy-start.22 = (f32[2048]{0:T(1024)S(1)}, f32[2048]{0:T(1024)}, u32[]{:S(2)}) copy-start(f32[2048]{0:T(1024)} %param.18) | copy-start | bytes 24580
  822.8 159.2 %copy-start.24 = (f32[256]{0:T(256)S(1)}, f32[256]{0:T(256)}, u32[]{:S(2)}) copy-start(f32[256]{0:T(256)} %copy-done.23) | copy-start | bytes 3076
  822.8 159.2 %copy-start.26 = (f32[256]{0:T(256)S(1)}, f32[256]{0:T(256)}, u32[]{:S(2)}) copy-start(f32[256]{0:T(256)} %copy-done.25) | copy-start | bytes 3076
  822.9 329.1 %copy-start.15 = (bf16[1,256,2048]{2,1,0:T(8,128)(2,1)S(1)}, bf16[1,256,2048]{2,1,0:T(8,128)(2,1)}, u32[]{:S(2)}) copy-start(bf16[1,256,2048]{2,1,0:T(8,128)(2,1)} %param.27) | copy-start | bytes 3145732
  822.9 329.1 %copy-start.27 = (f32[2048]{0:T(1024)S(1)}, f32[2048]{0:T(1024)}, u32[]{:S(2)}) copy-start(f32[2048]{0:T(1024)} %param.23) | copy-start | bytes 24580
  (44 other events, 291.4 us)
Sparse Core Ops, SparseCore 0:
  13.8 84.7 all-gather.2
  100.2 80.5 all-gather.4
  571.0 240.5 all-reduce.4
  813.8 168.2 reduce-scatter.4
  984.3 167.6 reduce-scatter.2
where the time goes:
time: 1180 us; the launch traced here: 1160 us
  waiting for transfers between devices  508 us (43%)
  matrix products  359 us (30%)
  other arithmetic  116 us (10%)
  local copies, waits for them, and re-layouts  84.7 us (7%)
  blocking collectives  63.8 us (5%)
  loops' own time  17.1 us (1%)
  between operations  14.4 us (1%)
    psum x1, waiting for transfers between devices, local(): lax.psum(grad_w_qkv.astype(jnp.bfloat16), 'rows').astype(jnp.float32)  163 us
    reduce_scatter x1, waiting for transfers between devices, local(): lax.psum_scatter(part_qkv + part_up, 'tp', scatter_dimension=1, tiled=True)  154 us
    reduce_scatter x1, waiting for transfers between devices, local(): lax.psum_scatter((attention_part + mlp_part).reshape(full_shape), 'tp', s...  128 us
    all_gather x1, waiting for transfers between devices, local(): lax.all_gather(normed, 'tp', axis=1, tiled=True)  62.7 us
    dot_general x4, matrix products, one_block(): jnp.einsum('rqhe,rkhe->rhqk', grad_block, value_vecs, preferred_element_t...  52.5 us
    dynamic_update_slice x8, local copies, waits for them, and re-layouts, attend_backward(): lax.scan(one_block, (empty, empty), (jnp.arange(blocks, dtype=jnp.int32),...  49.9 us
    dot_general x4, matrix products, one_block(): jnp.einsum('rhqk,rqhe->rkhe', probs, grad_block, preferred_element_type=j...  49.4 us
    convert_element_type x4, other arithmetic, one_block(): grad_scores = (soft * (grad_probs - inner)).astype(jnp.bfloat16)  43.8 us
  transfers between devices with their start and end apart: 5, of which 4 were waited for; matrix products, arithmetic and copies ran while one was open for 15% of the time, Pallas kernels for 0%

commit v1 on v0

v1 whole, which is shorter than its diff:
```python
from functools import partial
import math

import jax
import jax.numpy as jnp
from jax import lax
from jax.experimental import pallas as pl
from jax.experimental.pallas import tpu as pltpu
from jax.sharding import PartitionSpec as P

HEAD_DIM = 64
ROT = 32
EPSILON = 1e-05
NEGATIVE = -1e30
VMEM_BYTES = 56 * 2**20


def lane_heads(rows, width):
    return lax.broadcasted_iota(jnp.int32, (rows, width), 1) // HEAD_DIM


def swap_pairs(x):
    width = x.shape[1]
    lane = lax.broadcasted_iota(jnp.int32, x.shape, 1) % HEAD_DIM
    up = pltpu.roll(x, width - ROT // 2, 1)
    down = pltpu.roll(x, ROT // 2, 1)
    return jnp.where(lane < ROT // 2, up, down)


def mask_bias(starts, key_first, query_first, block):
    key_index = key_first + lax.broadcasted_iota(jnp.int32, (block, block), 0)
    query_index = query_first + lax.broadcasted_iota(jnp.int32, (block, block), 1)
    allowed = (key_index >= starts) & (key_index <= query_index)
    return jnp.where(allowed, 0.0, NEGATIVE).astype(jnp.float32)


NT = (((1,), (1,)), ((), ()))


def forward_kernel(lows, starts, q, k, v, context, lse, v_t, acc):
    block, width = q.shape
    heads = width // HEAD_DIM
    length = k.shape[0]
    i = pl.program_id(0)

    @pl.when(i == 0)
    def _():
        for j in range(length // block):
            rows = pl.ds(j * block, block)
            v_t[:, rows] = v[rows, :].T

    row_heads = lane_heads(block, width)
    scaled = q[...] * 0.125
    masked = [jnp.where(row_heads == h, scaled, 0).astype(jnp.bfloat16) for h in range(heads)]
    acc[...] = jnp.zeros_like(acc)

    def step(j, carry):
        tops, sums = carry
        first = pl.multiple_of(j * block, block)
        keys = k[pl.ds(first, block), :]
        bias = mask_bias(starts[0:1, :], first, i * block, block)
        new_tops, new_sums = [], []
        for h in range(heads):
            rows = pl.ds(h * HEAD_DIM, HEAD_DIM)
            scores = lax.dot_general(keys, masked[h], NT, preferred_element_type=jnp.float32) + bias
            top = jnp.maximum(tops[h], jnp.max(scores, axis=0, keepdims=True))
            weights = jnp.exp(scores - top)
            keep = jnp.exp(tops[h] - top)
            new_tops.append(top)
            new_sums.append(sums[h] * keep + jnp.sum(weights, axis=0, keepdims=True))
            acc[rows, :] = acc[rows, :] * keep + jnp.dot(
                v_t[rows, pl.ds(first, block)],
                weights.astype(jnp.bfloat16),
                preferred_element_type=jnp.float32,
            )
        return tuple(new_tops), tuple(new_sums)

    empty = tuple(jnp.full((1, block), NEGATIVE, jnp.float32) for _ in range(heads))
    nothing = tuple(jnp.zeros((1, block), jnp.float32) for _ in range(heads))
    tops, sums = lax.fori_loop(lows[i], i + 1, step, (empty, nothing))
    for h in range(heads):
        rows = pl.ds(h * HEAD_DIM, HEAD_DIM)
        acc[rows, :] = acc[rows, :] / sums[h]
        lse[h : h + 1, :] = tops[h] + jnp.log(sums[h])
    context[...] = acc[...].T.astype(jnp.bfloat16)


def attend_forward(lows, starts, mixed, block):
    length, triple = mixed.shape
    width = triple // 3
    blocks = length // block
    return pl.pallas_call(
        forward_kernel,
        grid_spec=pltpu.PrefetchScalarGridSpec(
            num_scalar_prefetch=1,
            grid=(blocks,),
            in_specs=[
                pl.BlockSpec((8, block), lambda i, lows: (0, i)),
                pl.BlockSpec((block, width), lambda i, lows: (i, 0)),
                pl.BlockSpec((length, width), lambda i, lows: (0, 1)),
                pl.BlockSpec((length, width), lambda i, lows: (0, 2)),
            ],
            out_specs=[
                pl.BlockSpec((block, width), lambda i, lows: (i, 0)),
                pl.BlockSpec((8, block), lambda i, lows: (0, i)),
            ],
            scratch_shapes=[
                pltpu.VMEM((width, length), jnp.bfloat16),
                pltpu.VMEM((width, block), jnp.float32),
            ],
        ),
        out_shape=[
            jax.ShapeDtypeStruct((length, width), jnp.bfloat16),
            jax.ShapeDtypeStruct((8, length), jnp.float32),
        ],
        compiler_params=pltpu.CompilerParams(vmem_limit_bytes=VMEM_BYTES),
        cost_estimate=pl.CostEstimate(
            flops=2 * length * length * width * 8,
            bytes_accessed=length * width * 8,
            transcendentals=0,
        ),
        name="attend_forward",
    )(lows, starts, mixed, mixed, mixed)


def backward_kernel(
    lows, starts, lse, q, k, v, context, grad, cosine, sine, grad_mixed, k_t, grad_q, grad_k, grad_v
):
    block, width = q.shape
    heads = width // HEAD_DIM
    length = k.shape[0]
    i = pl.program_id(0)
    blocks = length // block

    @pl.when(i == 0)
    def _():
        grad_k[...] = jnp.zeros_like(grad_k)
        grad_v[...] = jnp.zeros_like(grad_v)
        for j in range(blocks):
            rows = pl.ds(j * block, block)
            k_t[:, rows] = k[rows, :].T

    row_heads = lane_heads(block, width)
    scaled = q[...] * 0.125
    grads = grad[...]
    masked_q = [jnp.where(row_heads == h, scaled, 0).astype(jnp.bfloat16) for h in range(heads)]
    masked_g = [jnp.where(row_heads == h, grads, 0).astype(jnp.bfloat16) for h in range(heads)]
    products = (grads.astype(jnp.float32) * context[...].astype(jnp.float32)).T
    inner = [
        jnp.sum(products[h * HEAD_DIM : (h + 1) * HEAD_DIM, :], axis=0, keepdims=True)
        for h in range(heads)
    ]
    grad_q[...] = jnp.zeros_like(grad_q)

    def step(j, carry):
        first = pl.multiple_of(j * block, block)
        here = pl.ds(first, block)
        keys = k[here, :]
        values = v[here, :]
        bias = mask_bias(starts[0:1, :], first, i * block, block)
        probs, slopes = [], []
        for h in range(heads):
            rows = pl.ds(h * HEAD_DIM, HEAD_DIM)
            scores = lax.dot_general(
                keys, masked_q[h], NT, preferred_element_type=jnp.float32
            )
            soft = jnp.exp(scores + bias - lse[h : h + 1, :])
            grad_probs = lax.dot_general(
                values, masked_g[h], NT, preferred_element_type=jnp.float32
            )
            slope = (soft * (grad_probs - inner[h])).astype(jnp.bfloat16)
            grad_q[rows, :] += jnp.dot(k_t[rows, here], slope, preferred_element_type=jnp.float32)
            probs.append(soft.astype(jnp.bfloat16))
            slopes.append(slope)
        grad_v[here, :] += jnp.dot(
            jnp.concatenate(probs, axis=1),
            jnp.concatenate(masked_g, axis=0),
            preferred_element_type=jnp.float32,
        )
        grad_k[here, :] += jnp.dot(
            jnp.concatenate(slopes, axis=1),
            jnp.concatenate(masked_q, axis=0),
            preferred_element_type=jnp.float32,
        )
        return carry

    lax.fori_loop(lows[i], i + 1, step, 0)

    def unrotate(x, rows):
        parts = []
        for part in range(width // 128):
            piece = x[:, part * 128 : (part + 1) * 128]
            parts.append(piece * cosine[rows, :] - swap_pairs(piece) * sine[rows, :])
        return jnp.concatenate(parts, axis=1).astype(jnp.bfloat16)

    mine = pl.ds(pl.multiple_of(i * block, block), block)
    grad_mixed[mine, 0:width] = unrotate(grad_q[...].T * 0.125, mine)

    @pl.when(i == blocks - 1)
    def _():
        def finish(j, carry):
            rows = pl.ds(pl.multiple_of(j * block, block), block)
            grad_mixed[rows, width : 2 * width] = unrotate(grad_k[rows, :], rows)
            grad_mixed[rows, 2 * width : 3 * width] = grad_v[rows, :].astype(jnp.bfloat16)
            return carry

        lax.fori_loop(0, blocks, finish, 0)


def attend_backward(lows, starts, lse, mixed, context, grad_context, cosine, sine, block):
    length, triple = mixed.shape
    width = triple // 3
    blocks = length // block
    whole = lambda i, lows: (0, 0)
    row = lambda i, lows: (i, 0)
    column = lambda i, lows: (0, i)
    return pl.pallas_call(
        backward_kernel,
        grid_spec=pltpu.PrefetchScalarGridSpec(
            num_scalar_prefetch=1,
            grid=(blocks,),
            in_specs=[
                pl.BlockSpec((8, block), column),
                pl.BlockSpec((8, block), column),
                pl.BlockSpec((block, width), row),
                pl.BlockSpec((length, width), lambda i, lows: (0, 1)),
                pl.BlockSpec((length, width), lambda i, lows: (0, 2)),
                pl.BlockSpec((block, width), row),
                pl.BlockSpec((block, width), row),
                pl.BlockSpec((length, 128), whole),
                pl.BlockSpec((length, 128), whole),
            ],
            out_specs=pl.BlockSpec((length, triple), whole),
            scratch_shapes=[
                pltpu.VMEM((width, length), jnp.bfloat16),
                pltpu.VMEM((width, block), jnp.float32),
                pltpu.VMEM((length, width), jnp.float32),
                pltpu.VMEM((length, width), jnp.float32),
            ],
        ),
        out_shape=jax.ShapeDtypeStruct((length, triple), jnp.bfloat16),
        compiler_params=pltpu.CompilerParams(vmem_limit_bytes=VMEM_BYTES),
        cost_estimate=pl.CostEstimate(
            flops=2 * length * length * width * 20,
            bytes_accessed=length * width * 24,
            transcendentals=0,
        ),
        name="attend_backward",
    )(lows, starts, lse, mixed, mixed, mixed, context, grad_context, cosine, sine)


def positions_of(segments):
    ids = jnp.arange(8, dtype=jnp.int32)
    counts = jnp.sum((segments[None, :] < ids[:, None]).astype(jnp.int32), axis=1)
    return jnp.sum(jnp.where(segments[None, :] == ids[:, None], counts[:, None], 0), axis=0)


def rotary_tables(positions):
    lane = jnp.arange(128, dtype=jnp.int32) % HEAD_DIM
    step = (lane % (ROT // 2)).astype(jnp.float32)
    inverse = jnp.exp(step * (-2.0 * math.log(10000.0) / ROT))
    angles = positions.astype(jnp.float32)[:, None] * inverse[None, :]
    rotated = (lane < ROT)[None, :]
    cosine = jnp.where(rotated, jnp.cos(angles), 1.0)
    sine = jnp.where(rotated, jnp.where((lane < ROT // 2)[None, :], -1.0, 1.0) * jnp.sin(angles), 0.0)
    return cosine, sine


def gelu_pair(u):
    scale = math.sqrt(2.0 / math.pi)
    square = u * u
    bent = jnp.tanh(scale * u * (1.0 + 0.044715 * square))
    half = 0.5 * (1.0 + bent)
    slope = half + 0.5 * u * (1.0 - bent * bent) * (scale * (1.0 + 3 * 0.044715 * square))
    return u * half, slope


def project_kernel(
    place, x, gain, shift, w_qkv, b_qkv, w_up, b_up, cosine, sine, *refs
):
    normed, mixed, activated, slope = refs[-4:]
    n = pl.program_id(0)

    @pl.when(n == 0)
    def _():
        wide = x[...].astype(jnp.float32)
        centred = wide - jnp.mean(wide, axis=1, keepdims=True)
        inverse_std = lax.rsqrt(jnp.mean(centred * centred, axis=1, keepdims=True) + EPSILON)
        normed[...] = (centred * inverse_std * gain[...] + shift[...]).astype(jnp.bfloat16)

    @pl.when(n < 3)
    def _():
        y = jnp.dot(normed[...], w_qkv[...], preferred_element_type=jnp.float32) + b_qkv[...]

        @pl.when(n < 2)
        def _():
            parts = []
            for part in range(y.shape[1] // 128):
                piece = y[:, part * 128 : (part + 1) * 128]
                parts.append(piece * cosine[...] + swap_pairs(piece) * sine[...])
            mixed[...] = jnp.concatenate(parts, axis=1).astype(jnp.bfloat16)

        @pl.when(n == 2)
        def _():
            mixed[...] = y.astype(jnp.bfloat16)

    @pl.when(n >= 3)
    def _():
        u = jnp.dot(normed[...], w_up[...], preferred_element_type=jnp.float32) + b_up[...]
        high, tilt = gelu_pair(u)
        activated[...] = high.astype(jnp.bfloat16)
        slope[...] = tilt.astype(jnp.bfloat16)


def project(place, x, weights, tables, length, carried):
    gain, shift, w_qkv, b_qkv, w_up, b_up = weights
    block, width = x.shape
    local_width = w_qkv.shape[1] // 3
    hidden = w_up.shape[1]
    tile = min(256, hidden)
    whole = lambda n, place: (0, 0)
    qkv = lambda n, place: (0, jnp.minimum(n, 2))
    up = lambda n, place: (0, jnp.maximum(n - 3, 0))
    here = lambda n, place: (place[0], 0)
    in_specs = [
        pl.BlockSpec((block, width), whole),
        pl.BlockSpec((1, width), whole),
        pl.BlockSpec((1, width), whole),
        pl.BlockSpec((width, local_width), qkv),
        pl.BlockSpec((1, local_width), qkv),
        pl.BlockSpec((width, tile), up),
        pl.BlockSpec((1, tile), up),
        pl.BlockSpec((block, 128), here),
        pl.BlockSpec((block, 128), here),
    ]
    out_specs = [
        pl.BlockSpec((block, width), here),
        pl.BlockSpec((block, local_width), lambda n, place: (place[0], jnp.minimum(n, 2))),
        pl.BlockSpec((block, tile), lambda n, place: (place[0], jnp.maximum(n - 3, 0))),
        pl.BlockSpec((block, tile), lambda n, place: (place[0], jnp.maximum(n - 3, 0))),
    ]
    out_shape = [
        jax.ShapeDtypeStruct((length, columns), jnp.bfloat16)
        for columns in (width, 3 * local_width, hidden, hidden)
    ]
    operands = [place, x, gain, shift, w_qkv, b_qkv, w_up, b_up, *tables]
    aliases = {}
    if carried is not None:
        aliases = {len(operands) + i: i for i in range(4)}
        operands += list(carried)
        in_specs += [pl.BlockSpec(memory_space=pl.ANY)] * 4
    return pl.pallas_call(
        project_kernel,
        grid_spec=pltpu.PrefetchScalarGridSpec(
            num_scalar_prefetch=1,
            grid=(3 + hidden // tile,),
            in_specs=in_specs,
            out_specs=out_specs,
        ),
        out_shape=out_shape,
        input_output_aliases=aliases,
        compiler_params=pltpu.CompilerParams(vmem_limit_bytes=VMEM_BYTES),
        cost_estimate=pl.CostEstimate(
            flops=2 * block * width * (3 * local_width + hidden),
            bytes_accessed=2 * width * (3 * local_width + hidden) + 4 * block * width,
            transcendentals=0,
        ),
        name="project",
    )(*operands)


def finish_kernel(order, row_a, far_a, row_b, far_b, *outs):
    s = pl.program_id(0)
    for index, source in enumerate((row_a, far_a, row_b, far_b)):

        @pl.when(s // 2 == index)
        def _(source=source):
            start = 0
            for out in outs:
                rows = out.shape[0]
                out[...] = source[0, start : start + rows, :].astype(jnp.float32)
                start += rows


def finish(order, pieces, splits):
    _, rows, columns = pieces[0].shape
    in_specs = [
        pl.BlockSpec(
            (1, rows, columns),
            lambda s, order, i=i: (jnp.clip(s - 2 * i, 0, 1), 0, 0),
        )
        for i in range(4)
    ]
    return pl.pallas_call(
        finish_kernel,
        grid_spec=pltpu.PrefetchScalarGridSpec(
            num_scalar_prefetch=1,
            grid=(8,),
            in_specs=in_specs,
            out_specs=[
                pl.BlockSpec((part, columns), lambda s, order: (order[s], 0)) for part in splits
            ],
        ),
        out_shape=[jax.ShapeDtypeStruct((8 * part, columns), jnp.float32) for part in splits],
        compiler_params=pltpu.CompilerParams(vmem_limit_bytes=VMEM_BYTES),
        cost_estimate=pl.CostEstimate(
            flops=0, bytes_accessed=8 * rows * columns * 6, transcendentals=0
        ),
        name="finish",
    )(order, *pieces)


def add_low(one, other):
    return (one.astype(jnp.float32) + other.astype(jnp.float32)).astype(jnp.bfloat16)


def swap_rows(array, bit):
    return lax.ppermute(array, "rows", [(i, i ^ bit) for i in range(4)])


def sum_rows(parts, splits):
    row = lax.axis_index("rows")
    x, y = row % 2, row // 2
    pieces, order = [], []
    for half, (first, second, first_bit, second_bit) in enumerate(((x, y, 1, 2), (y, x, 2, 1))):
        group = parts[4 * half : 4 * half + 4].reshape(2, 2, *parts.shape[1:])
        away = lax.dynamic_index_in_dim(group, 1 - first, 0, False)
        keep = lax.dynamic_index_in_dim(group, first, 0, False)
        near = add_low(keep, swap_rows(away, first_bit))
        away = lax.dynamic_index_in_dim(near, 1 - second, 0, True)
        keep = lax.dynamic_index_in_dim(near, second, 0, True)
        own = add_low(keep, swap_rows(away, second_bit))
        other = swap_rows(own, second_bit)
        line = jnp.where(
            second == 0,
            jnp.concatenate([own, other], axis=0),
            jnp.concatenate([other, own], axis=0),
        )
        pieces += [line, swap_rows(line, first_bit)]
        for base in (2 * first, 2 * (1 - first)):
            order += [4 * half + base, 4 * half + base + 1]
    return finish(jnp.stack(order).astype(jnp.int32), pieces, splits)


def sum_all(array, rows, tp):
    for axis, size in (("tp", tp), ("rows", rows)):
        step = 1
        while step < size:
            array = array + lax.ppermute(array, axis, [(i, i ^ step) for i in range(size)])
            step *= 2
    return array


def token_sum(matrix):
    ones_row = jnp.ones((1, matrix.shape[0]), matrix.dtype)
    return jnp.dot(ones_row, matrix, preferred_element_type=jnp.float32)[0]


def transposed_dot(left, right):
    return lax.dot_general(
        left, right, (((0,), (0,)), ((), ())), preferred_element_type=jnp.float32
    )


def dot_transposed(left, right):
    return lax.dot_general(left, right, NT, preferred_element_type=jnp.float32)


def local(
    rows,
    tp,
    hidden_in,
    segment_ids,
    ln_gain,
    ln_bias,
    w_qkv,
    b_qkv,
    w_out,
    out_bias,
    w_up,
    b_up,
    w_down,
    cotangent,
):
    x = hidden_in[0]
    block, width = x.shape
    length = block * tp
    local_width = w_qkv.shape[2]
    hidden = w_up.shape[1]
    chips = tp // 2
    me = lax.axis_index("tp")
    chip, core = me // 2, me % 2

    around = [(i, (i + 2) % tp) for i in range(tp)]
    sibling = [(i, i ^ 1) for i in range(tp)]
    segments = lax.all_gather(segment_ids[0], "tp", axis=0, tiled=True)
    starts = positions_of(segments)
    tables = rotary_tables(jnp.arange(length, dtype=jnp.int32) - starts)
    lows = starts[::block] // block
    starts = jnp.broadcast_to(starts[None], (8, length))

    qkv_matrix = w_qkv.reshape(width, 3 * local_width)
    weights = (
        ln_gain.reshape(1, width),
        ln_bias.reshape(1, width),
        qkv_matrix,
        b_qkv.reshape(1, 3 * local_width),
        w_up,
        b_up.reshape(1, hidden),
    )
    carried = None
    travelling = x
    for s in range(chips):
        if s > 0:
            travelling = lax.ppermute(travelling, "tp", around)
        source = (chip - s + chips) % chips
        for flip, piece in enumerate((travelling, lax.ppermute(travelling, "tp", sibling))):
            place = (2 * source + (core ^ flip)).astype(jnp.int32).reshape(1)
            carried = project(place, piece, weights, tables, length, carried)
    normed, mixed, activated, slope = carried

    chunks = 2
    columns = width // chunks
    grads = [
        lax.all_gather(
            cotangent[0, :, c * columns : (c + 1) * columns], "tp", axis=0, tiled=True
        )
        for c in range(chunks)
    ]
    context, lse = attend_forward(lows, starts, mixed, block)

    w_down_parts, w_out_parts = [], []
    for grad in grads:
        low = transposed_dot(activated, grad).astype(jnp.bfloat16)
        low_out = transposed_dot(context, grad).astype(jnp.bfloat16)
        if rows == 4:
            parts = jnp.concatenate(
                [low.reshape(8, hidden // 8, columns), low_out.reshape(8, local_width // 8, columns)],
                axis=1,
            )
            total, total_out = sum_rows(parts, (hidden // 8, local_width // 8))
        else:
            total = lax.psum(low, "rows").astype(jnp.float32)
            total_out = lax.psum(low_out, "rows").astype(jnp.float32)
        w_down_parts.append(total)
        w_out_parts.append(total_out)
    grad_w_down = jnp.concatenate(w_down_parts, axis=1)
    grad_w_out = jnp.concatenate(w_out_parts, axis=1)

    grad_whole = jnp.concatenate(grads, axis=1)
    grad_up = (dot_transposed(grad_whole, w_down) * slope.astype(jnp.float32)).astype(jnp.bfloat16)
    grad_context = dot_transposed(grad_whole, w_out).astype(jnp.bfloat16)

    def reduce_weight(partial_sum):
        low = partial_sum.astype(jnp.bfloat16)
        if rows == 4:
            tall, wide = low.shape
            return sum_rows(low.reshape(8, tall // 8, wide), (tall // 8,))[0]
        return lax.psum(low, "rows").astype(jnp.float32)

    grad_w_up = reduce_weight(transposed_dot(normed, grad_up))
    grad_mixed = attend_backward(lows, starts, lse, mixed, context, grad_context, *tables, block)
    grad_w_qkv = reduce_weight(transposed_dot(normed, grad_mixed)).reshape(width, 3, local_width)

    branch = (
        jnp.dot(context, w_out, preferred_element_type=jnp.float32)
        + jnp.dot(activated, w_down, preferred_element_type=jnp.float32)
    ).astype(jnp.bfloat16)
    branch_total = lax.psum_scatter(branch, "tp", scatter_dimension=0, tiled=True)
    inputs = x.astype(jnp.float32)
    hidden_out = (inputs + branch_total.astype(jnp.float32) + out_bias).astype(jnp.bfloat16)

    part = (
        dot_transposed(grad_mixed, qkv_matrix) + dot_transposed(grad_up, w_up)
    ).astype(jnp.bfloat16)
    grad_normed = lax.psum_scatter(part, "tp", scatter_dimension=0, tiled=True).astype(jnp.float32)

    average = jnp.mean(inputs, axis=-1, keepdims=True)
    centred = inputs - average
    inverse_std = lax.rsqrt(jnp.mean(centred * centred, axis=-1, keepdims=True) + EPSILON)
    unit_rows = centred * inverse_std
    gain_terms = jnp.sum(grad_normed * unit_rows, axis=0)
    bias_terms = jnp.sum(grad_normed, axis=0)
    grad_unit = grad_normed * ln_gain
    grad_input = cotangent[0].astype(jnp.float32) + inverse_std * (
        grad_unit
        - jnp.mean(grad_unit, axis=-1, keepdims=True)
        - unit_rows * jnp.mean(grad_unit * unit_rows, axis=-1, keepdims=True)
    )
    small = lax.psum(jnp.concatenate([token_sum(grad_mixed), token_sum(grad_up)]), "rows")
    grad_b_qkv = small[: 3 * local_width].reshape(3, local_width)
    grad_b_up = small[3 * local_width :]
    tail = sum_all(jnp.stack([gain_terms, bias_terms, token_sum(cotangent[0])]), rows, tp)
    return (
        hidden_out[None],
        grad_input.astype(jnp.bfloat16)[None],
        tail[0],
        tail[1],
        grad_w_qkv,
        grad_b_qkv,
        grad_w_out,
        tail[2],
        grad_w_up,
        grad_b_up,
        grad_w_down,
    )


def solution(mesh):
    in_specs = (
        P("rows", "tp", None),
        P("rows", "tp"),
        P(),
        P(),
        P(None, None, "tp"),
        P(None, "tp"),
        P("tp", None),
        P(),
        P(None, "tp"),
        P("tp"),
        P("tp", None),
        P("rows", "tp", None),
    )
    out_specs = (
        P("rows", "tp", None),
        P("rows", "tp", None),
        P(),
        P(),
        P(None, None, "tp"),
        P(None, "tp"),
        P("tp", None),
        P(),
        P(None, "tp"),
        P("tp"),
        P("tp", None),
    )
    return jax.shard_map(
        partial(local, mesh.shape["rows"], mesh.shape["tp"]),
        mesh=mesh,
        in_specs=in_specs,
        out_specs=out_specs,
        check_vma=False,
    )
```

time: 1180 us -> 679 us (0.58)
  waiting for transfers between devices: 508 us -> 137 us
  matrix products: 359 us -> 118 us
  Pallas kernels: 0 us -> 185 us
  other arithmetic: 116 us -> 53.4 us
  starting transfers between devices: 0.2 us -> 55.6 us
  local copies, waits for them, and re-layouts: 84.7 us -> 38.8 us
  loops' own time: 17.1 us -> 0 us
    reduce_scatter x2, waiting for transfers between devices: 282 us -> 0.01 us  [the longest x1 0.01 us: local(): lax.psum_scatter(part, 'tp', scatter_dimension=0, tiled=True)]
    dot_general x40 -> x12, matrix products: 348 us -> 117 us  [the longest x4 55.9 us: dot_transposed(): return lax.dot_general(left, right, NT, preferred_element_type=jnp.float32)]
    pallas_call x0 -> x14, Pallas kernels: none -> 185 us  [the longest x8 81.8 us: project(): pl.pallas_call(project_kernel, grid_spec=pltpu.PrefetchScalarGridSpec(num...]
    psum x1 -> x0, waiting for transfers between devices: 163 us -> none  [local(): lax.psum(grad_w_qkv.astype(jnp.bfloat16), 'rows').astype(jnp.float32)]
    ppermute x0 -> x44, waiting for transfers between devices: none -> 136 us  [the longest x32 81.9 us: swap_rows(): return lax.ppermute(array, 'rows', [(i, i ^ bit) for i in range(4)])]
    all_gather x2, waiting for transfers between devices: 62.7 us -> 0.02 us  [local(): lax.all_gather(cotangent[0, :, c * columns:(c + 1) * columns], 'tp', axis...]
    ppermute x0 -> x44, starting transfers between devices: none -> 55.4 us  [the longest x32 33.2 us: swap_rows(): return lax.ppermute(array, 'rows', [(i, i ^ bit) for i in range(4)])]
    convert_element_type x17 -> x18, other arithmetic: 71.2 us -> 16.3 us  [the longest x16 9.11 us: add_low(): (one.astype(jnp.float32) + other.astype(jnp.float32)).astype(jnp.bfloat16)]
  transfers between devices with their start and end apart: 5 -> 48, of which waited for: 4 -> 16; matrix products, arithmetic and copies ran while one was open for 15% -> 21% of each run, Pallas kernels for 0% -> 21%
where the time goes in v1:
time: 679 us; the launch traced here: 673 us
  Pallas kernels  185 us (27%)
  waiting for transfers between devices  137 us (20%)
  matrix products  118 us (17%)
  blocking collectives  70.3 us (10%)
  starting transfers between devices  55.6 us (8%)
  other arithmetic  53.4 us (8%)
  local copies, waits for them, and re-layouts  38.8 us (6%)
  between operations  15 us (2%)
    ppermute x32, waiting for transfers between devices, swap_rows(): return lax.ppermute(array, 'rows', [(i, i ^ bit) for i in range(4)])  81.9 us
    pallas_call x8, Pallas kernels, project(): pl.pallas_call(project_kernel, grid_spec=pltpu.PrefetchScalarGridSpec(num...  81.8 us
    dot_general x4, matrix products, dot_transposed(): return lax.dot_general(left, right, NT, preferred_element_type=jnp.float32)  55.9 us
    all_gather x1, blocking collectives, local(): segments = lax.all_gather(segment_ids[0], 'tp', axis=0, tiled=True)  48.3 us
    ppermute x3, waiting for transfers between devices, local(): travelling = lax.ppermute(travelling, 'tp', around)  46.9 us
    pallas_call x1, Pallas kernels, attend_backward(): pl.pallas_call(backward_kernel, grid_spec=pltpu.PrefetchScalarGridSpec(nu...  43.4 us
    ppermute x32, starting transfers between devices, swap_rows(): return lax.ppermute(array, 'rows', [(i, i ^ bit) for i in range(4)])  33.2 us
    dot_general x6, matrix products, transposed_dot(): lax.dot_general(left, right, (((0,), (0,)), ((), ())), preferred_element_...  33.1 us
  transfers between devices with their start and end apart: 48, of which 16 were waited for; matrix products, arithmetic and copies ran while one was open for 21% of the time, Pallas kernels for 21%

profile of v1, /device:TPU:0, one launch (start us, length us, event | category | flops | bytes accessed | tf_op | source)
XLA Modules:
  0.0 673.3 jit_solution(17264724172103436396)
XLA Ops:
  13.6 39.9 %collective-permute-done.x = bf16[256,2048]{1,0:T(8,128)(2,1)S(1)} collective-permute-done((bf16[256,2048]{1,0:T(8,128)(2,1)S(1)}, bf16[256,2048]{1,0:T(8,128)(2,1)S(1)}, u32[]{:S(2)}, u32[]{:S(2)}) %collective-permute-start) | collective-permute-done | bytes 1048608 | tf_op jit(solution)/shard_map/ppermute | solution.py:515
  53.5 15.6 %collective-permute-start.1 = (bf16[256,2048]{1,0:T(8,128)(2,1)S(1)}, bf16[256,2048]{1,0:T(8,128)(2,1)}, u32[]{:S(2)}, u32[]{:S(2)}) collective-permute-start(bf16[256,2048]{1,0:T(8,128)(2,1)S(1)} %collective-permute-done.x), channel_id=1, source_target_pairs={{0,2},{1,3},{2,4},{3,5},{4,6},{5,7},{6,0},{7,1},{8,10},{9,11},{10,... | collective-permute-start | bytes 3145736 | tf_op jit(solution)/shard_map/ppermute | solution.py:515
  69.1 48.3 %all-gather = s32[1,2048]{1,0:T(1,128)S(1)} all-gather(s32[1,256]{1,0:T(1,128)S(1)} %copy-done.31), channel_id=2, replica_groups=mesh['rows'=4,'tp'=8] {'tp'}, dimensions={1}, use_global_device_ids=true | all-gather | bytes 9216 | tf_op jit(solution)/shard_map/all_gather | solution.py:496
  134.1 10.1 %project.8 = (bf16[2048,2048]{1,0:T(8,128)(2,1)}, bf16[2048,768]{1,0:T(8,128)(2,1)}, bf16[2048,1024]{1,0:T(8,128)(2,1)}, bf16[2048,1024]{1,0:T(8,128)(2,1)}) custom-call(s32[1]{0:T(128)} %bitcast.13.place, bf16[256,2048]{1,0:T(8,128)(2,1)} %bitcast.131, f32[1,2048]{1,0:T(1,128)} %bitcast.155, f32[1,2048]{1,0:T(1,128)} %bitcast.165, ...), custom_call_target="tpu_custom_call" | custom-call | flops 1879048192 | bytes 9437184 | tf_op jit(solution)/shard_map/project/pallas_call | solution.py:352
  151.8 10.5 %project.9 = (bf16[2048,2048]{1,0:T(8,128)(2,1)}, bf16[2048,768]{1,0:T(8,128)(2,1)}, bf16[2048,1024]{1,0:T(8,128)(2,1)}, bf16[2048,1024]{1,0:T(8,128)(2,1)}) custom-call(s32[1]{0:T(128)} %bitcast.12.place, bf16[256,2048]{1,0:T(8,128)(2,1)} %collective-permute-done.6.x, ...), custom_call_target="tpu_custom_call", output_to_operand_aliasing={{0}: (10, {}), {1}: (11, {}), {2}: (12, {}), {3}: (13, {})} | custom-call | flops 1879048192 | bytes 9437184 | tf_op jit(solution)/shard_map/project/pallas_call | solution.py:352
  162.3 10.2 %project.10 = (bf16[2048,2048]{1,0:T(8,128)(2,1)}, bf16[2048,768]{1,0:T(8,128)(2,1)}, bf16[2048,1024]{1,0:T(8,128)(2,1)}, bf16[2048,1024]{1,0:T(8,128)(2,1)}) custom-call(s32[1]{0:T(128)} %bitcast.11.place, bf16[256,2048]{1,0:T(8,128)(2,1)} %copy-done.14, ...), custom_call_target="tpu_custom_call", output_to_operand_aliasing={{0}: (10, {}), {1}: (11, {}), {2}: (12, {}), {3}: (13, {})} | custom-call | flops 1879048192 | bytes 9437184 | tf_op jit(solution)/shard_map/project/pallas_call | solution.py:352
  173.5 10.1 %project.11 = (bf16[2048,2048]{1,0:T(8,128)(2,1)}, bf16[2048,768]{1,0:T(8,128)(2,1)}, bf16[2048,1024]{1,0:T(8,128)(2,1)}, bf16[2048,1024]{1,0:T(8,128)(2,1)}) custom-call(s32[1]{0:T(128)} %bitcast.10.place, bf16[256,2048]{1,0:T(8,128)(2,1)} %copy-done.17, ...), custom_call_target="tpu_custom_call", output_to_operand_aliasing={{0}: (10, {}), {1}: (11, {}), {2}: (12, {}), {3}: (13, {})} | custom-call | flops 1879048192 | bytes 9437184 | tf_op jit(solution)/shard_map/project/pallas_call | solution.py:352
  183.6 10.2 %project.12 = (bf16[2048,2048]{1,0:T(8,128)(2,1)}, bf16[2048,768]{1,0:T(8,128)(2,1)}, bf16[2048,1024]{1,0:T(8,128)(2,1)}, bf16[2048,1024]{1,0:T(8,128)(2,1)}) custom-call(s32[1]{0:T(128)} %bitcast.9.place, bf16[256,2048]{1,0:T(8,128)(2,1)} %collective-permute-done.1.x, ...), custom_call_target="tpu_custom_call", output_to_operand_aliasing={{0}: (10, {}), {1}: (11, {}), {2}: (12, {}), {3}: (13, {})} | custom-call | flops 1879048192 | bytes 9437184 | tf_op jit(solution)/shard_map/project/pallas_call | solution.py:352
  194.9 10.4 %project.13 = (bf16[2048,2048]{1,0:T(8,128)(2,1)}, bf16[2048,768]{1,0:T(8,128)(2,1)}, bf16[2048,1024]{1,0:T(8,128)(2,1)}, bf16[2048,1024]{1,0:T(8,128)(2,1)}) custom-call(s32[1]{0:T(128)} %bitcast.8.place, bf16[256,2048]{1,0:T(8,128)(2,1)} %copy-done.16, ...), custom_call_target="tpu_custom_call", output_to_operand_aliasing={{0}: (10, {}), {1}: (11, {}), {2}: (12, {}), {3}: (13, {})} | custom-call | flops 1879048192 | bytes 9437184 | tf_op jit(solution)/shard_map/project/pallas_call | solution.py:352
  205.3 10.2 %project.14 = (bf16[2048,2048]{1,0:T(8,128)(2,1)}, bf16[2048,768]{1,0:T(8,128)(2,1)}, bf16[2048,1024]{1,0:T(8,128)(2,1)}, bf16[2048,1024]{1,0:T(8,128)(2,1)}) custom-call(s32[1]{0:T(128)} %bitcast.7.place, bf16[256,2048]{1,0:T(8,128)(2,1)} %copy-done.13, ...), custom_call_target="tpu_custom_call", output_to_operand_aliasing={{0}: (10, {}), {1}: (11, {}), {2}: (12, {}), {3}: (13, {})} | custom-call | flops 1879048192 | bytes 9437184 | tf_op jit(solution)/shard_map/project/pallas_call | solution.py:352
  216.4 10.1 %project.15 = (bf16[2048,2048]{1,0:T(8,128)(2,1)}, bf16[2048,768]{1,0:T(8,128)(2,1)}, bf16[2048,1024]{1,0:T(8,128)(2,1)}, bf16[2048,1024]{1,0:T(8,128)(2,1)}) custom-call(s32[1]{0:T(128)} %bitcast.2.place, bf16[256,2048]{1,0:T(8,128)(2,1)} %copy-done.15, ...), custom_call_target="tpu_custom_call", output_to_operand_aliasing={{0}: (10, {}), {1}: (11, {}), {2}: (12, {}), {3}: (13, {})} | custom-call | flops 1879048192 | bytes 9437184 | tf_op jit(solution)/shard_map/project/pallas_call | solution.py:352
  227.2 28.4 %attend_forward.1 = (bf16[2048,256]{1,0:T(8,128)(2,1)}, f32[8,2048]{1,0:T(8,128)}) custom-call(s32[8]{0:T(128)} %and_select_fusion.2.lows, s32[8,2048]{1,0:T(8,128)} %broadcast_in_dim.72.starts, bf16[2048,768]{1,0:T(8,128)(2,1)} %get-tuple-element.77.q.k.v, bf16[2048,768]{1,0:T(8,128)(2,1)} %get-tuple-element.77.q.k.v, bf16[2048,768]{1,0:T(8,128)(2,1)} %get-tuple-element.77.q.k.v), custom_call_target="tpu_custom_call" | custom-call | flops 17179869184 | bytes 4194304 | tf_op jit(solution)/shard_map/attend_forward/pallas_call | solution.py:92
  255.6 14.7 %fusion = f32[2048,1024]{1,0:T(8,128)} fusion(bf16[1024,2048]{1,0:T(8,128)(2,1)} %param.22, bf16[2048,1024]{1,0:T(8,128)(2,1)} %bitcast.202, bf16[2048,1024]{1,0:T(8,128)(2,1)} %bitcast.204), kind=kOutput, calls=%fused_computation.5 | convolution fusion | flops 8606711808 | bytes 20971520 | tf_op jit(solution)/shard_map/dot_general | solution.py:466
  270.3 14.1 %fusion.5.grad = bf16[2048,256]{1,0:T(8,128)(2,1)} fusion(bf16[256,2048]{1,0:T(8,128)(2,1)S(1)} %copy-done, bf16[2048,1024]{1,0:T(8,128)(2,1)S(1)} %bitcast.203, bf16[2048,1024]{1,0:T(8,128)(2,1)S(1)} %bitcast.205), kind=kOutput, calls=%fused_computation.22 | convolution fusion | flops 2164785152 | bytes 10485760 | tf_op jit(solution)/shard_map/dot_general | solution.py:466
  291.7 14.0 %fusion.58 = f32[2048,2048]{1,0:T(8,128)} fusion(bf16[2048,1024]{1,0:T(8,128)(2,1)} %multiply_convert_fusion, bf16[2048,1024]{1,0:T(8,128)(2,1)S(1)} %copy-done.1), kind=kOutput, calls=%fused_computation.146 | convolution fusion | flops 8589934592 | bytes 25165824 | tf_op jit(solution)/shard_map/dot_general | solution.py:466
  305.6 43.4 %attend_backward.1 = bf16[2048,768]{1,0:T(8,128)(2,1)} custom-call(s32[8]{0:T(128)} %and_select_fusion.2.lows, s32[8,2048]{1,0:T(8,128)} %broadcast_in_dim.72.starts, f32[8,2048]{1,0:T(8,128)} %get-tuple-element.80.lse, bf16[2048,768]{1,0:T(8,128)(2,1)} %get-tuple-element.77.q.k.v, bf16[2048,768]{1,0:T(8,128)(2,1)} %get-tuple-element.77.q.k.v, ...), custom_call_target="tpu_custom_call" | custom-call | flops 42949672960 | bytes 12582912 | tf_op jit(solution)/shard_map/attend_backward/pallas_call | solution.py:217
  349.0 13.2 %add_convert_fusion = bf16[2048,2048]{1,0:T(8,128)(2,1)} fusion(f32[2048,2048]{1,0:T(8,128)} %fusion.58, bf16[2048,768]{1,0:T(8,128)(2,1)} %attend_backward.1, bf16[2048,768]{0,1:T(8,128)(2,1)S(1)} %bitcast.136), kind=kOutput, calls=%fused_computation | convolution fusion | flops 6450839552 | bytes 31457280 | tf_op jit(solution)/shard_map/dot_general | solution.py:466
  364.9 16.2 %fusion.57 = f32[2048,2048]{1,0:T(8,128)} fusion(bf16[2048,1024]{1,0:T(8,128)(2,1)} %get-tuple-element.79, bf16[1024,2048]{1,0:T(8,128)(2,1)} %param.22), kind=kOutput, calls=%fused_computation.145 | convolution fusion | flops 8589934592 | bytes 25165824 | tf_op jit(solution)/shard_map/dot_general | solution.py:567
  381.2 11.7 %add_convert_fusion.1 = bf16[2048,2048]{1,0:T(8,128)(2,1)} fusion(f32[2048,2048]{1,0:T(8,128)} %fusion.57, bf16[2048,256]{1,0:T(8,128)(2,1)S(1)} %copy-done.20, bf16[256,2048]{1,0:T(8,128)(2,1)S(1)} %copy-done), kind=kOutput, calls=%fused_computation.1 | convolution fusion | flops 2155872256 | bytes 27262976 | tf_op jit(solution)/shard_map/dot_general | solution.py:566
  416.3 10.0 %convolution_convert_fusion = bf16[2048,1024]{1,0:T(8,128)(2,1)S(1)} fusion(bf16[2048,2048]{1,0:T(8,128)(2,1)S(1)} %bitcast.130, bf16[2048,1024]{1,0:T(8,128)(2,1)S(1)} %copy-done.6), kind=kOutput, calls=%fused_computation.7 | convolution fusion | flops 8592031744 | bytes 16777216 | tf_op jit(solution)/shard_map/dot_general | solution.py:460
  446.6 26.5 %collective-permute-done.16 = bf16[2,256,768]{2,1,0:T(8,128)(2,1)S(1)} collective-permute-done((bf16[2,256,768]{2,1,0:T(8,128)(2,1)S(1)}, bf16[2,256,768]{2,1,0:T(8,128)(2,1)S(1)}, u32[]{:S(2)}, u32[]{:S(2)}) %collective-permute-start.16) | collective-permute-done | bytes 786464 | tf_op jit(solution)/shard_map/ppermute | solution.py:418
  538.2 15.6 %collective-permute-done.14 = bf16[1,256,768]{2,1,0:T(8,128)(2,1)S(1)} collective-permute-done((bf16[1,256,768]{2,1,0:T(8,128)(2,1)S(1)}, bf16[1,256,768]{2,1,0:T(8,128)(2,1)S(1)}, u32[]{:S(2)}, u32[]{:S(2)}) %collective-permute-start.14) | collective-permute-done | bytes 393248 | tf_op jit(solution)/shard_map/ppermute | solution.py:418
  556.3 21.9 %psum.7 = f32[1792]{0:T(1024)} all-reduce(f32[1792]{0:T(1024)S(1)} %pad_maximum_fusion.10), channel_id=1, replica_groups=mesh['rows'=4,'tp'=8] {'rows'}, use_global_device_ids=true, to_apply=%region_10.11 | all-reduce | flops 1792 | bytes 14336 | tf_op jit(solution)/shard_map/psum | solution.py:590
  643.0 8.6 %finish.7 = f32[2048,1024]{1,0:T(8,128)} custom-call(s32[8]{0:T(128)} %stack.35.order, bf16[2,256,1024]{2,1,0:T(8,128)(2,1)} %maximum_select_fusion.row_a, bf16[2,256,1024]{2,1,0:T(8,128)(2,1)} %collective-permute-done.39.far_a, bf16[2,256,1024]{2,1,0:T(8,128)(2,1)} %maximum_select_fusion.1.row_b, bf16[2,256,1024]{2,1,0:T(8,128)(2,1)} %collective-permute-done.43.far_b), custom_call_target="tpu_custom_call" | custom-call | bytes 12582912 | tf_op jit(solution)/shard_map/finish/pallas_call | solution.py:394
  (266 shorter events, 234.4 us)
Async XLA Ops:
  7.2 248.4 %all-gather.6.cloned.1.call-start = ((), (), s32[]{:S(2)}) async-start(), calls=%async_computation.4 | async-start | bytes 4718592 | tf_op jit(solution)/shard_map/all_gather | solution.py:525
  9.7 245.9 %all-gather.8.cloned.1.call-start = ((), (), s32[]{:S(2)}) async-start(), calls=%async_computation.5 | async-start | bytes 4718592 | tf_op jit(solution)/shard_map/all_gather | solution.py:525
  10.4 599.4 %reduce-scatter.5.cloned.1.call-start = ((), (), s32[]{:S(2)}) async-start(), calls=%async_computation.3 | async-start | bytes 9437184 | tf_op jit(solution)/shard_map/reduce_scatter | solution.py:576
  10.5 43.0 %collective-permute-start = (bf16[256,2048]{1,0:T(8,128)(2,1)S(1)}, bf16[256,2048]{1,0:T(8,128)(2,1)S(1)}, u32[]{:S(2)}, u32[]{:S(2)}) collective-permute-start(bf16[256,2048]{1,0:T(8,128)(2,1)S(1)} %bitcast.132), channel_id=1, source_target_pairs={{0,2},{1,3},{2,4},{3,5},{4,6},{5,7},{6,0},{7,1},{8,10},{9,11},{10,... | collective-permute-start | bytes 3145736 | tf_op jit(solution)/shard_map/ppermute | solution.py:515
  53.5 64.2 %collective-permute-start.1 = (bf16[256,2048]{1,0:T(8,128)(2,1)S(1)}, bf16[256,2048]{1,0:T(8,128)(2,1)}, u32[]{:S(2)}, u32[]{:S(2)}) collective-permute-start(bf16[256,2048]{1,0:T(8,128)(2,1)S(1)} %collective-permute-done.x), channel_id=1, source_target_pairs={{0,2},{1,3},{2,4},{3,5},{4,6},{5,7},{6,0},{7,1},{8,10},{9,11},{10,... | collective-permute-start | bytes 3145736 | tf_op jit(solution)/shard_map/ppermute | solution.py:515
  69.1 82.7 %collective-permute-start.6 = (bf16[256,2048]{1,0:T(8,128)(2,1)S(1)}, bf16[256,2048]{1,0:T(8,128)(2,1)}, u32[]{:S(2)}, u32[]{:S(2)}) collective-permute-start(bf16[256,2048]{1,0:T(8,128)(2,1)S(1)} %bitcast.133), channel_id=1, source_target_pairs={{0,1},{1,0},{2,3},{3,2},{4,5},{5,4},{6,7},{7,6},{8,9},{9,8},{10,11... | collective-permute-start | bytes 3145736 | tf_op jit(solution)/shard_map/ppermute | solution.py:517
  128.0 44.5 %collective-permute-start.5 = (bf16[256,2048]{1,0:T(8,128)(2,1)}, bf16[256,2048]{1,0:T(8,128)(2,1)S(1)}, u32[]{:S(2)}, u32[]{:S(2)}) collective-permute-start(bf16[256,2048]{1,0:T(8,128)(2,1)} %copy-done.14), channel_id=1, source_target_pairs={{0,1},{1,0},{2,3},{3,2},{4,5},{5,4},{6,7},{7,6},{8,9},{9,8},{10,11... | collective-permute-start | bytes 3145736 | tf_op jit(solution)/shard_map/ppermute | solution.py:517
  133.9 60.0 %collective-permute-start.4 = (bf16[256,2048]{1,0:T(8,128)(2,1)}, bf16[256,2048]{1,0:T(8,128)(2,1)S(1)}, u32[]{:S(2)}, u32[]{:S(2)}) collective-permute-start(bf16[256,2048]{1,0:T(8,128)(2,1)} %collective-permute-done.1.x), channel_id=1, source_target_pairs={{0,1},{1,0},{2,3},{3,2},{4,5},{5,4},{6,7},{7,6},{8,9},{9,8},{10,11... | collective-permute-start | bytes 3145736 | tf_op jit(solution)/shard_map/ppermute | solution.py:517
  151.7 63.7 %collective-permute-start.3 = (bf16[256,2048]{1,0:T(8,128)(2,1)S(1)}, bf16[256,2048]{1,0:T(8,128)(2,1)S(1)}, u32[]{:S(2)}, u32[]{:S(2)}) collective-permute-start(bf16[256,2048]{1,0:T(8,128)(2,1)S(1)} %collective-permute-done.2.x), channel_id=1, source_target_pairs={{0,1},{1,0},{2,3},{3,2},{4,5},{5,4},{6,7},{7,6},{8,9},{9,8},{10,11... | collective-permute-start | bytes 3145736 | tf_op jit(solution)/shard_map/ppermute | solution.py:517
  362.3 299.6 %reduce-scatter.3.cloned.1.call-start = ((), (), s32[]{:S(2)}) async-start(), calls=%async_computation.2 | async-start | bytes 9437184 | tf_op jit(solution)/shard_map/reduce_scatter | solution.py:569
  402.8 34.2 %collective-permute-start.24 = (bf16[2,160,1024]{2,1,0:T(8,128)(2,1)S(1)}, bf16[2,160,1024]{2,1,0:T(8,128)(2,1)}, u32[]{:S(2)}, u32[]{:S(2)}) collective-permute-start(bf16[2,160,1024]{2,1,0:T(8,128)(2,1)S(1)} %dynamic-slice_bitcast_fusion.6), channel_id=1, source_target_pairs={{0,16},{8,24},{16,0},{24,8},{1,17},{9,25},{17,1},{25,9},{2,18},{10... | collective-permute-start | bytes 1966088 | tf_op jit(solution)/shard_map/ppermute | solution.py:418
  426.9 69.3 %collective-permute-start.40 = (bf16[2,256,1024]{2,1,0:T(8,128)(2,1)S(1)}, bf16[2,256,1024]{2,1,0:T(8,128)(2,1)S(1)}, u32[]{:S(2)}, u32[]{:S(2)}) collective-permute-start(bf16[2,256,1024]{2,1,0:T(8,128)(2,1)S(1)} %dynamic-slice_bitcast_fusion), channel_id=1, source_target_pairs={{0,16},{8,24},{16,0},{24,8},{1,17},{9,25},{17,1},{25,9},{2,18},{10... | collective-permute-start | bytes 3145736 | tf_op jit(solution)/shard_map/ppermute | solution.py:418
  437.0 60.8 %collective-permute-start.36 = (bf16[2,256,1024]{2,1,0:T(8,128)(2,1)S(1)}, bf16[2,256,1024]{2,1,0:T(8,128)(2,1)S(1)}, u32[]{:S(2)}, u32[]{:S(2)}) collective-permute-start(bf16[2,256,1024]{2,1,0:T(8,128)(2,1)S(1)} %dynamic-slice_bitcast_fusion.1), channel_id=1, source_target_pairs={{0,8},{8,0},{16,24},{24,16},{1,9},{9,1},{17,25},{25,17},{2,10},{10... | collective-permute-start | bytes 3145736 | tf_op jit(solution)/shard_map/ppermute | solution.py:418
  441.7 38.2 %collective-permute-start.12 = (bf16[2,256,768]{2,1,0:T(8,128)(2,1)S(1)}, bf16[2,256,768]{2,1,0:T(8,128)(2,1)S(1)}, u32[]{:S(2)}, u32[]{:S(2)}) collective-permute-start(bf16[2,256,768]{2,1,0:T(8,128)(2,1)S(1)} %dynamic-slice_bitcast_fusion.3), channel_id=1, source_target_pairs={{0,8},{8,0},{16,24},{24,16},{1,9},{9,1},{17,25},{25,17},{2,10},{10... | collective-permute-start | bytes 2359304 | tf_op jit(solution)/shard_map/ppermute | solution.py:418
  444.3 42.6 %collective-permute-start.25 = (bf16[1,160,1024]{2,1,0:T(8,128)(2,1)S(1)}, bf16[1,160,1024]{2,1,0:T(8,128)(2,1)S(1)}, u32[]{:S(2)}, u32[]{:S(2)}) collective-permute-start(bf16[1,160,1024]{2,1,0:T(8,128)(2,1)S(1)} %constant_dynamic-slice_fusion.3), channel_id=1, source_target_pairs={{0,8},{8,0},{16,24},{24,16},{1,9},{9,1},{17,25},{25,17},{2,10},{10... | collective-permute-start | bytes 983048 | tf_op jit(solution)/shard_map/ppermute | solution.py:418
  518.4 36.4 %collective-permute-start.27 = (bf16[2,160,1024]{2,1,0:T(8,128)(2,1)S(1)}, bf16[2,160,1024]{2,1,0:T(8,128)(2,1)S(1)}, u32[]{:S(2)}, u32[]{:S(2)}) collective-permute-start(bf16[2,160,1024]{2,1,0:T(8,128)(2,1)S(1)} %maximum_select_fusion.5.row_b), channel_id=1, source_target_pairs={{0,16},{8,24},{16,0},{24,8},{1,17},{9,25},{17,1},{25,9},{2,18},{10... | collective-permute-start | bytes 1966088 | tf_op jit(solution)/shard_map/ppermute | solution.py:418
  527.7 57.7 %collective-permute-start.23 = (bf16[2,160,1024]{2,1,0:T(8,128)(2,1)}, bf16[2,160,1024]{2,1,0:T(8,128)(2,1)}, u32[]{:S(2)}, u32[]{:S(2)}) collective-permute-start(bf16[2,160,1024]{2,1,0:T(8,128)(2,1)} %maximum_select_fusion.4.row_a), channel_id=1, source_target_pairs={{0,8},{8,0},{16,24},{24,16},{1,9},{9,1},{17,25},{25,17},{2,10},{10... | collective-permute-start | bytes 1966088 | tf_op jit(solution)/shard_map/ppermute | solution.py:418
  531.3 62.8 %collective-permute-start.35 = (bf16[2,160,1024]{2,1,0:T(8,128)(2,1)}, bf16[2,160,1024]{2,1,0:T(8,128)(2,1)}, u32[]{:S(2)}, u32[]{:S(2)}) collective-permute-start(bf16[2,160,1024]{2,1,0:T(8,128)(2,1)} %maximum_select_fusion.7.row_b), channel_id=1, source_target_pairs={{0,16},{8,24},{16,0},{24,8},{1,17},{9,25},{17,1},{25,9},{2,18},{10... | collective-permute-start | bytes 1966088 | tf_op jit(solution)/shard_map/ppermute | solution.py:418
  536.1 58.4 %collective-permute-start.31 = (bf16[2,160,1024]{2,1,0:T(8,128)(2,1)}, bf16[2,160,1024]{2,1,0:T(8,128)(2,1)}, u32[]{:S(2)}, u32[]{:S(2)}) collective-permute-start(bf16[2,160,1024]{2,1,0:T(8,128)(2,1)} %maximum_select_fusion.6.row_a), channel_id=1, source_target_pairs={{0,8},{8,0},{16,24},{24,16},{1,9},{9,1},{17,25},{25,17},{2,10},{10... | collective-permute-start | bytes 1966088 | tf_op jit(solution)/shard_map/ppermute | solution.py:418
  553.8 48.2 %collective-permute-start.42 = (bf16[1,256,1024]{2,1,0:T(8,128)(2,1)}, bf16[1,256,1024]{2,1,0:T(8,128)(2,1)}, u32[]{:S(2)}, u32[]{:S(2)}) collective-permute-start(bf16[1,256,1024]{2,1,0:T(8,128)(2,1)} %add_convert_fusion.2), channel_id=1, source_target_pairs={{0,8},{8,0},{16,24},{24,16},{1,9},{9,1},{17,25},{25,17},{2,10},{10... | collective-permute-start | bytes 1572872 | tf_op jit(solution)/shard_map/ppermute | solution.py:418
  554.8 50.8 %collective-permute-start.38 = (bf16[1,256,1024]{2,1,0:T(8,128)(2,1)}, bf16[1,256,1024]{2,1,0:T(8,128)(2,1)}, u32[]{:S(2)}, u32[]{:S(2)}) collective-permute-start(bf16[1,256,1024]{2,1,0:T(8,128)(2,1)} %add_convert_fusion.3), channel_id=1, source_target_pairs={{0,16},{8,24},{16,0},{24,8},{1,17},{9,25},{17,1},{25,9},{2,18},{10... | collective-permute-start | bytes 1572872 | tf_op jit(solution)/shard_map/ppermute | solution.py:418
  585.4 36.6 %collective-permute-start.19 = (bf16[2,256,768]{2,1,0:T(8,128)(2,1)}, bf16[2,256,768]{2,1,0:T(8,128)(2,1)}, u32[]{:S(2)}, u32[]{:S(2)}) collective-permute-start(bf16[2,256,768]{2,1,0:T(8,128)(2,1)} %maximum_select_fusion.3.row_b), channel_id=1, source_target_pairs={{0,16},{8,24},{16,0},{24,8},{1,17},{9,25},{17,1},{25,9},{2,18},{10... | collective-permute-start | bytes 2359304 | tf_op jit(solution)/shard_map/ppermute | solution.py:418
  604.7 38.3 %collective-permute-start.43 = (bf16[2,256,1024]{2,1,0:T(8,128)(2,1)}, bf16[2,256,1024]{2,1,0:T(8,128)(2,1)}, u32[]{:S(2)}, u32[]{:S(2)}) collective-permute-start(bf16[2,256,1024]{2,1,0:T(8,128)(2,1)} %maximum_select_fusion.1.row_b), channel_id=1, source_target_pairs={{0,16},{8,24},{16,0},{24,8},{1,17},{9,25},{17,1},{25,9},{2,18},{10... | collective-permute-start | bytes 3145736 | tf_op jit(solution)/shard_map/ppermute | solution.py:418
  608.3 34.6 %collective-permute-start.39 = (bf16[2,256,1024]{2,1,0:T(8,128)(2,1)}, bf16[2,256,1024]{2,1,0:T(8,128)(2,1)}, u32[]{:S(2)}, u32[]{:S(2)}) collective-permute-start(bf16[2,256,1024]{2,1,0:T(8,128)(2,1)} %maximum_select_fusion.row_a), channel_id=1, source_target_pairs={{0,8},{8,0},{16,24},{24,16},{1,9},{9,1},{17,25},{25,17},{2,10},{10... | collective-permute-start | bytes 3145736 | tf_op jit(solution)/shard_map/ppermute | solution.py:418
  (62 other events, 1241.8 us)
Sparse Core Ops, SparseCore 0:
  9.8 66.7 all-gather.5
  78.2 76.1 all-gather.7
  362.4 87.4 reduce-scatter.4
  452.1 87.9 reduce-scatter.2

commit v2 on v1

v2 whole, which is shorter than its diff:
```python
from functools import partial
import math

import jax
import jax.numpy as jnp
from jax import lax
from jax.experimental import pallas as pl
from jax.experimental.pallas import tpu as pltpu
from jax.sharding import PartitionSpec as P

HEAD_DIM = 64
ROT = 32
EPSILON = 1e-05
NEGATIVE = -1e30
VMEM_BYTES = 56 * 2**20
NT = (((1,), (1,)), ((), ()))


class Line:
    def __init__(self):
        self.token = jnp.zeros((8, 128), jnp.float32)

    def join(self, *arrays):
        *arrays, self.token = lax.optimization_barrier((*arrays, self.token))
        return arrays

    def call(
        self, body, name, grid, operands, in_specs, outs, scalars=0, scratch=(), aliases=None, cost=0
    ):
        inputs = len(operands)

        def whole_body(*refs):
            refs = list(refs)
            token = refs.pop(inputs + 1 + len(outs))
            refs.pop(inputs)
            token[...] = jnp.zeros_like(token)
            body(*refs)

        *results, self.token = pl.pallas_call(
            whole_body,
            grid_spec=pltpu.PrefetchScalarGridSpec(
                num_scalar_prefetch=scalars,
                grid=grid,
                in_specs=[*in_specs, pl.BlockSpec(memory_space=pl.ANY)],
                out_specs=[
                    *(spec for _, _, spec in outs),
                    pl.BlockSpec((8, 128), lambda *index: (0, 0)),
                ],
                scratch_shapes=list(scratch),
            ),
            out_shape=[
                *(jax.ShapeDtypeStruct(shape, dtype) for shape, dtype, _ in outs),
                jax.ShapeDtypeStruct((8, 128), jnp.float32),
            ],
            input_output_aliases=aliases or {},
            compiler_params=pltpu.CompilerParams(vmem_limit_bytes=VMEM_BYTES),
            cost_estimate=pl.CostEstimate(
                flops=2**20 + cost, bytes_accessed=2**16, transcendentals=0
            ),
            name=name,
        )(*operands, self.token)
        return results


def whole(*index):
    return (0, 0)


def row(i, *scalars):
    return (i, 0)


def lane_heads(rows, width):
    return lax.broadcasted_iota(jnp.int32, (rows, width), 1) // HEAD_DIM


def swap_pairs(x):
    width = x.shape[1]
    lane = lax.broadcasted_iota(jnp.int32, x.shape, 1) % HEAD_DIM
    up = pltpu.roll(x, width - ROT // 2, 1)
    down = pltpu.roll(x, ROT // 2, 1)
    return jnp.where(lane < ROT // 2, up, down)


def mask_bias(starts, key_first, query_first, block):
    key_index = key_first + lax.broadcasted_iota(jnp.int32, (block, block), 0)
    query_index = query_first + lax.broadcasted_iota(jnp.int32, (block, block), 1)
    allowed = (key_index >= starts) & (key_index <= query_index)
    return jnp.where(allowed, 0.0, NEGATIVE).astype(jnp.float32)


def stack_heads(source, stacked, block):
    length, width = source.shape
    row_heads = lane_heads(block, width)
    for j in range(length // block):
        rows = pl.ds(j * block, block)
        piece = source[rows, :]
        for h in range(width // HEAD_DIM):
            stacked[j, pl.ds(h * block, block), :] = jnp.where(row_heads == h, piece, 0).astype(
                jnp.bfloat16
            )


def forward_kernel(lows, starts, q, k, v, context, lse, v_t, k_heads, acc):
    block, width = q.shape
    heads = width // HEAD_DIM
    length = k.shape[0]
    i = pl.program_id(0)

    @pl.when(i == 0)
    def _():
        stack_heads(k, k_heads, block)
        for j in range(length // block):
            rows = pl.ds(j * block, block)
            v_t[:, rows] = v[rows, :].T

    turned = (q[...] * 0.125).T
    acc[...] = jnp.zeros_like(acc)

    def step(j, carry):
        tops, sums = carry
        first = pl.multiple_of(j * block, block)
        all_scores = jnp.dot(k_heads[j], turned, preferred_element_type=jnp.float32)
        bias = mask_bias(starts[0:1, :], first, i * block, block)
        new_tops, new_sums = [], []
        for h in range(heads):
            rows = pl.ds(h * HEAD_DIM, HEAD_DIM)
            scores = all_scores[h * block : (h + 1) * block, :] + bias
            top = jnp.maximum(tops[h], jnp.max(scores, axis=0, keepdims=True))
            weights = jnp.exp(scores - top)
            keep = jnp.exp(tops[h] - top)
            new_tops.append(top)
            new_sums.append(sums[h] * keep + jnp.sum(weights, axis=0, keepdims=True))
            acc[rows, :] = acc[rows, :] * keep + jnp.dot(
                v_t[rows, pl.ds(first, block)],
                weights.astype(jnp.bfloat16),
                preferred_element_type=jnp.float32,
            )
        return tuple(new_tops), tuple(new_sums)

    empty = tuple(jnp.full((1, block), NEGATIVE, jnp.float32) for _ in range(heads))
    nothing = tuple(jnp.zeros((1, block), jnp.float32) for _ in range(heads))
    tops, sums = lax.fori_loop(lows[i], i + 1, step, (empty, nothing))
    for h in range(heads):
        rows = pl.ds(h * HEAD_DIM, HEAD_DIM)
        acc[rows, :] = acc[rows, :] / sums[h]
        lse[h : h + 1, :] = tops[h] + jnp.log(sums[h])
    context[...] = acc[...].T.astype(jnp.bfloat16)


def attend_forward(line, lows, starts, mixed, block):
    length, triple = mixed.shape
    local_width = triple // 3
    blocks = length // block
    stack = (blocks, local_width // HEAD_DIM * block, local_width)
    column = lambda i, lows: (0, i)
    return line.call(
        forward_kernel,
        "attend_forward",
        (blocks,),
        [lows, starts, mixed, mixed, mixed],
        [
            pl.BlockSpec((8, block), column),
            pl.BlockSpec((block, local_width), row),
            pl.BlockSpec((length, local_width), lambda i, lows: (0, 1)),
            pl.BlockSpec((length, local_width), lambda i, lows: (0, 2)),
        ],
        [
            ((length, local_width), jnp.bfloat16, pl.BlockSpec((block, local_width), row)),
            ((8, length), jnp.float32, pl.BlockSpec((8, block), column)),
        ],
        scalars=1,
        scratch=[
            pltpu.VMEM((local_width, length), jnp.bfloat16),
            pltpu.VMEM(stack, jnp.bfloat16),
            pltpu.VMEM((local_width, block), jnp.float32),
        ],
    )


def backward_kernel(
    lows, starts, lse, q, k, v, context, grad, cosine, sine, grad_mixed, k_t, k_heads, v_heads, grad_q, grad_k, grad_v
):
    block, width = q.shape
    heads = width // HEAD_DIM
    length = k.shape[0]
    i = pl.program_id(0)
    blocks = length // block

    @pl.when(i == 0)
    def _():
        grad_k[...] = jnp.zeros_like(grad_k)
        grad_v[...] = jnp.zeros_like(grad_v)
        stack_heads(k, k_heads, block)
        stack_heads(v, v_heads, block)
        for j in range(blocks):
            rows = pl.ds(j * block, block)
            k_t[:, rows] = k[rows, :].T

    row_heads = lane_heads(block, width)
    scaled = q[...] * 0.125
    grads = grad[...]
    masked_q = [jnp.where(row_heads == h, scaled, 0).astype(jnp.bfloat16) for h in range(heads)]
    masked_g = [jnp.where(row_heads == h, grads, 0).astype(jnp.bfloat16) for h in range(heads)]
    turned_q = scaled.T
    turned_g = grads.T
    products = (grads.astype(jnp.float32) * context[...].astype(jnp.float32)).T
    inner = [
        jnp.sum(products[h * HEAD_DIM : (h + 1) * HEAD_DIM, :], axis=0, keepdims=True)
        for h in range(heads)
    ]
    grad_q[...] = jnp.zeros_like(grad_q)

    def step(j, carry):
        first = pl.multiple_of(j * block, block)
        here = pl.ds(first, block)
        all_scores = jnp.dot(k_heads[j], turned_q, preferred_element_type=jnp.float32)
        all_grads = jnp.dot(v_heads[j], turned_g, preferred_element_type=jnp.float32)
        bias = mask_bias(starts[0:1, :], first, i * block, block)
        probs, slopes = [], []
        for h in range(heads):
            rows = pl.ds(h * HEAD_DIM, HEAD_DIM)
            part = slice(h * block, (h + 1) * block)
            scores = all_scores[part, :]
            soft = jnp.exp(scores + bias - lse[h : h + 1, :])
            grad_probs = all_grads[part, :]
            slope = (soft * (grad_probs - inner[h])).astype(jnp.bfloat16)
            grad_q[rows, :] += jnp.dot(k_t[rows, here], slope, preferred_element_type=jnp.float32)
            probs.append(soft.astype(jnp.bfloat16))
            slopes.append(slope)
        grad_v[here, :] += jnp.dot(
            jnp.concatenate(probs, axis=1),
            jnp.concatenate(masked_g, axis=0),
            preferred_element_type=jnp.float32,
        )
        grad_k[here, :] += jnp.dot(
            jnp.concatenate(slopes, axis=1),
            jnp.concatenate(masked_q, axis=0),
            preferred_element_type=jnp.float32,
        )
        return carry

    lax.fori_loop(lows[i], i + 1, step, 0)

    def unrotate(x, rows):
        parts = []
        for part in range(width // 128):
            piece = x[:, part * 128 : (part + 1) * 128]
            parts.append(piece * cosine[rows, :] - swap_pairs(piece) * sine[rows, :])
        return jnp.concatenate(parts, axis=1).astype(jnp.bfloat16)

    mine = pl.ds(pl.multiple_of(i * block, block), block)
    grad_mixed[mine, 0:width] = unrotate(grad_q[...].T * 0.125, mine)

    @pl.when(i == blocks - 1)
    def _():
        def finish(j, carry):
            rows = pl.ds(pl.multiple_of(j * block, block), block)
            grad_mixed[rows, width : 2 * width] = unrotate(grad_k[rows, :], rows)
            grad_mixed[rows, 2 * width : 3 * width] = grad_v[rows, :].astype(jnp.bfloat16)
            return carry

        lax.fori_loop(0, blocks, finish, 0)


def attend_backward(line, lows, starts, lse, mixed, context, grad_context, cosine, sine, block):
    length, triple = mixed.shape
    local_width = triple // 3
    blocks = length // block
    stack = (blocks, local_width // HEAD_DIM * block, local_width)
    column = lambda i, lows: (0, i)
    return line.call(
        backward_kernel,
        "attend_backward",
        (blocks,),
        [lows, starts, lse, mixed, mixed, mixed, context, grad_context, cosine, sine],
        [
            pl.BlockSpec((8, block), column),
            pl.BlockSpec((8, block), column),
            pl.BlockSpec((block, local_width), row),
            pl.BlockSpec((length, local_width), lambda i, lows: (0, 1)),
            pl.BlockSpec((length, local_width), lambda i, lows: (0, 2)),
            pl.BlockSpec((block, local_width), row),
            pl.BlockSpec((block, local_width), row),
            pl.BlockSpec((length, 128), whole),
            pl.BlockSpec((length, 128), whole),
        ],
        [((length, triple), jnp.bfloat16, pl.BlockSpec((length, triple), whole))],
        scalars=1,
        scratch=[
            pltpu.VMEM((local_width, length), jnp.bfloat16),
            pltpu.VMEM(stack, jnp.bfloat16),
            pltpu.VMEM(stack, jnp.bfloat16),
            pltpu.VMEM((local_width, block), jnp.float32),
            pltpu.VMEM((length, local_width), jnp.float32),
            pltpu.VMEM((length, local_width), jnp.float32),
        ],
        cost=632 * 10**8,
    )[0]


def positions_of(segments):
    ids = jnp.arange(8, dtype=jnp.int32)
    counts = jnp.sum((segments[None, :] < ids[:, None]).astype(jnp.int32), axis=1)
    return jnp.sum(jnp.where(segments[None, :] == ids[:, None], counts[:, None], 0), axis=0)


def rotary_tables(positions):
    lane = jnp.arange(128, dtype=jnp.int32) % HEAD_DIM
    step = (lane % (ROT // 2)).astype(jnp.float32)
    inverse = jnp.exp(step * (-2.0 * math.log(10000.0) / ROT))
    angles = positions.astype(jnp.float32)[:, None] * inverse[None, :]
    rotated = (lane < ROT)[None, :]
    cosine = jnp.where(rotated, jnp.cos(angles), 1.0)
    sine = jnp.where(rotated, jnp.where((lane < ROT // 2)[None, :], -1.0, 1.0) * jnp.sin(angles), 0.0)
    return cosine, sine


def gelu_pair(u):
    scale = math.sqrt(2.0 / math.pi)
    square = u * u
    bent = jnp.tanh(scale * u * (1.0 + 0.044715 * square))
    half = 0.5 * (1.0 + bent)
    slope = half + 0.5 * u * (1.0 - bent * bent) * (scale * (1.0 + 3 * 0.044715 * square))
    return u * half, slope


def project_kernel(place, mine, other, gain, shift, w_qkv, b_qkv, w_up, b_up, cosine, sine, *refs):
    normed, unit, mixed, activated, slope = refs[-5:]
    n = pl.program_id(0)
    block = mine.shape[0]
    width = w_qkv.shape[2]
    strip = min(128, block)
    strips = [pl.ds(r * strip, strip) for r in range(2 * block // strip)]

    @pl.when(n == 0)
    def _():
        for source, first in ((mine, place[1] * block), (other, (1 - place[1]) * block)):
            for r in range(block // strip):
                wide = source[pl.ds(r * strip, strip), :].astype(jnp.float32)
                centred = wide - jnp.mean(wide, axis=1, keepdims=True)
                inverse_std = lax.rsqrt(
                    jnp.mean(centred * centred, axis=1, keepdims=True) + EPSILON
                )
                rows = pl.ds(pl.multiple_of(first + r * strip, strip), strip)
                even = centred * inverse_std
                unit[rows, :] = even.astype(jnp.bfloat16)
                normed[rows, :] = (even * gain[...] + shift[...]).astype(jnp.bfloat16)
        for rows in strips:
            for j in range(3):
                columns = slice(j * width, (j + 1) * width)
                y = jnp.dot(normed[rows, :], w_qkv[j], preferred_element_type=jnp.float32)
                y = y + b_qkv[:, columns]
                if j < 2:
                    parts = []
                    for part in range(width // 128):
                        piece = y[:, part * 128 : (part + 1) * 128]
                        parts.append(piece * cosine[rows, :] + swap_pairs(piece) * sine[rows, :])
                    y = jnp.concatenate(parts, axis=1)
                mixed[rows, columns] = y.astype(jnp.bfloat16)

    @pl.when(n > 0)
    def _():
        for rows in strips:
            u = jnp.dot(normed[rows, :], w_up[...], preferred_element_type=jnp.float32) + b_up[...]
            high, tilt = gelu_pair(u)
            activated[rows, :] = high.astype(jnp.bfloat16)
            slope[rows, :] = tilt.astype(jnp.bfloat16)


def project(line, place, mine, other, weights, tables, length, carried):
    gain, shift, w_qkv, b_qkv, w_up, b_up = weights
    block, width = mine.shape
    local_width = w_qkv.shape[2]
    hidden = w_up.shape[1]
    tile = min(512, hidden)
    up = lambda n, place: (0, jnp.maximum(n - 1, 0))
    here = lambda n, place: (place[0], 0)
    up_here = lambda n, place: (place[0], jnp.maximum(n - 1, 0))
    operands = [place, mine, other, gain, shift, w_qkv, b_qkv, w_up, b_up, *tables, *carried]
    return line.call(
        project_kernel,
        "project",
        (1 + hidden // tile,),
        operands,
        [
            pl.BlockSpec((block, width), whole),
            pl.BlockSpec((block, width), whole),
            pl.BlockSpec((1, width), whole),
            pl.BlockSpec((1, width), whole),
            pl.BlockSpec((3, width, local_width), lambda n, place: (0, 0, 0)),
            pl.BlockSpec((1, 3 * local_width), whole),
            pl.BlockSpec((width, tile), up),
            pl.BlockSpec((1, tile), up),
            pl.BlockSpec((2 * block, 128), here),
            pl.BlockSpec((2 * block, 128), here),
            *[pl.BlockSpec(memory_space=pl.ANY)] * len(carried),
        ],
        [
            ((length, columns), jnp.bfloat16, pl.BlockSpec((2 * block, wide), index))
            for columns, wide, index in (
                (width, width, here),
                (width, width, here),
                (3 * local_width, 3 * local_width, here),
                (hidden, tile, up_here),
                (hidden, tile, up_here),
            )
        ],
        scalars=1,
        aliases={len(operands) - 5 + i: i for i in range(len(carried))},
    )


def backward_products_kernel(layout, *refs):
    grads = refs[:layout]
    w_down, w_out, slope, grad_up, grad_context, total = refs[layout:]
    columns = grads[0].shape[1]
    up, context = 0.0, 0.0
    for c in range(layout):
        part = slice(c * columns, (c + 1) * columns)
        piece = grads[c][...]
        up = up + lax.dot_general(piece, w_down[:, part], NT, preferred_element_type=jnp.float32)
        context = context + lax.dot_general(
            piece, w_out[:, part], NT, preferred_element_type=jnp.float32
        )
    low = (up * slope[...].astype(jnp.float32)).astype(jnp.bfloat16)
    grad_up[...] = low
    grad_context[...] = context.astype(jnp.bfloat16)

    @pl.when(pl.program_id(0) == 0)
    def _():
        total[...] = jnp.zeros_like(total)

    total[...] += jnp.sum(low.astype(jnp.float32), axis=0, keepdims=True)


def backward_products(line, grads, w_down, w_out, slope):
    length, columns = grads[0].shape
    hidden, width = w_down.shape
    local_width = w_out.shape[0]
    tile = min(256, length)
    return line.call(
        partial(backward_products_kernel, len(grads)),
        "backward_products",
        (length // tile,),
        [*grads, w_down, w_out, slope],
        [pl.BlockSpec((tile, columns), row) for _ in grads]
        + [
            pl.BlockSpec((hidden, width), whole),
            pl.BlockSpec((local_width, width), whole),
            pl.BlockSpec((tile, hidden), row),
        ],
        [
            ((length, hidden), jnp.bfloat16, pl.BlockSpec((tile, hidden), row)),
            ((length, local_width), jnp.bfloat16, pl.BlockSpec((tile, local_width), row)),
            ((1, hidden), jnp.float32, pl.BlockSpec((1, hidden), whole)),
        ],
    )


def branch_kernel(context, activated, w_out, w_down, out):
    total = jnp.dot(context[...], w_out[...], preferred_element_type=jnp.float32)
    total = total + jnp.dot(activated[...], w_down[...], preferred_element_type=jnp.float32)
    out[...] = total.astype(jnp.bfloat16)


def branch_sum(line, context, activated, w_out, w_down):
    length, local_width = context.shape
    hidden, width = w_down.shape
    tile = min(256, length)
    return line.call(
        branch_kernel,
        "branch_sum",
        (length // tile,),
        [context, activated, w_out, w_down],
        [
            pl.BlockSpec((tile, local_width), row),
            pl.BlockSpec((tile, hidden), row),
            pl.BlockSpec((local_width, width), whole),
            pl.BlockSpec((hidden, width), whole),
        ],
        [((length, width), jnp.bfloat16, pl.BlockSpec((tile, width), row))],
    )[0]


def normed_kernel(mixed, up, unit, w_qkv, w_up, out, gain, shift):
    width = w_qkv.shape[2]
    total = lax.dot_general(up[...], w_up[...], NT, preferred_element_type=jnp.float32)
    for j in range(3):
        total = total + lax.dot_general(
            mixed[:, j * width : (j + 1) * width],
            w_qkv[j],
            NT,
            preferred_element_type=jnp.float32,
        )
    out[...] = total.astype(jnp.bfloat16)

    @pl.when(pl.program_id(0) == 0)
    def _():
        gain[...] = jnp.zeros_like(gain)
        shift[...] = jnp.zeros_like(shift)

    gain[...] += jnp.sum(total * unit[...].astype(jnp.float32), axis=0, keepdims=True)
    shift[...] += jnp.sum(total, axis=0, keepdims=True)


def normed_sum(line, grad_mixed, grad_up, unit, w_qkv, w_up):
    length, triple = grad_mixed.shape
    width, hidden = w_up.shape
    tile = min(256, length)
    return line.call(
        normed_kernel,
        "normed_sum",
        (length // tile,),
        [grad_mixed, grad_up, unit, w_qkv, w_up],
        [
            pl.BlockSpec((tile, triple), row),
            pl.BlockSpec((tile, hidden), row),
            pl.BlockSpec((tile, width), row),
            pl.BlockSpec(w_qkv.shape, lambda i: (0, 0, 0)),
            pl.BlockSpec((width, hidden), whole),
        ],
        [
            ((length, width), jnp.bfloat16, pl.BlockSpec((tile, width), row)),
            ((1, width), jnp.float32, pl.BlockSpec((1, width), whole)),
            ((1, width), jnp.float32, pl.BlockSpec((1, width), whole)),
        ],
    )


def finish_kernel(layout, order, *refs):
    s = pl.program_id(0)
    outs = refs[-1:] if isinstance(layout, int) else refs[-len(layout) :]
    for index, source in enumerate(refs[:4]):

        @pl.when(s == index)
        def _(source=source):
            if isinstance(layout, int):
                group = outs[0].shape[2]
                for j in range(layout):
                    columns = slice(j * group, (j + 1) * group)
                    outs[0][j] = source[:, columns].astype(jnp.float32)
            else:
                start = 0
                columns = source.shape[1]
                for out in outs:
                    rows, spread = out.shape
                    for j in range(spread // columns):
                        out[:, j * columns : (j + 1) * columns] = source[
                            start : start + rows, :
                        ].astype(jnp.float32)
                        start += rows


def finish(line, order, pieces, layout, carried=()):
    rows, columns = pieces[0].shape
    in_specs = [pl.BlockSpec(pieces[0].shape, whole) for _ in range(4)]
    in_specs += [pl.BlockSpec(memory_space=pl.ANY)] * len(carried)
    if isinstance(layout, int):
        group = columns // layout
        spec = pl.BlockSpec((layout, rows, group), lambda s, order: (0, order[s], 0))
        outs = [((layout, 4 * rows, group), jnp.float32, spec)]
    else:
        outs = [
            (
                (4 * tall, spread),
                jnp.float32,
                pl.BlockSpec((tall, wide), lambda s, order, place=place: (order[s], place)),
            )
            for tall, wide, spread, place in layout
        ]
    return line.call(
        partial(finish_kernel, layout),
        "finish",
        (4,),
        [order, *pieces, *carried],
        in_specs,
        outs,
        scalars=1,
        aliases={5 + i: i for i in range(len(carried))},
        cost=460 * 10**8,
    )


def add_low(one, other):
    return (one.astype(jnp.float32) + other.astype(jnp.float32)).astype(jnp.bfloat16)


def swap_rows(array, bit):
    return lax.ppermute(array, "rows", [(i, i ^ bit) for i in range(4)])


def outer_kernel(extra, order, left, right, *refs):
    s = pl.program_id(0)
    dims = (((0,), (0,)), ((), ()))
    low = lax.dot_general(left[...], right[...], dims, preferred_element_type=jnp.float32)
    parts = [low.astype(jnp.bfloat16)]
    outs = refs[:4]
    if extra:
        second, *more = refs[: 1 + extra]
        outs, held = refs[1 + extra : 5 + extra], refs[-1]

        @pl.when(s == 0)
        def _():
            for k, other in enumerate((*more, right)):
                held[k] = lax.dot_general(
                    second[...], other[...], dims, preferred_element_type=jnp.float32
                ).astype(jnp.bfloat16)

        rows = held.shape[1] // 4
        here = pl.ds(pl.multiple_of(order[s] * rows, rows), rows)
        parts += [held[k, here, :] for k in range(extra + 1)]
    for index, out in enumerate(outs):

        @pl.when(s == index)
        def _(out=out):
            start = 0
            for part in parts:
                out[start : start + part.shape[0], :] = part
                start += part.shape[0]


def outer_parts(line, order, left, right, second=None, more=()):
    length, tall = left.shape
    columns = right.shape[1]
    extra = len(more)
    rows = (tall + (second.shape[1] * (extra + 1) if extra else 0)) // 4
    return line.call(
        partial(outer_kernel, extra),
        "outer_parts",
        (4,),
        [order, left, right] + ([second, *more] if extra else []),
        [
            pl.BlockSpec((length, tall // 4), lambda s, order: (0, order[s])),
            pl.BlockSpec((length, columns), whole),
        ]
        + ([pl.BlockSpec(array.shape, whole) for array in (second, *more)] if extra else []),
        [((rows, columns), jnp.bfloat16, pl.BlockSpec((rows, columns), whole)) for _ in range(4)],
        scalars=1,
        scratch=[pltpu.VMEM((extra + 1, second.shape[1], columns), jnp.bfloat16)] if extra else (),
    )


class RowsSum:
    def __init__(self, rows, line, left, right, second=None, more=()):
        self.rows, self.line, self.phase = rows, line, 0
        if rows != 4:
            self.order = jnp.arange(4, dtype=jnp.int32)
            self.pieces = lax.psum(outer_parts(line, self.order, left, right, second, more), "rows")
            return
        place = lax.axis_index("rows")
        x, y = place % 2, place // 2
        away = jnp.stack([1 - x, 3 - y, x, 2 + y]).astype(jnp.int32)
        self.order = jnp.stack([x, 1 - x, 2 + y, 3 - y]).astype(jnp.int32)
        self.bits = ((1, 2), (2, 1))
        *away, keep_a, keep_b = outer_parts(line, away, left, right, second, more)
        self.keep = [keep_a, keep_b]
        self.send(0, away)

    def send(self, which, arrays):
        arrays = self.line.join(*arrays)
        self.came = [swap_rows(a, bits[which]) for a, bits in zip(arrays, self.bits)]
        return arrays

    def advance(self):
        if self.rows != 4:
            return
        self.phase += 1
        came = self.line.join(*self.came)
        if self.phase < 3:
            self.keep = [add_low(k, c) for k, c in zip(self.keep, came)]
            self.keep = self.send(2 - self.phase, self.keep)
        else:
            self.pieces = [self.keep[0], came[0], self.keep[1], came[1]]

    def finish(self, *layout, **more):
        self.advance()
        return finish(self.line, self.order, self.pieces, *layout, **more)


def sum_all(array, rows, tp):
    for axis, size in (("tp", tp), ("rows", rows)):
        step = 1
        while step < size:
            array = array + lax.ppermute(array, axis, [(i, i ^ step) for i in range(size)])
            step *= 2
    return array


def gather_small(array, me, tp):
    step = 1
    while step < tp:
        other = lax.ppermute(array, "tp", [(i, i ^ step) for i in range(tp)])
        array = jnp.where(
            (me // step) % 2 == 0,
            jnp.concatenate([array, other]),
            jnp.concatenate([other, array]),
        )
        step *= 2
    return array


def token_sum(matrix):
    ones_row = jnp.ones((1, matrix.shape[0]), matrix.dtype)
    return jnp.dot(ones_row, matrix, preferred_element_type=jnp.float32)[0]


def local(
    rows,
    tp,
    hidden_in,
    segment_ids,
    ln_gain,
    ln_bias,
    w_qkv,
    b_qkv,
    w_out,
    out_bias,
    w_up,
    b_up,
    w_down,
    cotangent,
):
    x = hidden_in[0]
    block, width = x.shape
    length = block * tp
    local_width = w_qkv.shape[2]
    hidden = w_up.shape[1]
    chips = tp // 2
    me = lax.axis_index("tp")
    chip, core = me // 2, me % 2
    line = Line()

    around = [(i, (i + 2) % tp) for i in range(tp)]
    sibling = [(i, i ^ 1) for i in range(tp)]
    segments = gather_small(segment_ids[0], me, tp)
    mine, segments = lax.optimization_barrier((x, segments))
    coming = lax.ppermute(mine, "tp", around)
    other = lax.ppermute(mine, "tp", sibling)
    starts = positions_of(segments)
    tables = rotary_tables(jnp.arange(length, dtype=jnp.int32) - starts)
    lows = starts[::block] // block
    starts = jnp.broadcast_to(starts[None], (8, length))
    w_three = jnp.transpose(w_qkv, (1, 0, 2))
    weights = (
        ln_gain.reshape(1, width),
        ln_bias.reshape(1, width),
        w_three,
        b_qkv.reshape(1, 3 * local_width),
        w_up,
        b_up.reshape(1, hidden),
    )
    carried = ()
    for s in range(chips):
        place = jnp.stack([(chip - s + chips) % chips, core]).astype(jnp.int32)
        mine, other = line.join(mine, other)
        carried = project(line, place, mine, other, weights, tables, length, carried)
        if s < chips - 1:
            (mine,) = line.join(coming)
            if s < chips - 2:
                coming = lax.ppermute(mine, "tp", around)
            other = lax.ppermute(mine, "tp", sibling)
            if s == max(chips - 3, 0):
                chunks = 2
                columns = width // chunks
                pieces = [cotangent[0, :, c * columns : (c + 1) * columns] for c in range(chunks)]
                *pieces, mine = lax.optimization_barrier((*pieces, mine))
                grads = [lax.all_gather(piece, "tp", axis=0, tiled=True) for piece in pieces]
    normed, unit, mixed, activated, slope = carried

    hidden_parts, local_parts = hidden // 4, local_width // 4
    sums = partial(RowsSum, rows, line)
    d0 = sums(activated, grads[0])
    context, lse = attend_forward(line, lows, starts, mixed, block)
    d0.advance()
    branch = branch_sum(line, context, activated, w_out, w_down)
    branch_total = lax.psum_scatter(branch, "tp", scatter_dimension=0, tiled=True)
    d1 = sums(activated, grads[1], context, [grads[0]])
    d0.advance()
    grad_up, grad_context, grad_b_up = backward_products(line, grads, w_down, w_out, slope)
    d1.advance()
    up = sums(normed, grad_up)
    d1.advance()
    grad_mixed = attend_backward(
        line, lows, starts, lse, mixed, context, grad_context, *tables, block
    )
    up.advance()
    down = d0.finish([(hidden_parts, columns, width, 0)])
    (branch_total,) = line.join(branch_total)
    part, gain_part, shift_part = normed_sum(line, grad_mixed, grad_up, unit, w_three, w_up)
    grad_normed = lax.psum_scatter(part, "tp", scatter_dimension=0, tiled=True).astype(jnp.float32)
    three = sums(normed, grad_mixed)
    up.advance()
    down = d1.finish(
        [(hidden_parts, columns, width, 1), (local_parts, width, width, 0)], carried=down
    )
    three.advance()
    up = up.finish([(width // 4, hidden, hidden, 0)])
    three.advance()
    three = three.finish(3)
    grad_w_down, grad_w_out = down
    grad_w_up = up[0]
    grad_w_qkv = jnp.transpose(three[0], (1, 0, 2))

    inputs = x.astype(jnp.float32)
    hidden_out = (inputs + branch_total.astype(jnp.float32) + out_bias).astype(jnp.bfloat16)
    average = jnp.mean(inputs, axis=-1, keepdims=True)
    centred = inputs - average
    inverse_std = lax.rsqrt(jnp.mean(centred * centred, axis=-1, keepdims=True) + EPSILON)
    unit_rows = centred * inverse_std
    grad_unit = grad_normed * ln_gain
    grad_input = cotangent[0].astype(jnp.float32) + inverse_std * (
        grad_unit
        - jnp.mean(grad_unit, axis=-1, keepdims=True)
        - unit_rows * jnp.mean(grad_unit * unit_rows, axis=-1, keepdims=True)
    )
    small = sum_all(jnp.concatenate([token_sum(grad_mixed), grad_b_up[0]]), rows, 1)
    grad_b_qkv = small[: 3 * local_width].reshape(3, local_width)
    grad_b_up = small[3 * local_width :]
    tail = sum_all(
        jnp.concatenate([gain_part, shift_part, token_sum(cotangent[0])[None]]), rows, tp
    )
    return (
        hidden_out[None],
        grad_input.astype(jnp.bfloat16)[None],
        tail[0],
        tail[1],
        grad_w_qkv,
        grad_b_qkv,
        grad_w_out,
        tail[2],
        grad_w_up,
        grad_b_up,
        grad_w_down,
    )


def solution(mesh):
    in_specs = (
        P("rows", "tp", None),
        P("rows", "tp"),
        P(),
        P(),
        P(None, None, "tp"),
        P(None, "tp"),
        P("tp", None),
        P(),
        P(None, "tp"),
        P("tp"),
        P("tp", None),
        P("rows", "tp", None),
    )
    out_specs = (
        P("rows", "tp", None),
        P("rows", "tp", None),
        P(),
        P(),
        P(None, None, "tp"),
        P(None, "tp"),
        P("tp", None),
        P(),
        P(None, "tp"),
        P("tp"),
        P("tp", None),
    )
    return jax.shard_map(
        partial(local, mesh.shape["rows"], mesh.shape["tp"]),
        mesh=mesh,
        in_specs=in_specs,
        out_specs=out_specs,
        check_vma=False,
    )
```

time: 679 us -> 457 us (0.67)
  the two profiles are of different devices: /device:TPU:0 before, /device:TPU:16 now
where the time goes in v2:
time: 457 us; the launch traced here: 449 us
  Pallas kernels  244 us (53%)
  waiting for transfers between devices  113 us (25%)
  starting transfers between devices  40.6 us (9%)
  other arithmetic  24.3 us (5%)
  between operations  14.7 us (3%)
  local copies, waits for them, and re-layouts  10.1 us (2%)
    pallas_call x17, Pallas kernels, call(): pl.pallas_call(whole_body, grid_spec=pltpu.PrefetchScalarGridSpec(num_sca...  244 us
    ppermute x3, waiting for transfers between devices, local(): coming = lax.ppermute(mine, 'tp', around)  49.4 us
    ppermute x24, waiting for transfers between devices, swap_rows(): return lax.ppermute(array, 'rows', [(i, i ^ bit) for i in range(4)])  38.5 us
    ppermute x24, starting transfers between devices, swap_rows(): return lax.ppermute(array, 'rows', [(i, i ^ bit) for i in range(4)])  23.5 us
    ppermute x7, waiting for transfers between devices, sum_all(): lax.ppermute(array, axis, [(i, i ^ step) for i in range(size)])  15.2 us
    ppermute x7, starting transfers between devices, sum_all(): lax.ppermute(array, axis, [(i, i ^ step) for i in range(size)])  9.8 us
  transfers between devices with their start and end apart: 45, of which 14 were waited for; matrix products, arithmetic and copies ran while one was open for 6% of the time, Pallas kernels for 54%

profile of v2, /device:TPU:16, one launch (start us, length us, event | category | flops | bytes accessed | tf_op | source)
XLA Modules:
  0.0 449.3 jit_solution(5609274372191332659)
XLA Ops:
  19.3 5.6 %fusion.15 = (f32[2048,128]{1,0:T(8,128)}, f32[2048,128]{1,0:T(8,128)}) fusion(f32[128]{0:T(128)S(1)} %get-tuple-element.354, f32[128]{0:T(128)S(1)} %get-tuple-element.355, f32[2048]{0:T(1024)S(1)} %subtract_convert_fusion, pred[128]{0:T(512)(128)(4,1)S(1)} %broadcast_compare_fusion), kind=kLoop, calls=%fused_computation.34 | loop fusion | flops 1048576 | bytes 2106496 | tf_op jit(solution)/shard_map/jit(_where)/select_n | solution.py:315
  25.9 14.6 %project.4 = (bf16[2048,2048]{1,0:T(8,128)(2,1)}, bf16[2048,2048]{1,0:T(8,128)(2,1)}, bf16[2048,768]{1,0:T(8,128)(2,1)}, bf16[2048,1024]{1,0:T(8,128)(2,1)}, bf1...) custom-call(s32[2]{0:T(128)} %get-tuple-element.351.refs_0_, bf16[256,2048]{1,0:T(8,128)(2,1)} %bitcast.49, ...), custom_call_target="tpu_custom_call" | custom-call | flops 1048576 | bytes 65536 | tf_op jit(solution)/shard_map/project/pallas_call | solution.py:39
  47.0 14.5 %project.5 = (bf16[2048,2048]{1,0:T(8,128)(2,1)}, bf16[2048,2048]{1,0:T(8,128)(2,1)}, bf16[2048,768]{1,0:T(8,128)(2,1)}, bf16[2048,1024]{1,0:T(8,128)(2,1)}, bf1...) custom-call(s32[2]{0:T(128)} %get-tuple-element.352.refs_0_, ...), custom_call_target="tpu_custom_call", output_to_operand_aliasing={{0}: (11, {}), {1}: (12, {}), {2}: (13, {}), {3}: (14, {}),... | custom-call | flops 1048576 | bytes 65536 | tf_op jit(solution)/shard_map/project/pallas_call | solution.py:39
  61.5 7.8 %collective-permute-done.5.refs_1_ = bf16[256,2048]{1,0:T(8,128)(2,1)S(1)} collective-permute-done((bf16[256,2048]{1,0:T(8,128)(2,1)S(1)}, bf16[256,2048]{1,0:T(8,128)(2,1)S(1)}, u32[]{:S(2)}, u32[]{:S(2)}) %collective-permute-start.5) | collective-permute-done | bytes 1048608 | tf_op jit(solution)/shard_map/ppermute | solution.py:761
  73.8 14.5 %project.6 = (bf16[2048,2048]{1,0:T(8,128)(2,1)}, bf16[2048,2048]{1,0:T(8,128)(2,1)}, bf16[2048,768]{1,0:T(8,128)(2,1)}, bf16[2048,1024]{1,0:T(8,128)(2,1)}, bf1...) custom-call(s32[2]{0:T(128)} %get-tuple-element.353.refs_0_, ...), custom_call_target="tpu_custom_call", output_to_operand_aliasing={{0}: (11, {}), {1}: (12, {}), {2}: (13, {}), {3}: (14, {}),... | custom-call | flops 1048576 | bytes 65536 | tf_op jit(solution)/shard_map/project/pallas_call | solution.py:39
  88.3 38.8 %collective-permute-done.7.refs_1_ = bf16[256,2048]{1,0:T(8,128)(2,1)S(1)} collective-permute-done((bf16[256,2048]{1,0:T(8,128)(2,1)S(1)}, bf16[256,2048]{1,0:T(8,128)(2,1)S(1)}, u32[]{:S(2)}, u32[]{:S(2)}) %collective-permute-start.7) | collective-permute-done | bytes 1048608 | tf_op jit(solution)/shard_map/ppermute | solution.py:761
  130.7 14.5 %project.7 = (bf16[2048,2048]{1,0:T(8,128)(2,1)}, bf16[2048,2048]{1,0:T(8,128)(2,1)}, bf16[2048,768]{1,0:T(8,128)(2,1)}, bf16[2048,1024]{1,0:T(8,128)(2,1)}, bf1...) custom-call(s32[2]{0:T(128)} %get-tuple-element.350.refs_0_, ...), custom_call_target="tpu_custom_call", output_to_operand_aliasing={{0}: (11, {}), {1}: (12, {}), {2}: (13, {}), {3}: (14, {}),... | custom-call | flops 1048576 | bytes 65536 | tf_op jit(solution)/shard_map/project/pallas_call | solution.py:39
  145.2 10.4 %outer_parts.4 = (bf16[256,1024]{1,0:T(8,128)(2,1)}, bf16[256,1024]{1,0:T(8,128)(2,1)}, bf16[256,1024]{1,0:T(8,128)(2,1)}, bf16[256,1024]{1,0:T(8,128)(2,1)}, f32[8,128]{1,0:T(8,128)}) custom-call(s32[4]{0:T(128)} %pad_add_fusion.4.refs_0_, bf16[2048,1024]{1,0:T(8,128)(2,1)} %get-tuple-element.215.refs_1_, ...), custom_call_target="tpu_custom_call" | custom-call | flops 1048576 | bytes 65536 | tf_op jit(solution)/shard_map/outer_parts/pallas_call | solution.py:39
  159.8 20.3 %attend_forward.1 = (bf16[2048,256]{1,0:T(8,128)(2,1)}, f32[8,2048]{1,0:T(8,128)}, f32[8,128]{1,0:T(8,128)}) custom-call(s32[8]{0:T(128)} %and_select_fusion.2.refs_0_, s32[8,2048]{1,0:T(8,128)} %broadcast_in_dim.78.refs_1_, bf16[2048,768]{1,0:T(8,128)(2,1)} %get-tuple-element.214.refs_2_.refs_3_.refs_4_.refs_5_, ...), custom_call_target="tpu_custom_call" | custom-call | flops 1048576 | bytes 65536 | tf_op jit(solution)/shard_map/attend_forward/pallas_call | solution.py:39
  180.6 16.2 %branch_sum.1 = (bf16[2048,2048]{1,0:T(8,128)(2,1)}, f32[8,128]{1,0:T(8,128)}) custom-call(bf16[2048,256]{1,0:T(8,128)(2,1)} %get-tuple-element.222.refs_0_.refs_3_.refs_6_, bf16[2048,1024]{1,0:T(8,128)(2,1)} %get-tuple-element.215.refs_1_, bf16[256,2048]{1,0:T(8,128)(2,1)} %refs_3_.3, bf16[1024,2048]{1,0:T(8,128)(2,1)} %refs_2_.3, ...), custom_call_target="tpu_custom_call" | custom-call | flops 1048576 | bytes 65536 | tf_op jit(solution)/shard_map/branch_sum/pallas_call | solution.py:39
  197.1 14.4 %outer_parts.5 = (bf16[384,1024]{1,0:T(8,128)(2,1)}, bf16[384,1024]{1,0:T(8,128)(2,1)}, bf16[384,1024]{1,0:T(8,128)(2,1)}, bf16[384,1024]{1,0:T(8,128)(2,1)}, f32[8,128]{1,0:T(8,128)}) custom-call(s32[4]{0:T(128)} %pad_add_fusion.4.refs_0_, bf16[2048,1024]{1,0:T(8,128)(2,1)} %get-tuple-element.215.refs_1_, ...), custom_call_target="tpu_custom_call" | custom-call | flops 1048576 | bytes 65536 | tf_op jit(solution)/shard_map/outer_parts/pallas_call | solution.py:39
  217.1 17.5 %backward_products.1 = (bf16[2048,1024]{1,0:T(8,128)(2,1)}, bf16[2048,256]{1,0:T(8,128)(2,1)}, f32[1,1024]{1,0:T(1,128)}, f32[8,128]{1,0:T(8,128)}) custom-call(bf16[2048,1024]{1,0:T(8,128)(2,1)} %all-gather.3.cloned.1.call-done.refs_2_.refs_4_.refs_0_, bf16[2048,1024]{1,0:T(8,128)(2,1)} %all-gather.5.cloned.1.call-done.refs_2_.refs_1_, ...), custom_call_target="tpu_custom_call" | custom-call | flops 1048576 | bytes 65536 | tf_op jit(solution)/shard_map/backward_products/pallas_call | solution.py:39
  242.3 15.6 %outer_parts.6 = (bf16[512,1024]{1,0:T(8,128)(2,1)}, bf16[512,1024]{1,0:T(8,128)(2,1)}, bf16[512,1024]{1,0:T(8,128)(2,1)}, bf16[512,1024]{1,0:T(8,128)(2,1)}, f32[8,128]{1,0:T(8,128)}) custom-call(s32[4]{0:T(128)} %pad_add_fusion.4.refs_0_, bf16[2048,2048]{1,0:T(8,128)(2,1)} %get-tuple-element.246.refs_1_, ...), custom_call_target="tpu_custom_call" | custom-call | flops 1048576 | bytes 65536 | tf_op jit(solution)/shard_map/outer_parts/pallas_call | solution.py:39
  262.4 31.6 %attend_backward.1 = (bf16[2048,768]{1,0:T(8,128)(2,1)}, f32[8,128]{1,0:T(8,128)}) custom-call(s32[8]{0:T(128)} %and_select_fusion.2.refs_0_, s32[8,2048]{1,0:T(8,128)} %broadcast_in_dim.78.refs_1_, f32[8,2048]{1,0:T(8,128)} %get-tuple-element.265.refs_2_, bf16[2048,768]{1,0:T(8,128)(2,1)} %get-tuple-element.214.refs_2_.refs_3_.refs_4_.refs_5_, ...), custom_call_target="tpu_custom_call" | custom-call | flops 63201050624 | bytes 65536 | tf_op jit(solution)/shard_map/attend_backward/pallas_call | solution.py:39
  299.5 4.7 %finish.4 = (f32[1024,2048]{1,0:T(8,128)}, f32[8,128]{1,0:T(8,128)}) custom-call(s32[4]{0:T(128)} %pad_add_fusion.5.refs_0_, bf16[256,1024]{1,0:T(8,128)(2,1)} %copy-done.23, bf16[256,1024]{1,0:T(8,128)(2,1)} %collective-permute-done.14.refs_2_, bf16[256,1024]{1,0:T(8,128)(2,1)} %copy-done.22, bf16[256,1024]{1,0:T(8,128)(2,1)} %collective-permute-done.15.refs_4_, ...), custom_call_target="tpu_custom_call" | custom-call | flops 46001049600 | bytes 65536 | tf_op jit(solution)/shard_map/finish/pallas_call | solution.py:39
  304.2 24.9 %normed_sum.1 = (bf16[2048,2048]{1,0:T(8,128)(2,1)}, f32[1,2048]{1,0:T(1,128)}, f32[1,2048]{1,0:T(1,128)}, f32[8,128]{1,0:T(8,128)}) custom-call(bf16[2048,768]{1,0:T(8,128)(2,1)} %get-tuple-element.285.refs_0_.refs_2_, bf16[2048,1024]{1,0:T(8,128)(2,1)} %get-tuple-element.249.refs_2_.refs_1_, bf16[2048,2048]{1,0:T(8,128)(2,1)} %get-tuple-element.286.refs_2_, ...), custom_call_target="tpu_custom_call" | custom-call | flops 1048576 | bytes 65536 | tf_op jit(solution)/shard_map/normed_sum/pallas_call | solution.py:39
  329.8 12.9 %outer_parts.7 = (bf16[512,768]{1,0:T(8,128)(2,1)}, bf16[512,768]{1,0:T(8,128)(2,1)}, bf16[512,768]{1,0:T(8,128)(2,1)}, bf16[512,768]{1,0:T(8,128)(2,1)}, f32[8,128]{1,0:T(8,128)}) custom-call(s32[4]{0:T(128)} %pad_add_fusion.4.refs_0_, bf16[2048,2048]{1,0:T(8,128)(2,1)} %get-tuple-element.246.refs_1_, bf16[2048,768]{1,0:T(8,128)(2,1)} %get-tuple-element.285.refs_0_.refs_2_, ...), custom_call_target="tpu_custom_call" | custom-call | flops 1048576 | bytes 65536 | tf_op jit(solution)/shard_map/outer_parts/pallas_call | solution.py:39
  352.8 5.7 %finish.5 = (f32[1024,2048]{1,0:T(8,128)}, f32[256,2048]{1,0:T(8,128)}, f32[8,128]{1,0:T(8,128)}) custom-call(s32[4]{0:T(128)} %pad_add_fusion.5.refs_0_, bf16[384,1024]{1,0:T(8,128)(2,1)} %add_convert_fusion.9.refs_1_, bf16[384,1024]{1,0:T(8,128)(2,1)} %collective-permute-done.29.refs_2_, ...), custom_call_target="tpu_custom_call", output_to_operand_aliasing={{0}: (5, {})} | custom-call | flops 46001049600 | bytes 65536 | tf_op jit(solution)/shard_map/finish/pallas_call | solution.py:39
  360.5 8.5 %collective-permute-done.27 = bf16[512,768]{1,0:T(8,128)(2,1)S(1)} collective-permute-done((bf16[512,768]{1,0:T(8,128)(2,1)}, bf16[512,768]{1,0:T(8,128)(2,1)S(1)}, u32[]{:S(2)}, u32[]{:S(2)}) %collective-permute-start.27) | collective-permute-done | bytes 786464 | tf_op jit(solution)/shard_map/ppermute | solution.py:590
  372.3 19.3 %collective-permute-done.35.refs_2_ = bf16[512,1024]{1,0:T(8,128)(2,1)S(1)} collective-permute-done((bf16[512,1024]{1,0:T(8,128)(2,1)S(1)}, bf16[512,1024]{1,0:T(8,128)(2,1)S(1)}, u32[]{:S(2)}, u32[]{:S(2)}) %collective-permute-start.35) | collective-permute-done | bytes 1048608 | tf_op jit(solution)/shard_map/ppermute | solution.py:590
  393.7 6.5 %finish.6 = (f32[2048,1024]{1,0:T(8,128)}, f32[8,128]{1,0:T(8,128)}) custom-call(s32[4]{0:T(128)} %pad_add_fusion.5.refs_0_, bf16[512,1024]{1,0:T(8,128)(2,1)} %copy-done.9, bf16[512,1024]{1,0:T(8,128)(2,1)} %copy-done.34, bf16[512,1024]{1,0:T(8,128)(2,1)} %copy-done.7, bf16[512,1024]{1,0:T(8,128)(2,1)} %collective-permute-done.36.refs_4_, ...), custom_call_target="tpu_custom_call" | custom-call | flops 46001049600 | bytes 65536 | tf_op jit(solution)/shard_map/finish/pallas_call | solution.py:39
  400.3 9.2 %collective-permute-done.33 = bf16[512,768]{1,0:T(8,128)(2,1)S(1)} collective-permute-done((bf16[512,768]{1,0:T(8,128)(2,1)S(1)}, bf16[512,768]{1,0:T(8,128)(2,1)S(1)}, u32[]{:S(2)}, u32[]{:S(2)}) %collective-permute-start.33) | collective-permute-done | bytes 786464 | tf_op jit(solution)/shard_map/ppermute | solution.py:590
  415.1 15.2 %collective-permute-done.40 = f32[1792]{0:T(1024)S(1)} collective-permute-done((f32[1792]{0:T(1024)S(1)}, f32[1792]{0:T(1024)S(1)}, u32[]{:S(2)}, u32[]{:S(2)}) %collective-permute-start.40) | collective-permute-done | bytes 7200 | tf_op jit(solution)/shard_map/ppermute | solution.py:685
  432.2 5.7 %finish.7 = (f32[3,2048,256]{2,1,0:T(8,128)}, f32[8,128]{1,0:T(8,128)}) custom-call(s32[4]{0:T(128)} %pad_add_fusion.5.refs_0_, bf16[512,768]{1,0:T(8,128)(2,1)} %copy-done.19, bf16[512,768]{1,0:T(8,128)(2,1)} %collective-permute-done.37.refs_2_, bf16[512,768]{1,0:T(8,128)(2,1)} %copy-done.18, bf16[512,768]{1,0:T(8,128)(2,1)} %collective-permute-done.38.refs_4_, ...), custom_call_target="tpu_custom_call" | custom-call | flops 46001049600 | bytes 65536 | tf_op jit(solution)/shard_map/finish/pallas_call | solution.py:39
  (215 shorter events, 85.9 us)
Async XLA Ops:
  7.2 138.0 %all-gather.3.cloned.1.call-start = ((), (), s32[]{:S(2)}) async-start(), calls=%async_computation.2 | async-start | bytes 4718592 | tf_op jit(solution)/shard_map/all_gather | solution.py:768
  17.5 25.8 %collective-permute-start.3 = (bf16[256,2048]{1,0:T(8,128)(2,1)}, bf16[256,2048]{1,0:T(8,128)(2,1)S(1)}, u32[]{:S(2)}, u32[]{:S(2)}) collective-permute-start(bf16[256,2048]{1,0:T(8,128)(2,1)} %bitcast.48), channel_id=1, source_target_pairs={{0,2},{1,3},{2,4},{3,5},{4,6},{5,7},{6,0},{7,1},{8,10},{9,11},{10,... | collective-permute-start | bytes 3145736 | tf_op jit(solution)/shard_map/ppermute | solution.py:738
  43.3 26.0 %collective-permute-start.5 = (bf16[256,2048]{1,0:T(8,128)(2,1)S(1)}, bf16[256,2048]{1,0:T(8,128)(2,1)S(1)}, u32[]{:S(2)}, u32[]{:S(2)}) collective-permute-start(bf16[256,2048]{1,0:T(8,128)(2,1)S(1)} %collective-permute-done.3.refs_1_), channel_id=1, source_target_pairs={{0,2},{1,3},{2,4},{3,5},{4,6},{5,7},{6,0},{7,1},{8,10},{9,11},{10,... | collective-permute-start | bytes 3145736 | tf_op jit(solution)/shard_map/ppermute | solution.py:761
  69.3 127.7 %all-gather.5.cloned.1.call-start = ((), (), s32[]{:S(2)}) async-start(), calls=%async_computation.4 | async-start | bytes 4718592 | tf_op jit(solution)/shard_map/all_gather | solution.py:768
  70.1 234.1 %reduce-scatter.3.cloned.1.call-start = ((), (), s32[]{:S(2)}) async-start(), calls=%async_computation.3 | async-start | bytes 9437184 | tf_op jit(solution)/shard_map/reduce_scatter | solution.py:777
  70.2 56.9 %collective-permute-start.7 = (bf16[256,2048]{1,0:T(8,128)(2,1)S(1)}, bf16[256,2048]{1,0:T(8,128)(2,1)S(1)}, u32[]{:S(2)}, u32[]{:S(2)}) collective-permute-start(bf16[256,2048]{1,0:T(8,128)(2,1)S(1)} %collective-permute-done.5.refs_1_), channel_id=1, source_target_pairs={{0,2},{1,3},{2,4},{3,5},{4,6},{5,7},{6,0},{7,1},{8,10},{9,11},{10,... | collective-permute-start | bytes 3145736 | tf_op jit(solution)/shard_map/ppermute | solution.py:761
  155.6 24.6 %collective-permute-start.10 = (bf16[256,1024]{1,0:T(8,128)(2,1)}, bf16[256,1024]{1,0:T(8,128)(2,1)S(1)}, u32[]{:S(2)}, u32[]{:S(2)}) collective-permute-start(bf16[256,1024]{1,0:T(8,128)(2,1)} %get-tuple-element.224), channel_id=1, source_target_pairs={{0,8},{8,0},{16,24},{24,16},{1,9},{9,1},{17,25},{25,17},{2,10},{10... | collective-permute-start | bytes 1572872 | tf_op jit(solution)/shard_map/ppermute | solution.py:590
  157.1 23.1 %collective-permute-start.11 = (bf16[256,1024]{1,0:T(8,128)(2,1)}, bf16[256,1024]{1,0:T(8,128)(2,1)S(1)}, u32[]{:S(2)}, u32[]{:S(2)}) collective-permute-start(bf16[256,1024]{1,0:T(8,128)(2,1)} %get-tuple-element.225), channel_id=1, source_target_pairs={{0,16},{8,24},{16,0},{24,8},{1,17},{9,25},{17,1},{25,9},{2,18},{10... | collective-permute-start | bytes 1572872 | tf_op jit(solution)/shard_map/ppermute | solution.py:590
  196.8 241.0 %reduce-scatter.5.cloned.1.call-start = ((), (), s32[]{:S(2)}) async-start(), calls=%async_computation.5 | async-start | bytes 9437184 | tf_op jit(solution)/shard_map/reduce_scatter | solution.py:791
  211.4 23.2 %collective-permute-start.16 = (bf16[384,1024]{1,0:T(8,128)(2,1)}, bf16[384,1024]{1,0:T(8,128)(2,1)S(1)}, u32[]{:S(2)}, u32[]{:S(2)}) collective-permute-start(bf16[384,1024]{1,0:T(8,128)(2,1)} %get-tuple-element.251), channel_id=1, source_target_pairs={{0,8},{8,0},{16,24},{24,16},{1,9},{9,1},{17,25},{25,17},{2,10},{10... | collective-permute-start | bytes 2359304 | tf_op jit(solution)/shard_map/ppermute | solution.py:590
  236.1 21.9 %collective-permute-start.20 = (bf16[384,1024]{1,0:T(8,128)(2,1)S(1)}, bf16[384,1024]{1,0:T(8,128)(2,1)S(1)}, u32[]{:S(2)}, u32[]{:S(2)}) collective-permute-start(bf16[384,1024]{1,0:T(8,128)(2,1)S(1)} %add_convert_fusion.11), channel_id=1, source_target_pairs={{0,16},{8,24},{16,0},{24,8},{1,17},{9,25},{17,1},{25,9},{2,18},{10... | collective-permute-start | bytes 2359304 | tf_op jit(solution)/shard_map/ppermute | solution.py:590
  238.4 59.8 %collective-permute-start.14 = (bf16[256,1024]{1,0:T(8,128)(2,1)S(1)}, bf16[256,1024]{1,0:T(8,128)(2,1)}, u32[]{:S(2)}, u32[]{:S(2)}) collective-permute-start(bf16[256,1024]{1,0:T(8,128)(2,1)S(1)} %add_convert_fusion.13.refs_1_), channel_id=1, source_target_pairs={{0,8},{8,0},{16,24},{24,16},{1,9},{9,1},{17,25},{25,17},{2,10},{10... | collective-permute-start | bytes 1572872 | tf_op jit(solution)/shard_map/ppermute | solution.py:590
  240.4 57.8 %collective-permute-start.15 = (bf16[256,1024]{1,0:T(8,128)(2,1)S(1)}, bf16[256,1024]{1,0:T(8,128)(2,1)}, u32[]{:S(2)}, u32[]{:S(2)}) collective-permute-start(bf16[256,1024]{1,0:T(8,128)(2,1)S(1)} %add_convert_fusion.12.refs_3_), channel_id=1, source_target_pairs={{0,16},{8,24},{16,0},{24,8},{1,17},{9,25},{17,1},{25,9},{2,18},{10... | collective-permute-start | bytes 1572872 | tf_op jit(solution)/shard_map/ppermute | solution.py:590
  257.9 38.6 %collective-permute-start.18 = (bf16[512,1024]{1,0:T(8,128)(2,1)}, bf16[512,1024]{1,0:T(8,128)(2,1)S(1)}, u32[]{:S(2)}, u32[]{:S(2)}) collective-permute-start(bf16[512,1024]{1,0:T(8,128)(2,1)} %get-tuple-element.263), channel_id=1, source_target_pairs={{0,8},{8,0},{16,24},{24,16},{1,9},{9,1},{17,25},{25,17},{2,10},{10... | collective-permute-start | bytes 3145736 | tf_op jit(solution)/shard_map/ppermute | solution.py:590
  258.0 38.6 %collective-permute-start.19 = (bf16[512,1024]{1,0:T(8,128)(2,1)}, bf16[512,1024]{1,0:T(8,128)(2,1)S(1)}, u32[]{:S(2)}, u32[]{:S(2)}) collective-permute-start(bf16[512,1024]{1,0:T(8,128)(2,1)} %get-tuple-element.264), channel_id=1, source_target_pairs={{0,16},{8,24},{16,0},{24,8},{1,17},{9,25},{17,1},{25,9},{2,18},{10... | collective-permute-start | bytes 3145736 | tf_op jit(solution)/shard_map/ppermute | solution.py:590
  260.5 87.9 %collective-permute-start.29 = (bf16[384,1024]{1,0:T(8,128)(2,1)}, bf16[384,1024]{1,0:T(8,128)(2,1)}, u32[]{:S(2)}, u32[]{:S(2)}) collective-permute-start(bf16[384,1024]{1,0:T(8,128)(2,1)} %add_convert_fusion.9.refs_1_), channel_id=1, source_target_pairs={{0,8},{8,0},{16,24},{24,16},{1,9},{9,1},{17,25},{25,17},{2,10},{10... | collective-permute-start | bytes 2359304 | tf_op jit(solution)/shard_map/ppermute | solution.py:590
  296.5 51.9 %collective-permute-start.30 = (bf16[384,1024]{1,0:T(8,128)(2,1)}, bf16[384,1024]{1,0:T(8,128)(2,1)}, u32[]{:S(2)}, u32[]{:S(2)}) collective-permute-start(bf16[384,1024]{1,0:T(8,128)(2,1)} %add_convert_fusion.8.refs_3_), channel_id=1, source_target_pairs={{0,16},{8,24},{16,0},{24,8},{1,17},{9,25},{17,1},{25,9},{2,18},{10... | collective-permute-start | bytes 2359304 | tf_op jit(solution)/shard_map/ppermute | solution.py:590
  298.1 44.6 %collective-permute-start.31 = (bf16[512,1024]{1,0:T(8,128)(2,1)S(1)}, bf16[512,1024]{1,0:T(8,128)(2,1)S(1)}, u32[]{:S(2)}, u32[]{:S(2)}) collective-permute-start(bf16[512,1024]{1,0:T(8,128)(2,1)S(1)} %add_convert_fusion.3), channel_id=1, source_target_pairs={{0,16},{8,24},{16,0},{24,8},{1,17},{9,25},{17,1},{25,9},{2,18},{10... | collective-permute-start | bytes 3145736 | tf_op jit(solution)/shard_map/ppermute | solution.py:590
  299.5 43.2 %collective-permute-start.32 = (bf16[512,1024]{1,0:T(8,128)(2,1)S(1)}, bf16[512,1024]{1,0:T(8,128)(2,1)}, u32[]{:S(2)}, u32[]{:S(2)}) collective-permute-start(bf16[512,1024]{1,0:T(8,128)(2,1)S(1)} %add_convert_fusion.2), channel_id=1, source_target_pairs={{0,8},{8,0},{16,24},{24,16},{1,9},{9,1},{17,25},{25,17},{2,10},{10... | collective-permute-start | bytes 3145736 | tf_op jit(solution)/shard_map/ppermute | solution.py:590
  351.2 40.4 %collective-permute-start.35 = (bf16[512,1024]{1,0:T(8,128)(2,1)S(1)}, bf16[512,1024]{1,0:T(8,128)(2,1)S(1)}, u32[]{:S(2)}, u32[]{:S(2)}) collective-permute-start(bf16[512,1024]{1,0:T(8,128)(2,1)S(1)} %add_convert_fusion.1.refs_1_), channel_id=1, source_target_pairs={{0,8},{8,0},{16,24},{24,16},{1,9},{9,1},{17,25},{25,17},{2,10},{10... | collective-permute-start | bytes 3145736 | tf_op jit(solution)/shard_map/ppermute | solution.py:590
  351.2 42.5 %collective-permute-start.36 = (bf16[512,1024]{1,0:T(8,128)(2,1)S(1)}, bf16[512,1024]{1,0:T(8,128)(2,1)}, u32[]{:S(2)}, u32[]{:S(2)}) collective-permute-start(bf16[512,1024]{1,0:T(8,128)(2,1)S(1)} %add_convert_fusion.refs_3_), channel_id=1, source_target_pairs={{0,16},{8,24},{16,0},{24,8},{1,17},{9,25},{17,1},{25,9},{2,18},{10... | collective-permute-start | bytes 3145736 | tf_op jit(solution)/shard_map/ppermute | solution.py:590
  358.5 54.4 %collective-permute-start.39 = (f32[1792]{0:T(1024)S(1)}, f32[1792]{0:T(1024)S(1)}, u32[]{:S(2)}, u32[]{:S(2)}) collective-permute-start(f32[1792]{0:T(1024)S(1)} %pad_maximum_fusion.1), channel_id=1, source_target_pairs={{0,8},{8,0},{16,24},{24,16},{1,9},{9,1},{17,25},{25,17},{2,10},{10... | collective-permute-start | bytes 21512 | tf_op jit(solution)/shard_map/ppermute | solution.py:685
  369.1 45.3 %collective-permute-start.25 = (f32[3,2048]{1,0:T(4,128)S(1)}, f32[3,2048]{1,0:T(4,128)S(1)}, u32[]{:S(2)}, u32[]{:S(2)}) collective-permute-start(f32[3,2048]{1,0:T(4,128)S(1)} %add.226), channel_id=1, source_target_pairs={{0,8},{8,0},{16,24},{24,16},{1,9},{9,1},{17,25},{25,17},{2,10},{10... | collective-permute-start | bytes 73736 | tf_op jit(solution)/shard_map/ppermute | solution.py:685
  371.6 37.9 %collective-permute-start.33 = (bf16[512,768]{1,0:T(8,128)(2,1)S(1)}, bf16[512,768]{1,0:T(8,128)(2,1)S(1)}, u32[]{:S(2)}, u32[]{:S(2)}) collective-permute-start(bf16[512,768]{1,0:T(8,128)(2,1)S(1)} %add_convert_fusion.7), channel_id=1, source_target_pairs={{0,16},{8,24},{16,0},{24,8},{1,17},{9,25},{17,1},{25,9},{2,18},{10... | collective-permute-start | bytes 2359304 | tf_op jit(solution)/shard_map/ppermute | solution.py:590
  (56 other events, 585.3 us)
Sparse Core Ops, SparseCore 0:
  69.5 65.4 all-gather.2
  136.6 45.8 all-gather.4
  197.0 87.6 reduce-scatter.2
  329.2 91.0 reduce-scatter.4

commit v3 on v2

--- a/solution.py
+++ b/solution.py
@@ -145,7 +145,7 @@
         rows = pl.ds(h * HEAD_DIM, HEAD_DIM)
         acc[rows, :] = acc[rows, :] / sums[h]
         lse[h : h + 1, :] = tops[h] + jnp.log(sums[h])
-    context[...] = acc[...].T.astype(jnp.bfloat16)
+    context[...] = acc[...].astype(jnp.bfloat16).T
 
 
 def attend_forward(line, lows, starts, mixed, block):
@@ -179,7 +179,7 @@
 
 
 def backward_kernel(
-    lows, starts, lse, q, k, v, context, grad, cosine, sine, grad_mixed, k_t, k_heads, v_heads, grad_q, grad_k, grad_v
+    lows, starts, lse, q, k, v, context, grad, cosine, sine, turned_tables, grad_mixed, k_t, k_heads, v_heads, grad_q, grad_k, grad_v
 ):
     block, width = q.shape
     heads = width // HEAD_DIM
@@ -204,11 +204,14 @@
     masked_g = [jnp.where(row_heads == h, grads, 0).astype(jnp.bfloat16) for h in range(heads)]
     turned_q = scaled.T
     turned_g = grads.T
-    products = (grads.astype(jnp.float32) * context[...].astype(jnp.float32)).T
-    inner = [
-        jnp.sum(products[h * HEAD_DIM : (h + 1) * HEAD_DIM, :], axis=0, keepdims=True)
-        for h in range(heads)
-    ]
+    products = grads.astype(jnp.float32) * context[...].astype(jnp.float32)
+    high = products.astype(jnp.bfloat16)
+    low = (products - high.astype(jnp.float32)).astype(jnp.bfloat16)
+    chooser = lax.broadcasted_iota(jnp.int32, (8, width), 0) == lane_heads(8, width)
+    chooser = jnp.where(chooser, 1.0, 0.0).astype(jnp.bfloat16)
+    sums = lax.dot_general(chooser, high, NT, preferred_element_type=jnp.float32)
+    sums = sums + lax.dot_general(chooser, low, NT, preferred_element_type=jnp.float32)
+    inner = [sums[h : h + 1, :] for h in range(heads)]
     grad_q[...] = jnp.zeros_like(grad_q)
 
     def step(j, carry):
@@ -250,7 +253,14 @@
         return jnp.concatenate(parts, axis=1).astype(jnp.bfloat16)
 
     mine = pl.ds(pl.multiple_of(i * block, block), block)
-    grad_mixed[mine, 0:width] = unrotate(grad_q[...].T * 0.125, mine)
+    cos_t, sin_t = turned_tables[0 : ROT // 2, :], turned_tables[ROT // 2 : ROT, :]
+    for h in range(heads):
+        top = pl.ds(h * HEAD_DIM, ROT // 2)
+        bottom = pl.ds(h * HEAD_DIM + ROT // 2, ROT // 2)
+        one, two = grad_q[top, :], grad_q[bottom, :]
+        grad_q[top, :] = one * cos_t + two * sin_t
+        grad_q[bottom, :] = two * cos_t - one * sin_t
+    grad_mixed[mine, 0:width] = (grad_q[...] * 0.125).astype(jnp.bfloat16).T
 
     @pl.when(i == blocks - 1)
     def _():
@@ -263,7 +273,7 @@
         lax.fori_loop(0, blocks, finish, 0)
 
 
-def attend_backward(line, lows, starts, lse, mixed, context, grad_context, cosine, sine, block):
+def attend_backward(line, lows, starts, lse, mixed, context, grad_context, cosine, sine, turned, block):
     length, triple = mixed.shape
     local_width = triple // 3
     blocks = length // block
@@ -273,7 +283,7 @@
         backward_kernel,
         "attend_backward",
         (blocks,),
-        [lows, starts, lse, mixed, mixed, mixed, context, grad_context, cosine, sine],
+        [lows, starts, lse, mixed, mixed, mixed, context, grad_context, cosine, sine, turned],
         [
             pl.BlockSpec((8, block), column),
             pl.BlockSpec((8, block), column),
@@ -284,6 +294,7 @@
             pl.BlockSpec((block, local_width), row),
             pl.BlockSpec((length, 128), whole),
             pl.BlockSpec((length, 128), whole),
+            pl.BlockSpec((ROT, block), column),
         ],
         [((length, triple), jnp.bfloat16, pl.BlockSpec((length, triple), whole))],
         scalars=1,
@@ -313,7 +324,8 @@
     rotated = (lane < ROT)[None, :]
     cosine = jnp.where(rotated, jnp.cos(angles), 1.0)
     sine = jnp.where(rotated, jnp.where((lane < ROT // 2)[None, :], -1.0, 1.0) * jnp.sin(angles), 0.0)
-    return cosine, sine
+    turned = jnp.concatenate([cosine[:, : ROT // 2], sine[:, ROT // 2 : ROT]], axis=1).T
+    return cosine, sine, turned
 
 
 def gelu_pair(u):
@@ -552,7 +564,7 @@
                         start += rows
 
 
-def finish(line, order, pieces, layout, carried=()):
+def finish(line, order, pieces, layout, carried=(), cost=0):
     rows, columns = pieces[0].shape
     in_specs = [pl.BlockSpec(pieces[0].shape, whole) for _ in range(4)]
     in_specs += [pl.BlockSpec(memory_space=pl.ANY)] * len(carried)
@@ -578,7 +590,7 @@
         outs,
         scalars=1,
         aliases={5 + i: i for i in range(len(carried))},
-        cost=460 * 10**8,
+        cost=cost,
     )
 
 
@@ -674,30 +686,59 @@
             self.pieces = [self.keep[0], came[0], self.keep[1], came[1]]
 
     def finish(self, *layout, **more):
-        self.advance()
+        if self.phase < 3:
+            self.advance()
         return finish(self.line, self.order, self.pieces, *layout, **more)
 
 
-def sum_all(array, rows, tp):
-    for axis, size in (("tp", tp), ("rows", rows)):
-        step = 1
-        while step < size:
-            array = array + lax.ppermute(array, axis, [(i, i ^ step) for i in range(size)])
-            step *= 2
-    return array
-
-
-def gather_small(array, me, tp):
-    step = 1
-    while step < tp:
-        other = lax.ppermute(array, "tp", [(i, i ^ step) for i in range(tp)])
-        array = jnp.where(
-            (me // step) % 2 == 0,
+class SmallSum:
+    def __init__(self, line, array, more, rows, tp):
+        self.line, self.array, self.more = line, array, more
+        self.steps = [("tp", 1 << i, tp) for i in range(tp.bit_length() - 1)]
+        self.steps += [("rows", 1 << i, rows) for i in range(rows.bit_length() - 1)]
+        self.send()
+
+    def send(self):
+        if self.steps:
+            axis, step, size = self.steps.pop(0)
+            if axis == "rows" and self.more is not None:
+                self.array, self.more = jnp.concatenate([self.array, self.more]), None
+            (self.array,) = self.line.join(self.array)
+            self.came = lax.ppermute(self.array, axis, [(i, i ^ step) for i in range(size)])
+        else:
+            self.came = None
+
+    def step(self):
+        if self.came is not None:
+            (came,) = self.line.join(self.came)
+            self.array = self.array + came
+            self.send()
+
+    def rest(self):
+        while self.came is not None:
+            self.step()
+        return self.array
+
+
+class SmallGather:
+    def __init__(self, line, array, me, tp):
+        self.line, self.me, self.step = line, me, 1
+        while 2 * self.step < tp:
+            other = lax.ppermute(array, "tp", [(i, i ^ self.step) for i in range(tp)])
+            array = self.laid(array, other)
+            self.step *= 2
+        (self.array,) = line.join(array)
+        self.other = lax.ppermute(self.array, "tp", [(i, i ^ self.step) for i in range(tp)])
+
+    def laid(self, array, other):
+        return jnp.where(
+            (self.me // self.step) % 2 == 0,
             jnp.concatenate([array, other]),
             jnp.concatenate([other, array]),
         )
-        step *= 2
-    return array
+
+    def whole(self):
+        return self.line.join(self.laid(self.array, *self.line.join(self.other)))[0]
 
 
 def token_sum(matrix):
@@ -733,10 +774,26 @@
 
     around = [(i, (i + 2) % tp) for i in range(tp)]
     sibling = [(i, i ^ 1) for i in range(tp)]
-    segments = gather_small(segment_ids[0], me, tp)
-    mine, segments = lax.optimization_barrier((x, segments))
-    coming = lax.ppermute(mine, "tp", around)
-    other = lax.ppermute(mine, "tp", sibling)
+    mine, others = [x], [lax.ppermute(x, "tp", sibling)]
+    coming = lax.ppermute(x, "tp", around)
+    ids = SmallGather(line, segment_ids[0], me, tp)
+    grads = []
+
+    def serve():
+        nonlocal coming
+        (arrived,) = line.join(coming)
+        mine.append(arrived)
+        if len(mine) < chips:
+            coming = lax.ppermute(arrived, "tp", around)
+        others.append(lax.ppermute(arrived, "tp", sibling))
+        if len(mine) == max(chips - 1, 2):
+            halves = [cotangent[0, :, :columns], cotangent[0, :, columns:]]
+            *halves, mine[-1] = lax.optimization_barrier((*halves, arrived))
+            grads.extend(lax.all_gather(half, "tp", axis=0, tiled=True) for half in halves)
+
+    columns = width // 2
+    serve()
+    segments = ids.whole()
     starts = positions_of(segments)
     tables = rotary_tables(jnp.arange(length, dtype=jnp.int32) - starts)
     lows = starts[::block] // block
@@ -751,21 +808,19 @@
         b_up.reshape(1, hidden),
     )
     carried = ()
-    for s in range(chips):
+
+    def project_slot(s):
         place = jnp.stack([(chip - s + chips) % chips, core]).astype(jnp.int32)
-        mine, other = line.join(mine, other)
-        carried = project(line, place, mine, other, weights, tables, length, carried)
-        if s < chips - 1:
-            (mine,) = line.join(coming)
-            if s < chips - 2:
-                coming = lax.ppermute(mine, "tp", around)
-            other = lax.ppermute(mine, "tp", sibling)
-            if s == max(chips - 3, 0):
-                chunks = 2
-                columns = width // chunks
-                pieces = [cotangent[0, :, c * columns : (c + 1) * columns] for c in range(chunks)]
-                *pieces, mine = lax.optimization_barrier((*pieces, mine))
-                grads = [lax.all_gather(piece, "tp", axis=0, tiled=True) for piece in pieces]
+        pair = line.join(mine[s], others[s])
+        return project(line, place, *pair, weights, tables[:2], length, carried)
+
+    carried = project_slot(0)
+    for s in range(1, chips):
+        if s > 1:
+            serve()
+        if s != 1 or chips == 2:
+            for t in (1, 2) if s == 2 else (s,):
+                carried = project_slot(t)
     normed, unit, mixed, activated, slope = carried
 
     hidden_parts, local_parts = hidden // 4, local_width // 4
@@ -784,20 +839,35 @@
     grad_mixed = attend_backward(
         line, lows, starts, lse, mixed, context, grad_context, *tables, block
     )
+    d0.advance()
     up.advance()
-    down = d0.finish([(hidden_parts, columns, width, 0)])
+    d1.advance()
     (branch_total,) = line.join(branch_total)
     part, gain_part, shift_part = normed_sum(line, grad_mixed, grad_up, unit, w_three, w_up)
     grad_normed = lax.psum_scatter(part, "tp", scatter_dimension=0, tiled=True).astype(jnp.float32)
+    up.advance()
     three = sums(normed, grad_mixed)
-    up.advance()
+    small = SmallSum(
+        line,
+        jnp.concatenate([gain_part, shift_part, token_sum(cotangent[0])[None]], axis=1)[0],
+        jnp.concatenate([token_sum(grad_mixed), grad_b_up[0]]),
+        rows,
+        tp,
+    )
+    down = d0.finish([(hidden_parts, columns, width, 0)])
+    small.step()
     down = d1.finish(
         [(hidden_parts, columns, width, 1), (local_parts, width, width, 0)], carried=down
     )
+    up.advance()
     three.advance()
-    up = up.finish([(width // 4, hidden, hidden, 0)])
+    small.step()
+    up = up.finish([(width // 4, hidden, hidden, 0)], cost=1035 * 10**8)
     three.advance()
-    three = three.finish(3)
+    small.step()
+    small.step()
+    three = three.finish(3, cost=230 * 10**8)
+    small = small.rest()
     grad_w_down, grad_w_out = down
     grad_w_up = up[0]
     grad_w_qkv = jnp.transpose(three[0], (1, 0, 2))
@@ -814,12 +884,9 @@
         - jnp.mean(grad_unit, axis=-1, keepdims=True)
         - unit_rows * jnp.mean(grad_unit * unit_rows, axis=-1, keepdims=True)
     )
-    small = sum_all(jnp.concatenate([token_sum(grad_mixed), grad_b_up[0]]), rows, 1)
-    grad_b_qkv = small[: 3 * local_width].reshape(3, local_width)
-    grad_b_up = small[3 * local_width :]
-    tail = sum_all(
-        jnp.concatenate([gain_part, shift_part, token_sum(cotangent[0])[None]]), rows, tp
-    )
+    tail = small[: 3 * width].reshape(3, width)
+    grad_b_qkv = small[3 * width : 3 * (width + local_width)].reshape(3, local_width)
+    grad_b_up = small[3 * (width + local_width) :]
     return (
         hidden_out[None],
         grad_input.astype(jnp.bfloat16)[None],

time: 457 us -> 443 us (0.969)
  the two profiles are of different devices: /device:TPU:16 before, /device:TPU:0 now
where the time goes in v3:
time: 443 us; the launch traced here: 435 us
  Pallas kernels  244 us (55%)
  waiting for transfers between devices  68.2 us (15%)
  starting transfers between devices  65.5 us (15%)
  other arithmetic  26.7 us (6%)
  between operations  14.9 us (3%)
  local copies, waits for them, and re-layouts  14.7 us (3%)
    pallas_call x17, Pallas kernels, call(): pl.pallas_call(whole_body, grid_spec=pltpu.PrefetchScalarGridSpec(num_sca...  244 us
    ppermute x5, starting transfers between devices, send(): lax.ppermute(self.array, axis, [(i, i ^ step) for i in range(size)])  28.7 us
    ppermute x24, starting transfers between devices, swap_rows(): return lax.ppermute(array, 'rows', [(i, i ^ bit) for i in range(4)])  25 us
    ppermute x5, waiting for transfers between devices, send(): lax.ppermute(self.array, axis, [(i, i ^ step) for i in range(size)])  18.5 us
    ppermute x2, waiting for transfers between devices, __init__(): other = lax.ppermute(array, 'tp', [(i, i ^ self.step) for i in range(tp)])  17.7 us
    ppermute x2, waiting for transfers between devices, serve(): coming = lax.ppermute(arrived, 'tp', around)  14.5 us
    convert_element_type x16, other arithmetic, add_low(): (one.astype(jnp.float32) + other.astype(jnp.float32)).astype(jnp.bfloat16)  13.7 us
    ppermute x24, waiting for transfers between devices, swap_rows(): return lax.ppermute(array, 'rows', [(i, i ^ bit) for i in range(4)])  9.36 us
  transfers between devices with their start and end apart: 43, of which 11 were waited for; matrix products, arithmetic and copies ran while one was open for 7% of the time, Pallas kernels for 56%

profile of v3, /device:TPU:0, one launch (start us, length us, event | category | flops | bytes accessed | tf_op | source)
XLA Modules:
  0.0 434.8 jit_solution(7508950817587756376)
XLA Ops:
  15.4 17.7 %collective-permute-done.1 = s32[512]{0:T(512)S(1)} collective-permute-done((s32[512]{0:T(512)S(1)}, s32[512]{0:T(512)S(1)}, u32[]{:S(2)}, u32[]{:S(2)}) %collective-permute-start.1) | collective-permute-done | bytes 2080 | tf_op jit(solution)/shard_map/ppermute | solution.py:727
  40.2 3.8 fusion.15
  47.3 14.5 %project.4 = (bf16[2048,2048]{1,0:T(8,128)(2,1)}, bf16[2048,2048]{1,0:T(8,128)(2,1)}, bf16[2048,768]{1,0:T(8,128)(2,1)}, bf16[2048,1024]{1,0:T(8,128)(2,1)}, bf1...) custom-call(s32[2]{0:T(128)} %get-tuple-element.395.refs_0_, bf16[256,2048]{1,0:T(8,128)(2,1)} %bitcast.49, ...), custom_call_target="tpu_custom_call" | custom-call | flops 1048576 | bytes 65536 | tf_op jit(solution)/shard_map/project/pallas_call | solution.py:39
  67.7 15.2 %project.5 = (bf16[2048,2048]{1,0:T(8,128)(2,1)}, bf16[2048,2048]{1,0:T(8,128)(2,1)}, bf16[2048,768]{1,0:T(8,128)(2,1)}, bf16[2048,1024]{1,0:T(8,128)(2,1)}, bf1...) custom-call(s32[2]{0:T(128)} %get-tuple-element.397.refs_0_, ...), custom_call_target="tpu_custom_call", output_to_operand_aliasing={{0}: (11, {}), {1}: (12, {}), {2}: (13, {}), {3}: (14, {}),... | custom-call | flops 1048576 | bytes 65536 | tf_op jit(solution)/shard_map/project/pallas_call | solution.py:39
  82.9 14.5 %project.6 = (bf16[2048,2048]{1,0:T(8,128)(2,1)}, bf16[2048,2048]{1,0:T(8,128)(2,1)}, bf16[2048,768]{1,0:T(8,128)(2,1)}, bf16[2048,1024]{1,0:T(8,128)(2,1)}, bf1...) custom-call(s32[2]{0:T(128)} %get-tuple-element.396.refs_0_, ...), custom_call_target="tpu_custom_call", output_to_operand_aliasing={{0}: (11, {}), {1}: (12, {}), {2}: (13, {}), {3}: (14, {}),... | custom-call | flops 1048576 | bytes 65536 | tf_op jit(solution)/shard_map/project/pallas_call | solution.py:39
  97.4 13.0 %collective-permute-done.6.refs_1_ = bf16[256,2048]{1,0:T(8,128)(2,1)} collective-permute-done((bf16[256,2048]{1,0:T(8,128)(2,1)}, bf16[256,2048]{1,0:T(8,128)(2,1)}, u32[]{:S(2)}, u32[]{:S(2)}) %collective-permute-start.6) | collective-permute-done | bytes 1048608 | tf_op jit(solution)/shard_map/ppermute | solution.py:787
  114.4 14.7 %project.7 = (bf16[2048,2048]{1,0:T(8,128)(2,1)}, bf16[2048,2048]{1,0:T(8,128)(2,1)}, bf16[2048,768]{1,0:T(8,128)(2,1)}, bf16[2048,1024]{1,0:T(8,128)(2,1)}, bf1...) custom-call(s32[2]{0:T(128)} %get-tuple-element.394.refs_0_, ...), custom_call_target="tpu_custom_call", output_to_operand_aliasing={{0}: (11, {}), {1}: (12, {}), {2}: (13, {}), {3}: (14, {}),... | custom-call | flops 1048576 | bytes 65536 | tf_op jit(solution)/shard_map/project/pallas_call | solution.py:39
  129.1 10.1 %outer_parts.4 = (bf16[256,1024]{1,0:T(8,128)(2,1)}, bf16[256,1024]{1,0:T(8,128)(2,1)}, bf16[256,1024]{1,0:T(8,128)(2,1)}, bf16[256,1024]{1,0:T(8,128)(2,1)}, f32[8,128]{1,0:T(8,128)}) custom-call(s32[4]{0:T(128)} %pad_add_fusion.4.refs_0_, bf16[2048,1024]{1,0:T(8,128)(2,1)} %get-tuple-element.241.refs_1_, ...), custom_call_target="tpu_custom_call" | custom-call | flops 1048576 | bytes 65536 | tf_op jit(solution)/shard_map/outer_parts/pallas_call | solution.py:39
  143.4 20.2 %attend_forward.1 = (bf16[2048,256]{1,0:T(8,128)(2,1)}, f32[8,2048]{1,0:T(8,128)}, f32[8,128]{1,0:T(8,128)}) custom-call(s32[8]{0:T(128)} %and_select_fusion.2.refs_0_, s32[8,2048]{1,0:T(8,128)} %broadcast_in_dim.79.refs_1_, bf16[2048,768]{1,0:T(8,128)(2,1)} %get-tuple-element.240.refs_2_.refs_3_.refs_4_.refs_5_, ...), custom_call_target="tpu_custom_call" | custom-call | flops 1048576 | bytes 65536 | tf_op jit(solution)/shard_map/attend_forward/pallas_call | solution.py:39
  165.1 16.2 %branch_sum.1 = (bf16[2048,2048]{1,0:T(8,128)(2,1)}, f32[8,128]{1,0:T(8,128)}) custom-call(bf16[2048,256]{1,0:T(8,128)(2,1)} %get-tuple-element.248.refs_0_.refs_3_.refs_6_, bf16[2048,1024]{1,0:T(8,128)(2,1)} %get-tuple-element.241.refs_1_, bf16[256,2048]{1,0:T(8,128)(2,1)} %refs_3_.3, bf16[1024,2048]{1,0:T(8,128)(2,1)} %refs_2_.3, ...), custom_call_target="tpu_custom_call" | custom-call | flops 1048576 | bytes 65536 | tf_op jit(solution)/shard_map/branch_sum/pallas_call | solution.py:39
  183.3 14.7 %outer_parts.5 = (bf16[384,1024]{1,0:T(8,128)(2,1)}, bf16[384,1024]{1,0:T(8,128)(2,1)}, bf16[384,1024]{1,0:T(8,128)(2,1)}, bf16[384,1024]{1,0:T(8,128)(2,1)}, f32[8,128]{1,0:T(8,128)}) custom-call(s32[4]{0:T(128)} %pad_add_fusion.4.refs_0_, bf16[2048,1024]{1,0:T(8,128)(2,1)} %get-tuple-element.241.refs_1_, ...), custom_call_target="tpu_custom_call" | custom-call | flops 1048576 | bytes 65536 | tf_op jit(solution)/shard_map/outer_parts/pallas_call | solution.py:39
  203.0 17.4 %backward_products.1 = (bf16[2048,1024]{1,0:T(8,128)(2,1)}, bf16[2048,256]{1,0:T(8,128)(2,1)}, f32[1,1024]{1,0:T(1,128)}, f32[8,128]{1,0:T(8,128)}) custom-call(bf16[2048,1024]{1,0:T(8,128)(2,1)} %all-gather.3.cloned.1.call-done.refs_2_.refs_4_.refs_0_, bf16[2048,1024]{1,0:T(8,128)(2,1)} %all-gather.5.cloned.1.call-done.refs_2_.refs_1_, ...), custom_call_target="tpu_custom_call" | custom-call | flops 1048576 | bytes 65536 | tf_op jit(solution)/shard_map/backward_products/pallas_call | solution.py:39
  227.1 15.5 %outer_parts.6 = (bf16[512,1024]{1,0:T(8,128)(2,1)}, bf16[512,1024]{1,0:T(8,128)(2,1)}, bf16[512,1024]{1,0:T(8,128)(2,1)}, bf16[512,1024]{1,0:T(8,128)(2,1)}, f32[8,128]{1,0:T(8,128)}) custom-call(s32[4]{0:T(128)} %pad_add_fusion.4.refs_0_, bf16[2048,2048]{1,0:T(8,128)(2,1)} %get-tuple-element.282.refs_1_, ...), custom_call_target="tpu_custom_call" | custom-call | flops 1048576 | bytes 65536 | tf_op jit(solution)/shard_map/outer_parts/pallas_call | solution.py:39
  247.0 7.5 %collective-permute-done.22.refs_2_ = bf16[256,1024]{1,0:T(8,128)(2,1)S(1)} collective-permute-done((bf16[256,1024]{1,0:T(8,128)(2,1)S(1)}, bf16[256,1024]{1,0:T(8,128)(2,1)S(1)}, u32[]{:S(2)}, u32[]{:S(2)}) %collective-permute-start.22) | collective-permute-done | bytes 524320 | tf_op jit(solution)/shard_map/ppermute | solution.py:602
  256.1 30.3 %attend_backward.1 = (bf16[2048,768]{1,0:T(8,128)(2,1)}, f32[8,128]{1,0:T(8,128)}) custom-call(s32[8]{0:T(128)} %and_select_fusion.2.refs_0_, s32[8,2048]{1,0:T(8,128)} %broadcast_in_dim.79.refs_1_, f32[8,2048]{1,0:T(8,128)} %get-tuple-element.299.refs_2_, bf16[2048,768]{1,0:T(8,128)(2,1)} %get-tuple-element.240.refs_2_.refs_3_.refs_4_.refs_5_, ...), custom_call_target="tpu_custom_call" | custom-call | flops 63201050624 | bytes 65536 | tf_op jit(solution)/shard_map/attend_backward/pallas_call | solution.py:39
  294.8 25.2 %normed_sum.1 = (bf16[2048,2048]{1,0:T(8,128)(2,1)}, f32[1,2048]{1,0:T(1,128)}, f32[1,2048]{1,0:T(1,128)}, f32[8,128]{1,0:T(8,128)}) custom-call(bf16[2048,768]{1,0:T(8,128)(2,1)} %get-tuple-element.311.refs_0_.refs_2_, bf16[2048,1024]{1,0:T(8,128)(2,1)} %get-tuple-element.283.refs_2_.refs_1_, bf16[2048,2048]{1,0:T(8,128)(2,1)} %get-tuple-element.312.refs_2_, ...), custom_call_target="tpu_custom_call" | custom-call | flops 1048576 | bytes 65536 | tf_op jit(solution)/shard_map/normed_sum/pallas_call | solution.py:39
  327.1 12.8 %outer_parts.7 = (bf16[512,768]{1,0:T(8,128)(2,1)}, bf16[512,768]{1,0:T(8,128)(2,1)}, bf16[512,768]{1,0:T(8,128)(2,1)}, bf16[512,768]{1,0:T(8,128)(2,1)}, f32[8,128]{1,0:T(8,128)}) custom-call(s32[4]{0:T(128)} %pad_add_fusion.4.refs_0_, bf16[2048,2048]{1,0:T(8,128)(2,1)} %get-tuple-element.282.refs_1_, bf16[2048,768]{1,0:T(8,128)(2,1)} %get-tuple-element.311.refs_0_.refs_2_, ...), custom_call_target="tpu_custom_call" | custom-call | flops 1048576 | bytes 65536 | tf_op jit(solution)/shard_map/outer_parts/pallas_call | solution.py:39
  343.2 4.7 %finish.4 = (f32[1024,2048]{1,0:T(8,128)}, f32[8,128]{1,0:T(8,128)}) custom-call(s32[4]{0:T(128)} %pad_add_fusion.5.refs_0_, bf16[256,1024]{1,0:T(8,128)(2,1)} %copy-done.7, bf16[256,1024]{1,0:T(8,128)(2,1)} %copy-done.23, bf16[256,1024]{1,0:T(8,128)(2,1)} %copy-done.6, bf16[256,1024]{1,0:T(8,128)(2,1)} %copy-done.24, f32[8,128]{1,0:T(8,128)} %get-tuple-element.331.refs_5_), custom_call_target="tpu_custom_call" | custom-call | flops 1048576 | bytes 65536 | tf_op jit(solution)/shard_map/finish/pallas_call | solution.py:39
  347.8 13.2 %collective-permute-start.27 = (f32[6144]{0:T(1024)S(1)}, f32[6144]{0:T(1024)S(1)}, u32[]{:S(2)}, u32[]{:S(2)}) collective-permute-start(f32[6144]{0:T(1024)S(1)} %add.220), channel_id=1, source_target_pairs={{0,2},{1,3},{2,0},{3,1},{4,6},{5,7},{6,4},{7,5},{8,10},{9,11},{10,... | collective-permute-start | bytes 73736 | tf_op jit(solution)/shard_map/ppermute | solution.py:707
  361.0 5.7 %finish.5 = (f32[1024,2048]{1,0:T(8,128)}, f32[256,2048]{1,0:T(8,128)}, f32[8,128]{1,0:T(8,128)}) custom-call(s32[4]{0:T(128)} %pad_add_fusion.5.refs_0_, bf16[384,1024]{1,0:T(8,128)(2,1)} %copy-done.5, bf16[384,1024]{1,0:T(8,128)(2,1)} %copy-done.22, bf16[384,1024]{1,0:T(8,128)(2,1)} %copy-done.4, ...), custom_call_target="tpu_custom_call", output_to_operand_aliasing={{0}: (5, {})} | custom-call | flops 1048576 | bytes 65536 | tf_op jit(solution)/shard_map/finish/pallas_call | solution.py:39
  369.6 13.6 %collective-permute-start.32 = (f32[6144]{0:T(1024)S(1)}, f32[6144]{0:T(1024)S(1)}, u32[]{:S(2)}, u32[]{:S(2)}) collective-permute-start(f32[6144]{0:T(1024)S(1)} %add.223), channel_id=1, source_target_pairs={{0,4},{1,5},{2,6},{3,7},{4,0},{5,1},{6,2},{7,3},{8,12},{9,13},{10,... | collective-permute-start | bytes 73736 | tf_op jit(solution)/shard_map/ppermute | solution.py:707
  383.2 6.5 %finish.6 = (f32[2048,1024]{1,0:T(8,128)}, f32[8,128]{1,0:T(8,128)}) custom-call(s32[4]{0:T(128)} %pad_add_fusion.5.refs_0_, bf16[512,1024]{1,0:T(8,128)(2,1)} %copy-done.10, bf16[512,1024]{1,0:T(8,128)(2,1)} %collective-permute-done.30.refs_2_, bf16[512,1024]{1,0:T(8,128)(2,1)} %copy-done.9, bf16[512,1024]{1,0:T(8,128)(2,1)} %collective-permute-done.31.refs_4_, ...), custom_call_target="tpu_custom_call" | custom-call | flops 103501045760 | bytes 65536 | tf_op jit(solution)/shard_map/finish/pallas_call | solution.py:39
  394.3 15.4 %collective-permute-done.35 = f32[7936]{0:T(1024)S(1)} collective-permute-done((f32[7936]{0:T(1024)S(1)}, f32[7936]{0:T(1024)S(1)}, u32[]{:S(2)}, u32[]{:S(2)}) %collective-permute-start.35) | collective-permute-done | bytes 31776 | tf_op jit(solution)/shard_map/ppermute | solution.py:707
  415.4 5.8 %finish.7 = (f32[3,2048,256]{2,1,0:T(8,128)}, f32[8,128]{1,0:T(8,128)}) custom-call(s32[4]{0:T(128)} %pad_add_fusion.5.refs_0_, bf16[512,768]{1,0:T(8,128)(2,1)} %add_convert_fusion.5.refs_1_, bf16[512,768]{1,0:T(8,128)(2,1)} %collective-permute-done.37.refs_2_, bf16[512,768]{1,0:T(8,128)(2,1)} %copy-done.19, ...), custom_call_target="tpu_custom_call" | custom-call | flops 23001049088 | bytes 65536 | tf_op jit(solution)/shard_map/finish/pallas_call | solution.py:39
  (212 shorter events, 91.6 us)
Async XLA Ops:
  7.2 121.9 %all-gather.3.cloned.1.call-start = ((), (), s32[]{:S(2)}) async-start(), calls=%async_computation.2 | async-start | bytes 4718592 | tf_op jit(solution)/shard_map/all_gather | solution.py:792
  7.2 29.7 %collective-permute-start.3 = (bf16[256,2048]{1,0:T(8,128)(2,1)}, bf16[256,2048]{1,0:T(8,128)(2,1)S(1)}, u32[]{:S(2)}, u32[]{:S(2)}) collective-permute-start(bf16[256,2048]{1,0:T(8,128)(2,1)} %bitcast.47), channel_id=1, source_target_pairs={{0,2},{1,3},{2,4},{3,5},{4,6},{5,7},{6,0},{7,1},{8,10},{9,11},{10,... | collective-permute-start | bytes 3145736 | tf_op jit(solution)/shard_map/ppermute | solution.py:778
  10.3 36.4 %collective-permute-start.5 = (bf16[256,2048]{1,0:T(8,128)(2,1)}, bf16[256,2048]{1,0:T(8,128)(2,1)}, u32[]{:S(2)}, u32[]{:S(2)}) collective-permute-start(bf16[256,2048]{1,0:T(8,128)(2,1)} %bitcast.48), channel_id=1, source_target_pairs={{0,1},{1,0},{2,3},{3,2},{4,5},{5,4},{6,7},{7,6},{8,9},{9,8},{10,11... | collective-permute-start | bytes 3145736 | tf_op jit(solution)/shard_map/ppermute | solution.py:777
  37.9 25.4 %collective-permute-start.4 = (bf16[256,2048]{1,0:T(8,128)(2,1)S(1)}, bf16[256,2048]{1,0:T(8,128)(2,1)}, u32[]{:S(2)}, u32[]{:S(2)}) collective-permute-start(bf16[256,2048]{1,0:T(8,128)(2,1)S(1)} %collective-permute-done.3.refs_1_), channel_id=1, source_target_pairs={{0,2},{1,3},{2,4},{3,5},{4,6},{5,7},{6,0},{7,1},{8,10},{9,11},{10,... | collective-permute-start | bytes 3145736 | tf_op jit(solution)/shard_map/ppermute | solution.py:787
  63.3 120.0 %all-gather.5.cloned.1.call-start = ((), (), s32[]{:S(2)}) async-start(), calls=%async_computation.4 | async-start | bytes 4718592 | tf_op jit(solution)/shard_map/all_gather | solution.py:792
  64.1 230.7 %reduce-scatter.3.cloned.1.call-start = ((), (), s32[]{:S(2)}) async-start(), calls=%async_computation.3 | async-start | bytes 9437184 | tf_op jit(solution)/shard_map/reduce_scatter | solution.py:832
  64.7 45.7 %collective-permute-start.6 = (bf16[256,2048]{1,0:T(8,128)(2,1)}, bf16[256,2048]{1,0:T(8,128)(2,1)}, u32[]{:S(2)}, u32[]{:S(2)}) collective-permute-start(bf16[256,2048]{1,0:T(8,128)(2,1)} %collective-permute-done.4.refs_1_), channel_id=1, source_target_pairs={{0,2},{1,3},{2,4},{3,5},{4,6},{5,7},{6,0},{7,1},{8,10},{9,11},{10,... | collective-permute-start | bytes 3145736 | tf_op jit(solution)/shard_map/ppermute | solution.py:787
  139.2 24.5 %collective-permute-start.10 = (bf16[256,1024]{1,0:T(8,128)(2,1)}, bf16[256,1024]{1,0:T(8,128)(2,1)}, u32[]{:S(2)}, u32[]{:S(2)}) collective-permute-start(bf16[256,1024]{1,0:T(8,128)(2,1)} %get-tuple-element.250), channel_id=1, source_target_pairs={{0,8},{8,0},{16,24},{24,16},{1,9},{9,1},{17,25},{25,17},{2,10},{10... | collective-permute-start | bytes 1572872 | tf_op jit(solution)/shard_map/ppermute | solution.py:602
  181.4 241.9 %reduce-scatter.5.cloned.1.call-start = ((), (), s32[]{:S(2)}) async-start(), calls=%async_computation.5 | async-start | bytes 9437184 | tf_op jit(solution)/shard_map/reduce_scatter | solution.py:847
  225.0 29.6 %collective-permute-start.22 = (bf16[256,1024]{1,0:T(8,128)(2,1)S(1)}, bf16[256,1024]{1,0:T(8,128)(2,1)S(1)}, u32[]{:S(2)}, u32[]{:S(2)}) collective-permute-start(bf16[256,1024]{1,0:T(8,128)(2,1)S(1)} %add_convert_fusion.13.refs_1_), channel_id=1, source_target_pairs={{0,8},{8,0},{16,24},{24,16},{1,9},{9,1},{17,25},{25,17},{2,10},{10... | collective-permute-start | bytes 1572872 | tf_op jit(solution)/shard_map/ppermute | solution.py:602
  225.6 60.8 %collective-permute-start.23 = (bf16[256,1024]{1,0:T(8,128)(2,1)S(1)}, bf16[256,1024]{1,0:T(8,128)(2,1)S(1)}, u32[]{:S(2)}, u32[]{:S(2)}) collective-permute-start(bf16[256,1024]{1,0:T(8,128)(2,1)S(1)} %add_convert_fusion.12.refs_3_), channel_id=1, source_target_pairs={{0,16},{8,24},{16,0},{24,8},{1,17},{9,25},{17,1},{25,9},{2,18},{10... | collective-permute-start | bytes 1572872 | tf_op jit(solution)/shard_map/ppermute | solution.py:602
  242.7 43.8 %collective-permute-start.20 = (bf16[512,1024]{1,0:T(8,128)(2,1)}, bf16[512,1024]{1,0:T(8,128)(2,1)S(1)}, u32[]{:S(2)}, u32[]{:S(2)}) collective-permute-start(bf16[512,1024]{1,0:T(8,128)(2,1)} %get-tuple-element.295), channel_id=1, source_target_pairs={{0,8},{8,0},{16,24},{24,16},{1,9},{9,1},{17,25},{25,17},{2,10},{10... | collective-permute-start | bytes 3145736 | tf_op jit(solution)/shard_map/ppermute | solution.py:602
  242.8 43.6 %collective-permute-start.21 = (bf16[512,1024]{1,0:T(8,128)(2,1)}, bf16[512,1024]{1,0:T(8,128)(2,1)S(1)}, u32[]{:S(2)}, u32[]{:S(2)}) collective-permute-start(bf16[512,1024]{1,0:T(8,128)(2,1)} %get-tuple-element.296), channel_id=1, source_target_pairs={{0,16},{8,24},{16,0},{24,8},{1,17},{9,25},{17,1},{25,9},{2,18},{10... | collective-permute-start | bytes 3145736 | tf_op jit(solution)/shard_map/ppermute | solution.py:602
  246.3 47.6 %collective-permute-start.18 = (bf16[384,1024]{1,0:T(8,128)(2,1)S(1)}, bf16[384,1024]{1,0:T(8,128)(2,1)S(1)}, u32[]{:S(2)}, u32[]{:S(2)}) collective-permute-start(bf16[384,1024]{1,0:T(8,128)(2,1)S(1)} %add_convert_fusion.9.refs_1_), channel_id=1, source_target_pairs={{0,8},{8,0},{16,24},{24,16},{1,9},{9,1},{17,25},{25,17},{2,10},{10... | collective-permute-start | bytes 2359304 | tf_op jit(solution)/shard_map/ppermute | solution.py:602
  254.6 40.2 %collective-permute-start.19 = (bf16[384,1024]{1,0:T(8,128)(2,1)S(1)}, bf16[384,1024]{1,0:T(8,128)(2,1)}, u32[]{:S(2)}, u32[]{:S(2)}) collective-permute-start(bf16[384,1024]{1,0:T(8,128)(2,1)S(1)} %add_convert_fusion.8.refs_3_), channel_id=1, source_target_pairs={{0,16},{8,24},{16,0},{24,8},{1,17},{9,25},{17,1},{25,9},{2,18},{10... | collective-permute-start | bytes 2359304 | tf_op jit(solution)/shard_map/ppermute | solution.py:602
  289.3 32.1 %collective-permute-start.24 = (bf16[512,1024]{1,0:T(8,128)(2,1)S(1)}, bf16[512,1024]{1,0:T(8,128)(2,1)}, u32[]{:S(2)}, u32[]{:S(2)}) collective-permute-start(bf16[512,1024]{1,0:T(8,128)(2,1)S(1)} %add_convert_fusion.3), channel_id=1, source_target_pairs={{0,16},{8,24},{16,0},{24,8},{1,17},{9,25},{17,1},{25,9},{2,18},{10... | collective-permute-start | bytes 3145736 | tf_op jit(solution)/shard_map/ppermute | solution.py:602
  289.9 31.5 %collective-permute-start.25 = (bf16[512,1024]{1,0:T(8,128)(2,1)S(1)}, bf16[512,1024]{1,0:T(8,128)(2,1)}, u32[]{:S(2)}, u32[]{:S(2)}) collective-permute-start(bf16[512,1024]{1,0:T(8,128)(2,1)S(1)} %add_convert_fusion.2), channel_id=1, source_target_pairs={{0,8},{8,0},{16,24},{24,16},{1,9},{9,1},{17,25},{25,17},{2,10},{10... | collective-permute-start | bytes 3145736 | tf_op jit(solution)/shard_map/ppermute | solution.py:602
  325.1 41.6 %collective-permute-start.30 = (bf16[512,1024]{1,0:T(8,128)(2,1)S(1)}, bf16[512,1024]{1,0:T(8,128)(2,1)}, u32[]{:S(2)}, u32[]{:S(2)}) collective-permute-start(bf16[512,1024]{1,0:T(8,128)(2,1)S(1)} %add_convert_fusion.1.refs_1_), channel_id=1, source_target_pairs={{0,8},{8,0},{16,24},{24,16},{1,9},{9,1},{17,25},{25,17},{2,10},{10... | collective-permute-start | bytes 3145736 | tf_op jit(solution)/shard_map/ppermute | solution.py:602
  326.5 40.2 %collective-permute-start.31 = (bf16[512,1024]{1,0:T(8,128)(2,1)S(1)}, bf16[512,1024]{1,0:T(8,128)(2,1)}, u32[]{:S(2)}, u32[]{:S(2)}) collective-permute-start(bf16[512,1024]{1,0:T(8,128)(2,1)S(1)} %add_convert_fusion.refs_3_), channel_id=1, source_target_pairs={{0,16},{8,24},{16,0},{24,8},{1,17},{9,25},{17,1},{25,9},{2,18},{10... | collective-permute-start | bytes 3145736 | tf_op jit(solution)/shard_map/ppermute | solution.py:602
  340.0 26.8 %collective-permute-start.28 = (bf16[512,768]{1,0:T(8,128)(2,1)}, bf16[512,768]{1,0:T(8,128)(2,1)S(1)}, u32[]{:S(2)}, u32[]{:S(2)}) collective-permute-start(bf16[512,768]{1,0:T(8,128)(2,1)} %get-tuple-element.337), channel_id=1, source_target_pairs={{0,8},{8,0},{16,24},{24,16},{1,9},{9,1},{17,25},{25,17},{2,10},{10... | collective-permute-start | bytes 2359304 | tf_op jit(solution)/shard_map/ppermute | solution.py:602
  341.8 25.0 %collective-permute-start.29 = (bf16[512,768]{1,0:T(8,128)(2,1)}, bf16[512,768]{1,0:T(8,128)(2,1)S(1)}, u32[]{:S(2)}, u32[]{:S(2)}) collective-permute-start(bf16[512,768]{1,0:T(8,128)(2,1)} %get-tuple-element.338), channel_id=1, source_target_pairs={{0,16},{8,24},{16,0},{24,8},{1,17},{9,25},{17,1},{25,9},{2,18},{10... | collective-permute-start | bytes 2359304 | tf_op jit(solution)/shard_map/ppermute | solution.py:602
  369.6 23.1 %collective-permute-start.32 = (f32[6144]{0:T(1024)S(1)}, f32[6144]{0:T(1024)S(1)}, u32[]{:S(2)}, u32[]{:S(2)}) collective-permute-start(f32[6144]{0:T(1024)S(1)} %add.223), channel_id=1, source_target_pairs={{0,4},{1,5},{2,6},{3,7},{4,0},{5,1},{6,2},{7,3},{8,12},{9,13},{10,... | collective-permute-start | bytes 73736 | tf_op jit(solution)/shard_map/ppermute | solution.py:707
  391.0 24.4 %collective-permute-start.37 = (bf16[512,768]{1,0:T(8,128)(2,1)}, bf16[512,768]{1,0:T(8,128)(2,1)}, u32[]{:S(2)}, u32[]{:S(2)}) collective-permute-start(bf16[512,768]{1,0:T(8,128)(2,1)} %add_convert_fusion.5.refs_1_), channel_id=1, source_target_pairs={{0,8},{8,0},{16,24},{24,16},{1,9},{9,1},{17,25},{25,17},{2,10},{10... | collective-permute-start | bytes 2359304 | tf_op jit(solution)/shard_map/ppermute | solution.py:602
  391.1 24.3 %collective-permute-start.38 = (bf16[512,768]{1,0:T(8,128)(2,1)S(1)}, bf16[512,768]{1,0:T(8,128)(2,1)}, u32[]{:S(2)}, u32[]{:S(2)}) collective-permute-start(bf16[512,768]{1,0:T(8,128)(2,1)S(1)} %add_convert_fusion.4.refs_3_), channel_id=1, source_target_pairs={{0,16},{8,24},{16,0},{24,8},{1,17},{9,25},{17,1},{25,9},{2,18},{10... | collective-permute-start | bytes 2359304 | tf_op jit(solution)/shard_map/ppermute | solution.py:602
  (53 other events, 693.2 us)
Sparse Core Ops, SparseCore 0:
  63.4 64.3 all-gather.2
  129.4 45.4 all-gather.4
  181.5 101.3 reduce-scatter.2
  320.1 103.1 reduce-scatter.4
